TPU v7x, 256 devices: a whole 4x4x8 slice. The times are simulated.
256 devices in a mesh: aux: 16 (over x, y_lo, core), virt: 16 (over z, y_hi).
Axes of the slice: x: 4, y: 4 (y_hi: 2, y_lo: 2; y = y_hi * 2 + y_lo), z: 8, core: 2. Of those that a mesh axis runs over, the one named last changes fastest.
Arguments:
- orbital_block: bfloat16 [16384, 4096], P('aux', 'virt'), may hold values from -0.046875 to 0.046875
- partner_blocks: bfloat16 [1, 16384, 4096], P(None, 'aux', 'virt'), may hold values from -0.046875 to 0.046875
- occ_energy: float32 [2], replicated, may hold values from -2 to -0.3
- virt_energy: float32 [4096], replicated, may hold values from 0.2 to 3
Outputs:
- gamma_own: float32 [16384, 4096], P('aux', 'virt')
- gamma_partner: float32 [1, 16384, 4096], P(None, 'aux', 'virt')
All inputs are finite; a program needn't handle non-finite values.
Results may differ from a plain program's by a relative error of at most 0.0038.
Values may be sent and summed in bfloat16 or wider, within the bound.
No kernel may reach another device: no remote copies, remote signals or barrier semaphores. Data moves between devices by JAX's collectives and lax.ppermute only.
A program may use at most 128 MiB of HBM per device.

v0:
```python
import jax
import jax.numpy as jnp
from jax import lax
from jax.sharding import PartitionSpec as P


def local(orbital_block, partner_blocks, occ_energy, virt_energy):
    width = orbital_block.shape[1]
    virt_count = lax.axis_size("virt")
    whole = width * virt_count
    slice_width = whole // lax.axis_size("aux")
    virt_index = lax.axis_index("virt")
    aux_index = lax.axis_index("aux")
    energy_rows = lax.dynamic_slice_in_dim(virt_energy, virt_index * width, width)
    energy_cols = lax.dynamic_slice_in_dim(virt_energy, aux_index * slice_width, slice_width)
    own_all = lax.all_gather(orbital_block, "virt", axis=1, tiled=True)
    partner_all = lax.all_gather(partner_blocks, "virt", axis=2, tiled=True)
    partner_own = partner_blocks[0]
    partner_full = partner_all[0]
    direct = jnp.einsum(
        "pa,pb->ab", orbital_block, partner_full, preferred_element_type=jnp.float32
    )
    swapped = jnp.einsum("pa,pb->ab", partner_own, own_all, preferred_element_type=jnp.float32)
    denom = occ_energy[0] + occ_energy[1] - energy_rows[:, None] - energy_cols[None, :]
    summed = lax.psum_scatter(2.0 * direct - swapped, "aux", scatter_dimension=1, tiled=True)
    amp_part = (summed / denom).astype(jnp.bfloat16)
    amp_full = lax.all_gather(amp_part, "aux", axis=1, tiled=True)
    gamma_own = jnp.einsum("pb,ab->pa", partner_full, amp_full, preferred_element_type=jnp.float32)
    terms = jnp.einsum(
        "pa,ab->pb", orbital_block, amp_full, preferred_element_type=jnp.float32
    ).astype(jnp.bfloat16)
    terms = lax.optimization_barrier(terms).astype(jnp.float32)
    results = [lax.psum_scatter(terms, "virt", scatter_dimension=1, tiled=True)]
    return (gamma_own, jnp.stack(results))


def solution(mesh):
    in_specs = (P("aux", "virt"), P(None, "aux", "virt"), P(), P())
    out_specs = (P("aux", "virt"), P(None, "aux", "virt"))
    return jax.shard_map(local, mesh=mesh, in_specs=in_specs, out_specs=out_specs, check_vma=False)
```

profile of v0, /device:TPU:1, one launch (start us, length us, event | category | flops | bytes accessed | tf_op | source)
XLA Modules:
  0.0 738.4 jit_solution(11537862093759635309)
XLA Ops:
  7.2 0.0 copy-start.2
  7.2 0.0 all-gather.4.cloned.1.call-start
  7.2 0.7 all-gather.4.cloned.1.call-update
  7.9 0.0 all-gather.6.cloned.1.call-start
  8.0 0.7 all-gather.6.cloned.1.call-update
  8.7 0.0 reduce-scatter.3.cloned.1.call-start
  8.7 151.1 %all-gather.4.cloned.1.call-done = bf16[1,1024,4096]{2,1,0:T(8,128)(2,1)} async-done(((bf16[1,1024,256]{2,1,0:T(8,128)(2,1)}), bf16[1,1024,4096]{2,1,0:T(8,128)(2,1)}) %all-gather.4.cloned.1.call-update) | async-done | bytes 8388624 | tf_op jit(solution)/shard_map/all_gather | solution.py:17
  159.8 7.9 %fusion.4 = f32[256,4096]{1,0:T(8,128)} fusion(bf16[1024,256]{1,0:T(8,128)(2,1)} %param.4, bf16[1,1024,4096]{2,1,0:T(8,128)(2,1)} %all-gather.4.cloned.1.call-done), kind=kOutput, calls=%fused_computation.5 | convolution fusion | flops 2148532224 | bytes 13107200 | tf_op jit(solution)/shard_map/pa,pb->ab/dot_general | solution.py:20
  167.7 0.0 copy-start.3
  167.7 0.0 copy-start
  167.7 138.9 %all-gather.6.cloned.1.call-done = bf16[1024,4096]{1,0:T(8,128)(2,1)} async-done(((bf16[1024,256]{1,0:T(8,128)(2,1)}), bf16[1024,4096]{1,0:T(8,128)(2,1)}) %all-gather.6.cloned.1.call-update) | async-done | bytes 8388624 | tf_op jit(solution)/shard_map/all_gather | solution.py:16
  306.6 0.0 copy-done.2
  306.6 8.9 %convolution_subtract_fusion = f32[256,4096]{1,0:T(8,128)} fusion(f32[256,4096]{1,0:T(8,128)} %fusion.4, bf16[1024,4096]{1,0:T(8,128)(2,1)} %all-gather.6.cloned.1.call-done, bf16[1,1024,256]{2,1,0:T(8,128)(2,1)S(1)} %copy-done.2), kind=kOutput, calls=%fused_computation.6 | convolution fusion | flops 2148532224 | bytes 17301504 | tf_op jit(solution)/shard_map/pa,pb->ab/dot_general | solution.py:23
  315.5 0.0 reduce-scatter.3.cloned.1.call-update
  315.6 0.0 all-gather.8.cloned.1.call-start
  315.6 0.0 copy-done.3
  315.6 0.6 fusion.11
  317.5 0.8 dynamic-slice_subtract_fusion
  318.4 63.0 %reduce-scatter.3.cloned.1.call-done = f32[256,256]{1,0:T(8,128)} async-done(((f32[256,4096]{1,0:T(8,128)}), f32[256,256]{1,0:T(8,128)}) %reduce-scatter.3.cloned.1.call-update) | async-done | bytes 262160 | tf_op jit(solution)/shard_map/reduce_scatter | solution.py:25
  381.4 1.7 divide_convert_fusion
  383.1 0.0 all-gather.8.cloned.1.call-update
  383.1 0.2 reduce-scatter.5.cloned.1.call-start
  383.4 42.2 %all-gather.8.cloned.1.call-done = bf16[256,4096]{1,0:T(8,128)(2,1)} async-done(((bf16[256,256]{1,0:T(8,128)(2,1)}), bf16[256,4096]{1,0:T(8,128)(2,1)}) %all-gather.8.cloned.1.call-update) | async-done | bytes 2097168 | tf_op jit(solution)/shard_map/all_gather | solution.py:27
  425.6 0.0 copy-done
  425.6 7.2 convert_bitcast_fusion
  432.8 11.3 %convert_element_type.15 = f32[1024,4096]{0,1:T(8,128)} convert(bf16[1024,4096]{0,1:T(8,128)(2,1)} %convert_bitcast_fusion) | non-fusion elementwise | flops 4194304 | bytes 25165824 | tf_op jit(solution)/shard_map/convert_element_type | solution.py:32
  444.1 0.0 reduce-scatter.5.cloned.1.call-update
  444.1 1.6 copy-done.1
  445.7 5.7 fusion.7
  451.4 1.3 copy.6
  452.7 276.6 %reduce-scatter.5.cloned.1.call-done = f32[1024,256]{0,1:T(8,128)} async-done(((f32[1024,4096]{0,1:T(8,128)}), f32[1024,256]{0,1:T(8,128)}) %reduce-scatter.5.cloned.1.call-update) | async-done | bytes 1048592 | tf_op jit(solution)/shard_map/reduce_scatter | solution.py:33
  729.4 2.5 copy.7
  (1 shorter events, 0.0 us)
Async XLA Ops:
  7.2 299.4 %copy-start.2 = (bf16[1,1024,256]{2,1,0:T(8,128)(2,1)S(1)}, bf16[1,1024,256]{2,1,0:T(8,128)(2,1)}, u32[]{:S(2)}) copy-start(bf16[1,1024,256]{2,1,0:T(8,128)(2,1)} %param.5) | copy-start | bytes 1572868
  7.2 152.6 %all-gather.4.cloned.1.call-start = ((), (), s32[]{:S(2)}) async-start(), calls=%async_computation.2 | async-start | bytes 8912896 | tf_op jit(solution)/shard_map/all_gather | solution.py:17
  7.9 298.7 %all-gather.6.cloned.1.call-start = ((), (), s32[]{:S(2)}) async-start(), calls=%async_computation.3 | async-start | bytes 8912896 | tf_op jit(solution)/shard_map/all_gather | solution.py:16
  8.7 372.7 %reduce-scatter.3.cloned.1.call-start = ((), (), s32[]{:S(2)}) async-start(), calls=%async_computation.4 | async-start | bytes 4456448 | tf_op jit(solution)/shard_map/reduce_scatter | solution.py:25
  167.7 147.9 %copy-start.3 = (f32[2]{0:T(128)S(1)}, f32[2]{0:T(128)}, u32[]{:S(2)}) copy-start(f32[2]{0:T(128)} %param.6) | copy-start | bytes 28
  167.7 257.9 %copy-start = (bf16[1024,256]{1,0:T(8,128)(2,1)S(1)}, bf16[1024,256]{1,0:T(8,128)(2,1)}, u32[]{:S(2)}) copy-start(bf16[1024,256]{1,0:T(8,128)(2,1)} %param.4) | copy-start | bytes 1572868
  315.6 110.0 %all-gather.8.cloned.1.call-start = ((), (), s32[]{:S(2)}) async-start(), calls=%async_computation.5 | async-start | bytes 2228224 | tf_op jit(solution)/shard_map/all_gather | solution.py:27
  383.1 346.2 %reduce-scatter.5.cloned.1.call-start = ((), (), s32[]{:S(2)}) async-start(), calls=%async_computation.6 | async-start | bytes 17825792 | tf_op jit(solution)/shard_map/reduce_scatter | solution.py:33
  444.1 1.6 copy-start.1
Sparse Core Ops, SparseCore 0:
  10.5 149.2 all-gather.3
  162.3 144.2 all-gather.5
  315.7 65.6 reduce-scatter.2
  383.6 41.9 all-gather.7
  444.2 285.0 reduce-scatter.4
where the time goes:
time: 739 us; the launch traced here: 738 us
  waiting for transfers between devices  673 us (91%)
  matrix products  29.8 us (4%)
  between operations  15.1 us (2%)
  other arithmetic  13.8 us (2%)
    reduce_scatter x1, waiting for transfers between devices, local(): results = [lax.psum_scatter(terms, 'virt', scatter_dimension=1, tiled=True)]  277 us
    all_gather x1, waiting for transfers between devices, local(): partner_all = lax.all_gather(partner_blocks, 'virt', axis=2, tiled=True)  151 us
    all_gather x1, waiting for transfers between devices, local(): own_all = lax.all_gather(orbital_block, 'virt', axis=1, tiled=True)  139 us
    reduce_scatter x1, waiting for transfers between devices, local(): lax.psum_scatter(2.0 * direct - swapped, 'aux', scatter_dimension=1, tile...  63 us
    all_gather x1, waiting for transfers between devices, local(): amp_full = lax.all_gather(amp_part, 'aux', axis=1, tiled=True)  42.2 us
  transfers between devices with their start and end apart: 5, of which 5 were waited for; matrix products, arithmetic and copies ran while one was open for 2% of the time, Pallas kernels for 0%

commit v1 on v0

v1 whole, which is shorter than its diff:
```python
import functools

import jax
import jax.numpy as jnp
from jax import lax
from jax.experimental import pallas as pl
from jax.experimental.pallas import tpu as pltpu
from jax.sharding import Mesh, PartitionSpec as P

AXES = ("x", "yl", "c", "z", "yh")
SIZES = (4, 2, 2, 8, 2)
NZ = 8
CHIPS = 8
F32, BF16 = jnp.float32, jnp.bfloat16


def shift(value, axis, size, step):
    return lax.ppermute(value, axis, [(i, (i + step) % size) for i in range(size)])


def swap(value, axis):
    return lax.ppermute(value, axis, [(0, 1), (1, 0)])


class Lazy:
    def __init__(self, scratch, copy):
        self.scratch, self.copy = scratch, copy

    def get(self):
        if self.copy is not None:
            self.copy.wait()
            self.copy = None
        return self.scratch


def call(kernel, out_shape, *args, scalar=False):
    lead = 1 if scalar else 0
    moved = args[lead:]
    count = len(moved)
    outs = len(jax.tree.leaves(out_shape))

    def body(*refs):
        sources = refs[lead:lead + count]
        targets = refs[lead + count:lead + count + outs]
        scratch = refs[lead + count + outs:-1]
        sems = refs[-1]
        lazy = []
        for index in range(count):
            copy = pltpu.make_async_copy(sources[index], scratch[index], sems.at[index])
            copy.start()
            lazy.append(Lazy(scratch[index], copy))
        kernel(*refs[:lead], *lazy, *targets)
        for item in lazy:
            item.get()

    specs = [pl.BlockSpec(memory_space=pltpu.SMEM)] * lead + [pl.BlockSpec(memory_space=pltpu.HBM)] * count
    out_specs = jax.tree.map(lambda _: pl.BlockSpec(memory_space=pltpu.VMEM), out_shape)
    return pl.pallas_call(
        body,
        out_shape=out_shape,
        in_specs=specs,
        out_specs=out_specs,
        scratch_shapes=[pltpu.VMEM(arg.shape, arg.dtype) for arg in moved] + [pltpu.SemaphoreType.DMA((count,))],
        cost_estimate=pl.CostEstimate(flops=0, bytes_accessed=0, transcendentals=0),
        compiler_params=pltpu.CompilerParams(vmem_limit_bytes=56 * 1024 * 1024),
    )(*args)


def prepare_kernel(width, core, *refs):
    out = refs[-1]
    parts = [ref.get() for ref in refs[:-1]]
    count = len(parts) // 2
    zero = core[0] == 0
    start = 0
    for index in range(count):
        here, peer = parts[index], parts[count + index]
        rows = here.shape[0]
        for side in range(2):
            columns = slice(side * width, (side + 1) * width)
            first, second = here[:, columns].T, peer[:, columns].T
            into = slice(start, start + rows)
            out[2 * side * width:(2 * side + 1) * width, into] = jnp.where(zero, first, second)
            out[(2 * side + 1) * width:(2 * side + 2) * width, into] = jnp.where(zero, second, first)
        start += rows


def products_kernel(counts, width, *refs):
    left = refs[0].get()
    kept, given = refs[-2:]
    position = 1
    for index, count in enumerate(counts):
        parts = [ref.get() for ref in refs[position:position + count]]
        position += count
        for side in range(2):
            columns = slice(width, 2 * width) if side == 0 else slice(0, width)
            total = None
            start = 0
            for part in parts:
                rows = part.shape[0]
                value = jnp.dot(
                    left[2 * side * width:(2 * side + 2) * width, start:start + rows],
                    part[:, columns],
                    preferred_element_type=F32,
                )
                total = value if total is None else total + value
                start += rows
            place = slice((2 * index + side) * width, (2 * index + side + 1) * width)
            kept[:, place] = total[:width]
            given[:, place] = total[width:].astype(BF16)


def products(left, blocks, width):
    counts = [len(block) for block in blocks]
    flat = [part for block in blocks for part in block]
    shape = (width, 2 * width * len(blocks))
    shapes = (jax.ShapeDtypeStruct(shape, F32), jax.ShapeDtypeStruct(shape, BF16))
    return call(functools.partial(products_kernel, counts, width), shapes, left, *flat)


def amplitude_kernel(count, width, copies, pieces, row_level, col_energy, out):
    pieces, row_level, col_energy = pieces.get(), row_level.get(), col_energy.get()
    for index in range(count):
        denom = row_level[...] - col_energy[:, index * width:(index + 1) * width]
        direct = None
        crossed = None
        for chip in range(CHIPS):
            first = pieces[chip, :, (2 * index) * width:(2 * index + 1) * width].astype(F32)
            second = pieces[chip, :, (2 * index + 1) * width:(2 * index + 2) * width].astype(F32)
            direct = first if direct is None else direct + first
            crossed = second if crossed is None else crossed + second
        amp = ((2.0 * direct - crossed) / denom).astype(BF16)
        amp_crossed = ((2.0 * crossed - direct) / denom).astype(BF16)
        for copy in range(copies):
            out[copy, :, (2 * index) * width:(2 * index + 1) * width] = amp
            out[copy, :, (2 * index + 1) * width:(2 * index + 2) * width] = amp_crossed


def contract(block, amps):
    return lax.dot_general(block, amps, (((1,), (1,)), ((), ())), preferred_element_type=F32)


def gamma_kernel(count, width, step, side, add, *refs):
    core, mine, other = refs[0], refs[1].get(), refs[2].get()
    flat = [ref.get() for ref in refs[3:3 + 2 * count]]
    outs = refs[-2:]
    sums = [ref.get() for ref in refs[3 + 2 * count:5 + 2 * count]] if add else None
    zero = core[0] == 0
    columns = slice(width, 2 * width) if side == 0 else slice(0, width)
    for store in range(2):
        chosen = zero if store == 0 else jnp.logical_not(zero)
        amps = []
        for index in range(count):
            place = slice((2 * index + side) * width, (2 * index + side + 1) * width)
            amps.append(jnp.where(chosen, mine[:, place], other[:, place]))
        for part in range(2):
            size = flat[part].shape[0]
            for start in range(0, size, step):
                rows = slice(start, start + step)
                into = slice(part * size + start, part * size + start + step)
                total = None
                for index in range(count):
                    value = contract(flat[2 * index + part][rows, columns], amps[index])
                    total = value if total is None else total + value
                if add:
                    total = total + sums[store][into, :]
                outs[store][into, :] = total.astype(outs[store].dtype)


def local(own, partner_blocks, occ_energy, virt_energy):
    x, yl, c, z, yh = (lax.axis_index(name) for name in AXES)
    k = x * 2 + yl
    depth, width = own.shape
    half = depth // 2
    rows = width // CHIPS
    step = min(256, half)
    first = c == 0
    core = c.astype(jnp.int32).reshape(1)

    base = jnp.concatenate([own, partner_blocks[0]], axis=1)
    base = base[:half], base[half:]
    base_peer = tuple(swap(part, "yh") for part in base)
    shape = jax.ShapeDtypeStruct((4 * width, depth), BF16)
    left = call(functools.partial(prepare_kernel, width), shape, core, *base, *base_peer, scalar=True)
    level = occ_energy[0] + occ_energy[1]
    row_energy = lax.dynamic_slice_in_dim(virt_energy, (z * 2 + (yh ^ c)) * width + k * rows, rows)
    row_level = (level - row_energy)[:, None]
    by_block = virt_energy.reshape(NZ, 2, width)
    col_energy = {d: lax.dynamic_slice(by_block, ((z + d) % NZ, yh, 0), (1, 1, width)).reshape(1, width) for d in range(-3, 5)}

    def after(values, *others):
        return lax.optimization_barrier((values, others))[0]

    def combined(blocks):
        kept, given = products(left, blocks, width)
        return (kept + swap(given, "c").astype(F32)).astype(BF16).reshape(CHIPS, rows, -1)

    def scatter(summed):
        return lax.all_to_all(summed, ("x", "yl"), 0, 0, tiled=True)

    def amplitudes(group, pieces, copies):
        cols = jnp.concatenate([col_energy[d] for d in group], axis=1)
        shape = jax.ShapeDtypeStruct((copies, rows, 2 * width * len(group)), BF16)
        kernel = functools.partial(amplitude_kernel, len(group), width, copies)
        return call(kernel, shape, pieces, row_level, cols)

    def spread(copies):
        return lax.all_to_all(copies, ("x", "yl"), 0, 0, tiled=True).reshape(width, -1)

    def gamma(side, blocks, mine, other, sums):
        kernel = functools.partial(gamma_kernel, len(blocks), width, step, side, sums is not None)
        shape = (depth, width)
        shapes = jax.ShapeDtypeStruct(shape, F32), jax.ShapeDtypeStruct(shape, F32 if sums is None else BF16)
        flat = [part for block in blocks for part in block]
        return call(kernel, shapes, core, mine, other, *flat, *(sums or ()), scalar=True)

    def both(parts, way):
        return tuple(shift(part, "z", NZ, way) for part in parts)

    up1, down1 = both(base, 1), both(base, -1)
    up2, down2 = both(up1, 1), both(down1, -1)
    up3, down3 = both(up2, 1), both(down2, -1)
    far = shift(up3[0], "z", NZ, 1), shift(down3[1], "z", NZ, -1)

    near, distant = (0, 1, -1, 2, -2), (3, -3, 4)
    near_blocks, distant_blocks = [base, down1, up1, down2, up2], [down3, up3, far]
    pieces_a = scatter(after(combined(near_blocks), up3[0], down3[0]))
    amp_a = amplitudes(near, after(pieces_a, far), CHIPS)
    pieces_b = scatter(combined(distant_blocks))
    mine_a = spread(amp_a)
    other_a = swap(mine_a, "c")
    sums = [gamma(side, near_blocks, mine_a, other_a, None) for side in range(2)]
    amp_b = amplitudes(distant, pieces_b, CHIPS)
    mine_b = spread(amp_b)
    other_b = swap(after(mine_b, sums), "c")
    outs = []
    for side in range(2):
        here, there = gamma(side, distant_blocks, mine_b, other_b, sums[side])
        outs.append(here + swap(there, "yh").astype(F32))
    gamma_own, gamma_partner = outs
    return gamma_own, gamma_partner[None]


def solution(mesh):
    grid = Mesh(mesh.devices.reshape(SIZES), AXES)
    aux, virt = ("x", "yl", "c"), ("z", "yh")
    in_specs = (P(aux, virt), P(None, aux, virt), P(), P())
    out_specs = (P(aux, virt), P(None, aux, virt))
    return jax.shard_map(local, mesh=grid, in_specs=in_specs, out_specs=out_specs, check_vma=False)
```

time: 739 us -> 224 us (0.30)
  waiting for transfers between devices: 673 us -> 106 us
  starting transfers between devices: 0.38 us -> 56.6 us
  Pallas kernels: 0 us -> 42.9 us
  matrix products: 29.8 us -> 0 us
  between operations: 15.1 us -> 2.26 us
    reduce_scatter x2 -> x0, waiting for transfers between devices: 340 us -> none  [the longest x1 277 us: local(): results = [lax.psum_scatter(terms, 'virt', scatter_dimension=1, tiled=True)]]
    all_gather x3 -> x0, waiting for transfers between devices: 332 us -> none  [the longest x1 151 us: local(): partner_all = lax.all_gather(partner_blocks, 'virt', axis=2, tiled=True)]
    ppermute x0 -> x22, waiting for transfers between devices: none -> 78.5 us  [the longest x14 54.7 us: shift(): lax.ppermute(value, axis, [(i, (i + step) % size) for i in range(size)])]
    pallas_call x0 -> x9, Pallas kernels: none -> 42.9 us  [call(): pl.pallas_call(body, out_shape=out_shape, in_specs=specs, out_specs=out_s...]
    ppermute x0 -> x22, starting transfers between devices: none -> 40 us  [the longest x8 20.8 us: swap(): return lax.ppermute(value, axis, [(0, 1), (1, 0)])]
    dot_general x4 -> x0, matrix products: 29.8 us -> none  [the longest x1 8.94 us: local(): jnp.einsum('pa,pb->ab', partner_own, own_all, preferred_element_type=jnp....]
    all_to_all x0 -> x4, waiting for transfers between devices: none -> 27.6 us  [the longest x2 18.1 us: spread(): lax.all_to_all(copies, ('x', 'yl'), 0, 0, tiled=True).reshape(width, -1)]
    all_to_all x0 -> x4, starting transfers between devices: none -> 16.6 us  [the longest x2 9.05 us: spread(): lax.all_to_all(copies, ('x', 'yl'), 0, 0, tiled=True).reshape(width, -1)]
  transfers between devices with their start and end apart: 5 -> 26, of which waited for: 5 -> 17; matrix products, arithmetic and copies ran while one was open for 2% -> 4% of each run, Pallas kernels for 0% -> 14%
where the time goes in v1:
time: 224 us; the launch traced here: 223 us
  waiting for transfers between devices  106 us (47%)
  starting transfers between devices  56.6 us (25%)
  Pallas kernels  42.9 us (19%)
  other arithmetic  9.46 us (4%)
  local copies, waits for them, and re-layouts  5.92 us (3%)
  between operations  2.26 us (1%)
    ppermute x14, waiting for transfers between devices, shift(): lax.ppermute(value, axis, [(i, (i + step) % size) for i in range(size)])  54.7 us
    pallas_call x9, Pallas kernels, call(): pl.pallas_call(body, out_shape=out_shape, in_specs=specs, out_specs=out_s...  42.9 us
    ppermute x8, waiting for transfers between devices, swap(): return lax.ppermute(value, axis, [(0, 1), (1, 0)])  23.8 us
    ppermute x8, starting transfers between devices, swap(): return lax.ppermute(value, axis, [(0, 1), (1, 0)])  20.8 us
    ppermute x14, starting transfers between devices, shift(): lax.ppermute(value, axis, [(i, (i + step) % size) for i in range(size)])  19.2 us
    all_to_all x2, waiting for transfers between devices, spread(): lax.all_to_all(copies, ('x', 'yl'), 0, 0, tiled=True).reshape(width, -1)  18.1 us
    all_to_all x2, waiting for transfers between devices, scatter(): return lax.all_to_all(summed, ('x', 'yl'), 0, 0, tiled=True)  9.52 us
    all_to_all x2, starting transfers between devices, spread(): lax.all_to_all(copies, ('x', 'yl'), 0, 0, tiled=True).reshape(width, -1)  9.05 us
  transfers between devices with their start and end apart: 26, of which 17 were waited for; matrix products, arithmetic and copies ran while one was open for 4% of the time, Pallas kernels for 14%

profile of v1, /device:TPU:1, one launch (start us, length us, event | category | flops | bytes accessed | tf_op | source)
XLA Modules:
  0.0 223.3 jit_solution(17786970223707352422)
XLA Ops:
  1.9 3.8 %collective-permute-start = (bf16[512,512]{1,0:T(8,128)(2,1)S(1)}, bf16[512,512]{1,0:T(8,128)(2,1)S(1)}, u32[]{:S(2)}, u32[]{:S(2)}) collective-permute-start(bf16[512,512]{1,0:T(8,128)(2,1)S(1)} %get-tuple-element.33.refs_1_.refs_3_), channel_id=1, source_target_pairs={{0,1},{1,0},{2,3},{3,2},{4,5},{5,4},{6,7},{7,6},{8,9},{9,8},{10,11... | collective-permute-start | bytes 1572872 | tf_op jit(solution)/shard_map/ppermute | solution.py:22
  5.7 5.6 %collective-permute-start.2 = (bf16[512,512]{1,0:T(8,128)(2,1)S(1)}, bf16[512,512]{1,0:T(8,128)(2,1)S(1)}, u32[]{:S(2)}, u32[]{:S(2)}) collective-permute-start(bf16[512,512]{1,0:T(8,128)(2,1)S(1)} %get-tuple-element.33.refs_1_.refs_3_), channel_id=1, source_target_pairs={{0,14},{2,0},{4,2},{6,4},{8,6},{10,8},{12,10},{14,12},{1,15},{3,1}... | collective-permute-start | bytes 1572872 | tf_op jit(solution)/shard_map/ppermute | solution.py:18
  12.8 3.5 %collective-permute-done.refs_3_ = bf16[512,512]{1,0:T(8,128)(2,1)S(1)} collective-permute-done((bf16[512,512]{1,0:T(8,128)(2,1)S(1)}, bf16[512,512]{1,0:T(8,128)(2,1)S(1)}, u32[]{:S(2)}, u32[]{:S(2)}) %collective-permute-start) | collective-permute-done | bytes 524320 | tf_op jit(solution)/shard_map/ppermute | solution.py:22
  16.3 3.7 %collective-permute-start.1 = (bf16[512,512]{1,0:T(8,128)(2,1)S(1)}, bf16[512,512]{1,0:T(8,128)(2,1)}, u32[]{:S(2)}, u32[]{:S(2)}) collective-permute-start(bf16[512,512]{1,0:T(8,128)(2,1)S(1)} %get-tuple-element.32.refs_2_.refs_4_), channel_id=1, source_target_pairs={{0,1},{1,0},{2,3},{3,2},{4,5},{5,4},{6,7},{7,6},{8,9},{9,8},{10,11... | collective-permute-start | bytes 1572872 | tf_op jit(solution)/shard_map/ppermute | solution.py:22
  21.6 4.0 %collective-permute-start.3 = (bf16[512,512]{1,0:T(8,128)(2,1)S(1)}, bf16[512,512]{1,0:T(8,128)(2,1)}, u32[]{:S(2)}, u32[]{:S(2)}) collective-permute-start(bf16[512,512]{1,0:T(8,128)(2,1)S(1)} %collective-permute-done.2.refs_3_.refs_5_), channel_id=1, source_target_pairs={{0,14},{2,0},{4,2},{6,4},{8,6},{10,8},{12,10},{14,12},{1,15},{3,1}... | collective-permute-start | bytes 1572872 | tf_op jit(solution)/shard_map/ppermute | solution.py:18
  25.6 7.2 %collective-permute-done.5.refs_4_.refs_6_ = bf16[512,512]{1,0:T(8,128)(2,1)S(1)} collective-permute-done((bf16[512,512]{1,0:T(8,128)(2,1)S(1)}, bf16[512,512]{1,0:T(8,128)(2,1)S(1)}, u32[]{:S(2)}, u32[]{:S(2)}) %collective-permute-start.5) | collective-permute-done | bytes 524320 | tf_op jit(solution)/shard_map/ppermute | solution.py:18
  32.8 3.5 %collective-permute-start.6 = (bf16[512,512]{1,0:T(8,128)(2,1)S(1)}, bf16[512,512]{1,0:T(8,128)(2,1)}, u32[]{:S(2)}, u32[]{:S(2)}) collective-permute-start(bf16[512,512]{1,0:T(8,128)(2,1)S(1)} %collective-permute-done.5.refs_4_.refs_6_), channel_id=1, source_target_pairs={{0,14},{2,0},{4,2},{6,4},{8,6},{10,8},{12,10},{14,12},{1,15},{3,1}... | collective-permute-start | bytes 1572872 | tf_op jit(solution)/shard_map/ppermute | solution.py:18
  36.5 3.8 %shard_map.59.refs_0_ = bf16[1024,1024]{1,0:T(8,128)(2,1)} custom-call(s32[1]{0:T(128)} %bitcast.refs_0_, bf16[512,512]{1,0:T(8,128)(2,1)} %copy-done.1, bf16[512,512]{1,0:T(8,128)(2,1)} %copy-done, bf16[512,512]{1,0:T(8,128)(2,1)} %copy-done.19, bf16[512,512]{1,0:T(8,128)(2,1)} %collective-permute-done.1.refs_4_), custom_call_target="tpu_custom_call" | custom-call | tf_op jit(solution)/shard_map/pallas_call | solution.py:58
  40.4 3.7 %collective-permute-done.3.refs_7_.refs_9_ = bf16[512,512]{1,0:T(8,128)(2,1)} collective-permute-done((bf16[512,512]{1,0:T(8,128)(2,1)S(1)}, bf16[512,512]{1,0:T(8,128)(2,1)}, u32[]{:S(2)}, u32[]{:S(2)}) %collective-permute-start.3) | collective-permute-done | bytes 524320 | tf_op jit(solution)/shard_map/ppermute | solution.py:18
  44.1 11.2 %collective-permute-done.6.refs_8_.refs_10_ = bf16[512,512]{1,0:T(8,128)(2,1)} collective-permute-done((bf16[512,512]{1,0:T(8,128)(2,1)S(1)}, bf16[512,512]{1,0:T(8,128)(2,1)}, u32[]{:S(2)}, u32[]{:S(2)}) %collective-permute-start.6) | collective-permute-done | bytes 524320 | tf_op jit(solution)/shard_map/ppermute | solution.py:18
  55.3 3.5 %collective-permute-done.12.refs_10_.refs_12_ = bf16[512,512]{1,0:T(8,128)(2,1)} collective-permute-done((bf16[512,512]{1,0:T(8,128)(2,1)S(1)}, bf16[512,512]{1,0:T(8,128)(2,1)}, u32[]{:S(2)}, u32[]{:S(2)}) %collective-permute-start.12) | collective-permute-done | bytes 524320 | tf_op jit(solution)/shard_map/ppermute | solution.py:18
  58.8 7.3 %shard_map.62 = (f32[256,2560]{1,0:T(8,128)}, bf16[256,2560]{1,0:T(8,128)(2,1)}) custom-call(bf16[1024,1024]{1,0:T(8,128)(2,1)} %shard_map.59.refs_0_, bf16[512,512]{1,0:T(8,128)(2,1)} %copy-done.1, bf16[512,512]{1,0:T(8,128)(2,1)} %copy-done, bf16[512,512]{1,0:T(8,128)(2,1)} %copy-done.6, bf16[512,512]{1,0:T(8,128)(2,1)} %copy-done.7, ...), custom_call_target="tpu_custom_call" | custom-call | tf_op jit(solution)/shard_map/pallas_call | solution.py:58
  66.2 4.5 %collective-permute-start.17 = (bf16[256,2560]{1,0:T(8,128)(2,1)}, bf16[256,2560]{1,0:T(8,128)(2,1)S(1)}, u32[]{:S(2)}, u32[]{:S(2)}) collective-permute-start(bf16[256,2560]{1,0:T(8,128)(2,1)} %get-tuple-element.20), channel_id=1, source_target_pairs={{0,16},{16,0},{1,17},{17,1},{2,18},{18,2},{3,19},{19,3},{4,20},{20... | collective-permute-start | bytes 3932168 | tf_op jit(solution)/shard_map/ppermute | solution.py:22
  73.5 3.2 %add_convert_fusion = bf16[256,2560]{1,0:T(8,128)(2,1)} fusion(f32[256,2560]{1,0:T(8,128)} %get-tuple-element.19, bf16[256,2560]{1,0:T(8,128)(2,1)S(1)} %collective-permute-done.17), kind=kLoop, calls=%fused_computation | loop fusion | flops 1966080 | bytes 5242880 | tf_op jit(solution)/shard_map/convert_element_type | solution.py:195
  76.7 7.6 %collective-permute-done.4.refs_1_.refs_3_ = bf16[512,512]{1,0:T(8,128)(2,1)S(1)} collective-permute-done((bf16[512,512]{1,0:T(8,128)(2,1)}, bf16[512,512]{1,0:T(8,128)(2,1)S(1)}, u32[]{:S(2)}, u32[]{:S(2)}) %collective-permute-start.4) | collective-permute-done | bytes 524320 | tf_op jit(solution)/shard_map/ppermute | solution.py:18
  85.2 4.0 %all-to-all-start.2 = ((bf16[8,32,2560]{2,1,0:T(8,128)(2,1)}), bf16[8,32,2560]{2,1,0:T(8,128)(2,1)S(1)}, u32[]{:S(2)}, u32[]{:S(2)}) async-start(bf16[8,32,2560]{2,1,0:T(8,128)(2,1)} %bitcast.9), calls=%async_computation.2 | async-start | bytes 2621440 | tf_op jit(solution)/shard_map/all_to_all | solution.py:198
  90.8 4.8 %collective-permute-done.7.refs_2_.refs_4_ = bf16[512,512]{1,0:T(8,128)(2,1)S(1)} collective-permute-done((bf16[512,512]{1,0:T(8,128)(2,1)}, bf16[512,512]{1,0:T(8,128)(2,1)S(1)}, u32[]{:S(2)}, u32[]{:S(2)}) %collective-permute-start.7) | collective-permute-done | bytes 524320 | tf_op jit(solution)/shard_map/ppermute | solution.py:18
  99.7 2.9 %collective-permute-done.13.refs_4_.refs_6_ = bf16[512,512]{1,0:T(8,128)(2,1)S(1)} collective-permute-done((bf16[512,512]{1,0:T(8,128)(2,1)}, bf16[512,512]{1,0:T(8,128)(2,1)S(1)}, u32[]{:S(2)}, u32[]{:S(2)}) %collective-permute-start.13) | collective-permute-done | bytes 524320 | tf_op jit(solution)/shard_map/ppermute | solution.py:18
  102.6 11.3 %collective-permute-done.14.refs_5_.refs_7_ = bf16[512,512]{1,0:T(8,128)(2,1)} collective-permute-done((bf16[512,512]{1,0:T(8,128)(2,1)S(1)}, bf16[512,512]{1,0:T(8,128)(2,1)}, u32[]{:S(2)}, u32[]{:S(2)}) %collective-permute-start.14) | collective-permute-done | bytes 524320 | tf_op jit(solution)/shard_map/ppermute | solution.py:18
  113.9 5.4 %shard_map.60 = (f32[256,1536]{1,0:T(8,128)}, bf16[256,1536]{1,0:T(8,128)(2,1)}) custom-call(bf16[1024,1024]{1,0:T(8,128)(2,1)} %shard_map.59.refs_0_, bf16[512,512]{1,0:T(8,128)(2,1)} %copy-done.10, bf16[512,512]{1,0:T(8,128)(2,1)} %copy-done.11, bf16[512,512]{1,0:T(8,128)(2,1)} %copy-done.12, bf16[512,512]{1,0:T(8,128)(2,1)} %copy-done.13, ...), custom_call_target="tpu_custom_call" | custom-call | tf_op jit(solution)/shard_map/pallas_call | solution.py:58
  123.6 2.6 %shard_map.63 = bf16[8,32,2560]{2,1,0:T(8,128)(2,1)} custom-call(bf16[8,32,2560]{2,1,0:T(8,128)(2,1)} %copy-done.4, f32[32,1]{1,0:T(8,128)} %copy.6.refs_1_, f32[1,1280]{1,0:T(1,128)} %copy-done.21), custom_call_target="tpu_custom_call" | custom-call | tf_op jit(solution)/shard_map/pallas_call | solution.py:58
  126.3 5.3 %all-to-all-start.3 = ((bf16[8,32,2560]{2,1,0:T(8,128)(2,1)}), bf16[8,32,2560]{2,1,0:T(8,128)(2,1)S(1)}, u32[]{:S(2)}, u32[]{:S(2)}) async-start(bf16[8,32,2560]{2,1,0:T(8,128)(2,1)} %shard_map.63), calls=%async_computation.3 | async-start | bytes 2621440 | tf_op jit(solution)/shard_map/all_to_all | solution.py:207
  133.7 18.1 %all-to-all-done.3 = bf16[8,32,2560]{2,1,0:T(8,128)(2,1)S(1)} async-done(((bf16[8,32,2560]{2,1,0:T(8,128)(2,1)}), bf16[8,32,2560]{2,1,0:T(8,128)(2,1)S(1)}, u32[]{:S(2)}, u32[]{:S(2)}) %all-to-all-start.3) | async-done | bytes 1310752 | tf_op jit(solution)/shard_map/all_to_all | solution.py:207
  151.9 3.5 %all-to-all-start = ((bf16[8,32,1536]{2,1,0:T(8,128)(2,1)}), bf16[8,32,1536]{2,1,0:T(8,128)(2,1)S(1)}, u32[]{:S(2)}, u32[]{:S(2)}) async-start(bf16[8,32,1536]{2,1,0:T(8,128)(2,1)} %bitcast.2), calls=%async_computation | async-start | bytes 1572864 | tf_op jit(solution)/shard_map/all_to_all | solution.py:198
  157.3 9.5 %all-to-all-done.refs_0_ = bf16[8,32,1536]{2,1,0:T(8,128)(2,1)S(1)} async-done(((bf16[8,32,1536]{2,1,0:T(8,128)(2,1)}), bf16[8,32,1536]{2,1,0:T(8,128)(2,1)S(1)}, u32[]{:S(2)}, u32[]{:S(2)}) %all-to-all-start) | async-done | bytes 786464 | tf_op jit(solution)/shard_map/all_to_all | solution.py:198
  169.9 3.8 %all-to-all-start.1 = ((bf16[8,32,1536]{2,1,0:T(8,128)(2,1)}), bf16[8,32,1536]{2,1,0:T(8,128)(2,1)S(1)}, u32[]{:S(2)}, u32[]{:S(2)}) async-start(bf16[8,32,1536]{2,1,0:T(8,128)(2,1)} %shard_map.61), calls=%async_computation.1 | async-start | bytes 1572864 | tf_op jit(solution)/shard_map/all_to_all | solution.py:207
  174.8 5.9 %shard_map.64 = (f32[1024,256]{1,0:T(8,128)}, f32[1024,256]{1,0:T(8,128)}) custom-call(s32[1]{0:T(128)} %bitcast.refs_0_, bf16[256,2560]{1,0:T(8,128)(2,1)} %bitcast.38, bf16[256,2560]{1,0:T(8,128)(2,1)} %copy-done.5, bf16[512,512]{1,0:T(8,128)(2,1)} %copy-done.1, bf16[512,512]{1,0:T(8,128)(2,1)} %copy-done, bf16[512,512]{1,0:T(8,128)(2,1)} %copy-done.6, ...), custom_call_target="tpu_custom_call" | custom-call | tf_op jit(solution)/shard_map/pallas_call | solution.py:58
  180.6 5.9 %shard_map.65 = (f32[1024,256]{1,0:T(8,128)}, f32[1024,256]{1,0:T(8,128)}) custom-call(s32[1]{0:T(128)} %bitcast.refs_0_, bf16[256,2560]{1,0:T(8,128)(2,1)} %bitcast.39, bf16[256,2560]{1,0:T(8,128)(2,1)} %copy-done.5, bf16[512,512]{1,0:T(8,128)(2,1)} %copy-done.1, bf16[512,512]{1,0:T(8,128)(2,1)} %copy-done, bf16[512,512]{1,0:T(8,128)(2,1)} %copy-done.6, ...), custom_call_target="tpu_custom_call" | custom-call | tf_op jit(solution)/shard_map/pallas_call | solution.py:58
  191.1 4.9 %shard_map.66 = (f32[1024,256]{1,0:T(8,128)}, bf16[1024,256]{1,0:T(8,128)(2,1)}) custom-call(s32[1]{0:T(128)} %bitcast.refs_0_, bf16[256,1536]{1,0:T(8,128)(2,1)} %bitcast.41, bf16[256,1536]{1,0:T(8,128)(2,1)} %copy-done.15, bf16[512,512]{1,0:T(8,128)(2,1)} %copy-done.10, bf16[512,512]{1,0:T(8,128)(2,1)} %copy-done.11, bf16[512,512]{1,0:T(8,128)(2,1)} %copy-done.12, ...), custom_call_target="tpu_custom_call" | custom-call | tf_op jit(solution)/shard_map/pallas_call | solution.py:58
  197.8 4.9 %shard_map.67 = (f32[1024,256]{1,0:T(8,128)}, bf16[1024,256]{1,0:T(8,128)(2,1)}) custom-call(s32[1]{0:T(128)} %bitcast.refs_0_, bf16[256,1536]{1,0:T(8,128)(2,1)} %bitcast.42, bf16[256,1536]{1,0:T(8,128)(2,1)} %copy-done.15, bf16[512,512]{1,0:T(8,128)(2,1)} %copy-done.10, bf16[512,512]{1,0:T(8,128)(2,1)} %copy-done.11, bf16[512,512]{1,0:T(8,128)(2,1)} %copy-done.12, ...), custom_call_target="tpu_custom_call" | custom-call | tf_op jit(solution)/shard_map/pallas_call | solution.py:58
  204.1 6.9 %collective-permute-done.20 = bf16[1024,256]{1,0:T(8,128)(2,1)S(1)} collective-permute-done((bf16[1024,256]{1,0:T(8,128)(2,1)}, bf16[1024,256]{1,0:T(8,128)(2,1)S(1)}, u32[]{:S(2)}, u32[]{:S(2)}) %collective-permute-start.20) | collective-permute-done | bytes 524320 | tf_op jit(solution)/shard_map/ppermute | solution.py:22
  212.1 10.2 %collective-permute-done.21 = bf16[1024,256]{1,0:T(8,128)(2,1)S(1)} collective-permute-done((bf16[1024,256]{1,0:T(8,128)(2,1)}, bf16[1024,256]{1,0:T(8,128)(2,1)S(1)}, u32[]{:S(2)}, u32[]{:S(2)}) %collective-permute-start.21) | collective-permute-done | bytes 524320 | tf_op jit(solution)/shard_map/ppermute | solution.py:22
  (91 shorter events, 34.9 us)
Async XLA Ops:
  1.9 34.6 %copy-start = (bf16[512,512]{1,0:T(8,128)(2,1)}, bf16[512,512]{1,0:T(8,128)(2,1)S(1)}, u32[]{:S(2)}) copy-start(bf16[512,512]{1,0:T(8,128)(2,1)S(1)} %get-tuple-element.32.refs_2_.refs_4_) | copy-start | bytes 1572868
  1.9 34.6 %copy-start.1 = (bf16[512,512]{1,0:T(8,128)(2,1)}, bf16[512,512]{1,0:T(8,128)(2,1)S(1)}, u32[]{:S(2)}) copy-start(bf16[512,512]{1,0:T(8,128)(2,1)S(1)} %get-tuple-element.33.refs_1_.refs_3_) | copy-start | bytes 1572868
  1.9 14.4 %collective-permute-start = (bf16[512,512]{1,0:T(8,128)(2,1)S(1)}, bf16[512,512]{1,0:T(8,128)(2,1)S(1)}, u32[]{:S(2)}, u32[]{:S(2)}) collective-permute-start(bf16[512,512]{1,0:T(8,128)(2,1)S(1)} %get-tuple-element.33.refs_1_.refs_3_), channel_id=1, source_target_pairs={{0,1},{1,0},{2,3},{3,2},{4,5},{5,4},{6,7},{7,6},{8,9},{9,8},{10,11... | collective-permute-start | bytes 1572872 | tf_op jit(solution)/shard_map/ppermute | solution.py:22
  5.7 15.8 %collective-permute-start.2 = (bf16[512,512]{1,0:T(8,128)(2,1)S(1)}, bf16[512,512]{1,0:T(8,128)(2,1)S(1)}, u32[]{:S(2)}, u32[]{:S(2)}) collective-permute-start(bf16[512,512]{1,0:T(8,128)(2,1)S(1)} %get-tuple-element.33.refs_1_.refs_3_), channel_id=1, source_target_pairs={{0,14},{2,0},{4,2},{6,4},{8,6},{10,8},{12,10},{14,12},{1,15},{3,1}... | collective-permute-start | bytes 1572872 | tf_op jit(solution)/shard_map/ppermute | solution.py:18
  11.3 21.5 %collective-permute-start.5 = (bf16[512,512]{1,0:T(8,128)(2,1)S(1)}, bf16[512,512]{1,0:T(8,128)(2,1)S(1)}, u32[]{:S(2)}, u32[]{:S(2)}) collective-permute-start(bf16[512,512]{1,0:T(8,128)(2,1)S(1)} %get-tuple-element.32.refs_2_.refs_4_), channel_id=1, source_target_pairs={{0,14},{2,0},{4,2},{6,4},{8,6},{10,8},{12,10},{14,12},{1,15},{3,1}... | collective-permute-start | bytes 1572872 | tf_op jit(solution)/shard_map/ppermute | solution.py:18
  12.1 24.3 %collective-permute-start.8 = (bf16[512,512]{1,0:T(8,128)(2,1)S(1)}, bf16[512,512]{1,0:T(8,128)(2,1)S(1)}, u32[]{:S(2)}, u32[]{:S(2)}) collective-permute-start(bf16[512,512]{1,0:T(8,128)(2,1)S(1)} %get-tuple-element.33.refs_1_.refs_3_), channel_id=1, source_target_pairs={{0,2},{2,4},{4,6},{6,8},{8,10},{10,12},{12,14},{14,0},{1,3},{3,5},... | collective-permute-start | bytes 1572872 | tf_op jit(solution)/shard_map/ppermute | solution.py:18
  12.8 23.6 %collective-permute-start.11 = (bf16[512,512]{1,0:T(8,128)(2,1)S(1)}, bf16[512,512]{1,0:T(8,128)(2,1)S(1)}, u32[]{:S(2)}, u32[]{:S(2)}) collective-permute-start(bf16[512,512]{1,0:T(8,128)(2,1)S(1)} %get-tuple-element.32.refs_2_.refs_4_), channel_id=1, source_target_pairs={{0,2},{2,4},{4,6},{6,8},{8,10},{10,12},{12,14},{14,0},{1,3},{3,5},... | collective-permute-start | bytes 1572872 | tf_op jit(solution)/shard_map/ppermute | solution.py:18
  16.3 20.1 %copy-start.19 = (bf16[512,512]{1,0:T(8,128)(2,1)}, bf16[512,512]{1,0:T(8,128)(2,1)S(1)}, u32[]{:S(2)}) copy-start(bf16[512,512]{1,0:T(8,128)(2,1)S(1)} %collective-permute-done.refs_3_) | copy-start | bytes 1572868
  16.3 20.2 %collective-permute-start.1 = (bf16[512,512]{1,0:T(8,128)(2,1)S(1)}, bf16[512,512]{1,0:T(8,128)(2,1)}, u32[]{:S(2)}, u32[]{:S(2)}) collective-permute-start(bf16[512,512]{1,0:T(8,128)(2,1)S(1)} %get-tuple-element.32.refs_2_.refs_4_), channel_id=1, source_target_pairs={{0,1},{1,0},{2,3},{3,2},{4,5},{5,4},{6,7},{7,6},{8,9},{9,8},{10,11... | collective-permute-start | bytes 1572872 | tf_op jit(solution)/shard_map/ppermute | solution.py:22
  21.6 22.5 %collective-permute-start.3 = (bf16[512,512]{1,0:T(8,128)(2,1)S(1)}, bf16[512,512]{1,0:T(8,128)(2,1)}, u32[]{:S(2)}, u32[]{:S(2)}) collective-permute-start(bf16[512,512]{1,0:T(8,128)(2,1)S(1)} %collective-permute-done.2.refs_3_.refs_5_), channel_id=1, source_target_pairs={{0,14},{2,0},{4,2},{6,4},{8,6},{10,8},{12,10},{14,12},{1,15},{3,1}... | collective-permute-start | bytes 1572872 | tf_op jit(solution)/shard_map/ppermute | solution.py:18
  32.8 22.5 %collective-permute-start.6 = (bf16[512,512]{1,0:T(8,128)(2,1)S(1)}, bf16[512,512]{1,0:T(8,128)(2,1)}, u32[]{:S(2)}, u32[]{:S(2)}) collective-permute-start(bf16[512,512]{1,0:T(8,128)(2,1)S(1)} %collective-permute-done.5.refs_4_.refs_6_), channel_id=1, source_target_pairs={{0,14},{2,0},{4,2},{6,4},{8,6},{10,8},{12,10},{14,12},{1,15},{3,1}... | collective-permute-start | bytes 1572872 | tf_op jit(solution)/shard_map/ppermute | solution.py:18
  36.4 18.9 %collective-permute-start.9 = (bf16[512,512]{1,0:T(8,128)(2,1)S(1)}, bf16[512,512]{1,0:T(8,128)(2,1)}, u32[]{:S(2)}, u32[]{:S(2)}) collective-permute-start(bf16[512,512]{1,0:T(8,128)(2,1)S(1)} %collective-permute-done.8.refs_5_.refs_7_), channel_id=1, source_target_pairs={{0,2},{2,4},{4,6},{6,8},{8,10},{10,12},{12,14},{14,0},{1,3},{3,5},... | collective-permute-start | bytes 1572872 | tf_op jit(solution)/shard_map/ppermute | solution.py:18
  36.4 22.4 %collective-permute-start.12 = (bf16[512,512]{1,0:T(8,128)(2,1)S(1)}, bf16[512,512]{1,0:T(8,128)(2,1)}, u32[]{:S(2)}, u32[]{:S(2)}) collective-permute-start(bf16[512,512]{1,0:T(8,128)(2,1)S(1)} %collective-permute-done.11.refs_6_.refs_8_), channel_id=1, source_target_pairs={{0,2},{2,4},{4,6},{6,8},{8,10},{10,12},{12,14},{14,0},{1,3},{3,5},... | collective-permute-start | bytes 1572872 | tf_op jit(solution)/shard_map/ppermute | solution.py:18
  66.2 7.4 %collective-permute-start.17 = (bf16[256,2560]{1,0:T(8,128)(2,1)}, bf16[256,2560]{1,0:T(8,128)(2,1)S(1)}, u32[]{:S(2)}, u32[]{:S(2)}) collective-permute-start(bf16[256,2560]{1,0:T(8,128)(2,1)} %get-tuple-element.20), channel_id=1, source_target_pairs={{0,16},{16,0},{1,17},{17,1},{2,18},{18,2},{3,19},{19,3},{4,20},{20... | collective-permute-start | bytes 3932168 | tf_op jit(solution)/shard_map/ppermute | solution.py:22
  70.7 13.7 %collective-permute-start.4 = (bf16[512,512]{1,0:T(8,128)(2,1)}, bf16[512,512]{1,0:T(8,128)(2,1)S(1)}, u32[]{:S(2)}, u32[]{:S(2)}) collective-permute-start(bf16[512,512]{1,0:T(8,128)(2,1)} %collective-permute-done.3.refs_7_.refs_9_), channel_id=1, source_target_pairs={{0,14},{2,0},{4,2},{6,4},{8,6},{10,8},{12,10},{14,12},{1,15},{3,1}... | collective-permute-start | bytes 1572872 | tf_op jit(solution)/shard_map/ppermute | solution.py:18
  70.7 24.9 %collective-permute-start.7 = (bf16[512,512]{1,0:T(8,128)(2,1)}, bf16[512,512]{1,0:T(8,128)(2,1)S(1)}, u32[]{:S(2)}, u32[]{:S(2)}) collective-permute-start(bf16[512,512]{1,0:T(8,128)(2,1)} %collective-permute-done.6.refs_8_.refs_10_), channel_id=1, source_target_pairs={{0,14},{2,0},{4,2},{6,4},{8,6},{10,8},{12,10},{14,12},{1,15},{3,1}... | collective-permute-start | bytes 1572872 | tf_op jit(solution)/shard_map/ppermute | solution.py:18
  70.7 14.5 %collective-permute-start.10 = (bf16[512,512]{1,0:T(8,128)(2,1)}, bf16[512,512]{1,0:T(8,128)(2,1)S(1)}, u32[]{:S(2)}, u32[]{:S(2)}) collective-permute-start(bf16[512,512]{1,0:T(8,128)(2,1)} %collective-permute-done.9.refs_9_.refs_11_), channel_id=1, source_target_pairs={{0,2},{2,4},{4,6},{6,8},{8,10},{10,12},{12,14},{14,0},{1,3},{3,5},... | collective-permute-start | bytes 1572872 | tf_op jit(solution)/shard_map/ppermute | solution.py:18
  76.7 20.3 %copy-start.22 = (f32[2]{0:T(128)S(1)}, f32[2]{0:T(128)}, u32[]{:S(2)}) copy-start(f32[2]{0:T(128)} %param.6) | copy-start | bytes 28
  84.4 29.5 %copy-start.10 = (bf16[512,512]{1,0:T(8,128)(2,1)}, bf16[512,512]{1,0:T(8,128)(2,1)S(1)}, u32[]{:S(2)}) copy-start(bf16[512,512]{1,0:T(8,128)(2,1)S(1)} %collective-permute-done.4.refs_1_.refs_3_) | copy-start | bytes 1572868
  85.2 28.8 %copy-start.12 = (bf16[512,512]{1,0:T(8,128)(2,1)}, bf16[512,512]{1,0:T(8,128)(2,1)S(1)}, u32[]{:S(2)}) copy-start(bf16[512,512]{1,0:T(8,128)(2,1)S(1)} %collective-permute-done.10.refs_3_.refs_5_) | copy-start | bytes 1572868
  85.2 36.8 %all-to-all-start.2 = ((bf16[8,32,2560]{2,1,0:T(8,128)(2,1)}), bf16[8,32,2560]{2,1,0:T(8,128)(2,1)S(1)}, u32[]{:S(2)}, u32[]{:S(2)}) async-start(bf16[8,32,2560]{2,1,0:T(8,128)(2,1)} %bitcast.9), calls=%async_computation.2 | async-start | bytes 2621440 | tf_op jit(solution)/shard_map/all_to_all | solution.py:198
  89.2 13.3 %collective-permute-start.13 = (bf16[512,512]{1,0:T(8,128)(2,1)}, bf16[512,512]{1,0:T(8,128)(2,1)S(1)}, u32[]{:S(2)}, u32[]{:S(2)}) collective-permute-start(bf16[512,512]{1,0:T(8,128)(2,1)} %collective-permute-done.12.refs_10_.refs_12_), channel_id=1, source_target_pairs={{0,2},{2,4},{4,6},{6,8},{8,10},{10,12},{12,14},{14,0},{1,3},{3,5},... | collective-permute-start | bytes 1572872 | tf_op jit(solution)/shard_map/ppermute | solution.py:18
  89.4 24.5 %collective-permute-start.14 = (bf16[512,512]{1,0:T(8,128)(2,1)S(1)}, bf16[512,512]{1,0:T(8,128)(2,1)}, u32[]{:S(2)}, u32[]{:S(2)}) collective-permute-start(bf16[512,512]{1,0:T(8,128)(2,1)S(1)} %collective-permute-done.10.refs_3_.refs_5_), channel_id=1, source_target_pairs={{0,2},{2,4},{4,6},{6,8},{8,10},{10,12},{12,14},{14,0},{1,3},{3,5},... | collective-permute-start | bytes 1572872 | tf_op jit(solution)/shard_map/ppermute | solution.py:18
  95.6 18.3 %collective-permute-start.15 = (bf16[512,512]{1,0:T(8,128)(2,1)S(1)}, bf16[512,512]{1,0:T(8,128)(2,1)}, u32[]{:S(2)}, u32[]{:S(2)}) collective-permute-start(bf16[512,512]{1,0:T(8,128)(2,1)S(1)} %collective-permute-done.7.refs_2_.refs_4_), channel_id=1, source_target_pairs={{0,14},{2,0},{4,2},{6,4},{8,6},{10,8},{12,10},{14,12},{1,15},{3,1}... | collective-permute-start | bytes 1572872 | tf_op jit(solution)/shard_map/ppermute | solution.py:18
  119.3 12.2 %collective-permute-start.16 = (bf16[256,1536]{1,0:T(8,128)(2,1)}, bf16[256,1536]{1,0:T(8,128)(2,1)}, u32[]{:S(2)}, u32[]{:S(2)}) collective-permute-start(bf16[256,1536]{1,0:T(8,128)(2,1)} %get-tuple-element.18), channel_id=1, source_target_pairs={{0,16},{16,0},{1,17},{17,1},{2,18},{18,2},{3,19},{19,3},{4,20},{20... | collective-permute-start | bytes 2359304 | tf_op jit(solution)/shard_map/ppermute | solution.py:22
  126.3 25.6 %all-to-all-start.3 = ((bf16[8,32,2560]{2,1,0:T(8,128)(2,1)}), bf16[8,32,2560]{2,1,0:T(8,128)(2,1)S(1)}, u32[]{:S(2)}, u32[]{:S(2)}) async-start(bf16[8,32,2560]{2,1,0:T(8,128)(2,1)} %shard_map.63), calls=%async_computation.3 | async-start | bytes 2621440 | tf_op jit(solution)/shard_map/all_to_all | solution.py:207
  151.9 14.9 %all-to-all-start = ((bf16[8,32,1536]{2,1,0:T(8,128)(2,1)}), bf16[8,32,1536]{2,1,0:T(8,128)(2,1)S(1)}, u32[]{:S(2)}, u32[]{:S(2)}) async-start(bf16[8,32,1536]{2,1,0:T(8,128)(2,1)} %bitcast.2), calls=%async_computation | async-start | bytes 1572864 | tf_op jit(solution)/shard_map/all_to_all | solution.py:198
  155.4 18.3 %collective-permute-start.18 = (bf16[256,2560]{1,0:T(8,128)(2,1)S(1)}, bf16[256,2560]{1,0:T(8,128)(2,1)S(1)}, u32[]{:S(2)}, u32[]{:S(2)}) collective-permute-start(bf16[256,2560]{1,0:T(8,128)(2,1)S(1)} %bitcast.37), channel_id=1, source_target_pairs={{0,16},{16,0},{1,17},{17,1},{2,18},{18,2},{3,19},{19,3},{4,20},{20... | collective-permute-start | bytes 3932168 | tf_op jit(solution)/shard_map/ppermute | solution.py:22
  169.9 16.6 %all-to-all-start.1 = ((bf16[8,32,1536]{2,1,0:T(8,128)(2,1)}), bf16[8,32,1536]{2,1,0:T(8,128)(2,1)S(1)}, u32[]{:S(2)}, u32[]{:S(2)}) async-start(bf16[8,32,1536]{2,1,0:T(8,128)(2,1)} %shard_map.61), calls=%async_computation.1 | async-start | bytes 1572864 | tf_op jit(solution)/shard_map/all_to_all | solution.py:207
  186.5 3.7 %collective-permute-start.19 = (bf16[256,1536]{1,0:T(8,128)(2,1)S(1)}, bf16[256,1536]{1,0:T(8,128)(2,1)S(1)}, u32[]{:S(2)}, u32[]{:S(2)}) collective-permute-start(bf16[256,1536]{1,0:T(8,128)(2,1)S(1)} %bitcast.40), channel_id=1, source_target_pairs={{0,16},{16,0},{1,17},{17,1},{2,18},{18,2},{3,19},{19,3},{4,20},{20... | collective-permute-start | bytes 2359304 | tf_op jit(solution)/shard_map/ppermute | solution.py:22
  196.1 14.9 %collective-permute-start.20 = (bf16[1024,256]{1,0:T(8,128)(2,1)}, bf16[1024,256]{1,0:T(8,128)(2,1)S(1)}, u32[]{:S(2)}, u32[]{:S(2)}) collective-permute-start(bf16[1024,256]{1,0:T(8,128)(2,1)} %get-tuple-element.29), channel_id=1, source_target_pairs={{0,1},{1,0},{2,3},{3,2},{4,5},{5,4},{6,7},{7,6},{8,9},{9,8},{10,11... | collective-permute-start | bytes 1572872 | tf_op jit(solution)/shard_map/ppermute | solution.py:22
  202.7 19.5 %collective-permute-start.21 = (bf16[1024,256]{1,0:T(8,128)(2,1)}, bf16[1024,256]{1,0:T(8,128)(2,1)S(1)}, u32[]{:S(2)}, u32[]{:S(2)}) collective-permute-start(bf16[1024,256]{1,0:T(8,128)(2,1)} %get-tuple-element.31), channel_id=1, source_target_pairs={{0,1},{1,0},{2,3},{3,2},{4,5},{5,4},{6,7},{7,6},{8,9},{9,8},{10,11... | collective-permute-start | bytes 1572872 | tf_op jit(solution)/shard_map/ppermute | solution.py:22
  (17 other events, 142.4 us)

commit v2 on v1

--- a/solution.py
+++ b/solution.py
@@ -33,7 +33,7 @@
         return self.scratch
 
 
-def call(kernel, out_shape, *args, scalar=False):
+def call(kernel, out_shape, *args, scalar=False, cost=0):
     lead = 1 if scalar else 0
     moved = args[lead:]
     count = len(moved)
@@ -61,7 +61,7 @@
         in_specs=specs,
         out_specs=out_specs,
         scratch_shapes=[pltpu.VMEM(arg.shape, arg.dtype) for arg in moved] + [pltpu.SemaphoreType.DMA((count,))],
-        cost_estimate=pl.CostEstimate(flops=0, bytes_accessed=0, transcendentals=0),
+        cost_estimate=pl.CostEstimate(flops=cost, bytes_accessed=0, transcendentals=0),
         compiler_params=pltpu.CompilerParams(vmem_limit_bytes=56 * 1024 * 1024),
     )(*args)
 
@@ -86,7 +86,7 @@
 
 def products_kernel(counts, width, *refs):
     left = refs[0].get()
-    kept, given = refs[-2:]
+    kept, given = refs[-1 - len(counts)], refs[-len(counts):]
     position = 1
     for index, count in enumerate(counts):
         parts = [ref.get() for ref in refs[position:position + count]]
@@ -106,15 +106,30 @@
                 start += rows
             place = slice((2 * index + side) * width, (2 * index + side + 1) * width)
             kept[:, place] = total[:width]
-            given[:, place] = total[width:].astype(BF16)
-
-
-def products(left, blocks, width):
+            given[index][:, side * width:(side + 1) * width] = total[width:]
+
+
+def products(left, blocks, width, cost):
     counts = [len(block) for block in blocks]
     flat = [part for block in blocks for part in block]
-    shape = (width, 2 * width * len(blocks))
-    shapes = (jax.ShapeDtypeStruct(shape, F32), jax.ShapeDtypeStruct(shape, BF16))
-    return call(functools.partial(products_kernel, counts, width), shapes, left, *flat)
+    kept = jax.ShapeDtypeStruct((width, 2 * width * len(blocks)), F32)
+    given = [jax.ShapeDtypeStruct((width, 2 * width), F32)] * len(blocks)
+    kept, *given = call(functools.partial(products_kernel, counts, width), [kept, *given], left, *flat, cost=cost)
+    return kept, given
+
+
+def sum_kernel(counts, width, *refs):
+    out = refs[-1]
+    position = 0
+    place = 0
+    for count in counts:
+        kept = refs[position].get()
+        for index in range(count):
+            columns = slice(index * 2 * width, (index + 1) * 2 * width)
+            arrived = refs[position + 1 + index].get()
+            out[:, place:place + 2 * width] = (kept[:, columns] + arrived[...]).astype(BF16)
+            place += 2 * width
+        position += count + 1
 
 
 def amplitude_kernel(count, width, copies, pieces, row_level, col_energy, out):
@@ -139,11 +154,16 @@
     return lax.dot_general(block, amps, (((1,), (1,)), ((), ())), preferred_element_type=F32)
 
 
-def gamma_kernel(count, width, step, side, add, *refs):
+def gamma_kernel(counts, width, step, side, add, *refs):
     core, mine, other = refs[0], refs[1].get(), refs[2].get()
-    flat = [ref.get() for ref in refs[3:3 + 2 * count]]
+    count = len(counts)
+    blocks = []
+    position = 3
+    for parts in counts:
+        blocks.append([ref.get() for ref in refs[position:position + parts]])
+        position += parts
     outs = refs[-2:]
-    sums = [ref.get() for ref in refs[3 + 2 * count:5 + 2 * count]] if add else None
+    sums = [ref.get() for ref in refs[position:position + 2]] if add else None
     zero = core[0] == 0
     columns = slice(width, 2 * width) if side == 0 else slice(0, width)
     for store in range(2):
@@ -152,18 +172,17 @@
         for index in range(count):
             place = slice((2 * index + side) * width, (2 * index + side + 1) * width)
             amps.append(jnp.where(chosen, mine[:, place], other[:, place]))
-        for part in range(2):
-            size = flat[part].shape[0]
-            for start in range(0, size, step):
-                rows = slice(start, start + step)
-                into = slice(part * size + start, part * size + start + step)
-                total = None
-                for index in range(count):
-                    value = contract(flat[2 * index + part][rows, columns], amps[index])
-                    total = value if total is None else total + value
-                if add:
-                    total = total + sums[store][into, :]
-                outs[store][into, :] = total.astype(outs[store].dtype)
+        for start in range(0, outs[store].shape[0], step):
+            into = slice(start, start + step)
+            total = None
+            for index, parts in enumerate(blocks):
+                size = parts[0].shape[0]
+                rows = slice(start % size, start % size + step)
+                value = contract(parts[start // size][rows, columns], amps[index])
+                total = value if total is None else total + value
+            if add:
+                total = total + sums[store][into, :]
+            outs[store][into, :] = total.astype(outs[store].dtype)
 
 
 def local(own, partner_blocks, occ_energy, virt_energy):
@@ -172,13 +191,13 @@
     depth, width = own.shape
     half = depth // 2
     rows = width // CHIPS
-    step = min(256, half)
+    step = half
     first = c == 0
     core = c.astype(jnp.int32).reshape(1)
 
     base = jnp.concatenate([own, partner_blocks[0]], axis=1)
-    base = base[:half], base[half:]
-    base_peer = tuple(swap(part, "yh") for part in base)
+    base = (base,)
+    base_peer = (swap(base[0], "yh"),)
     shape = jax.ShapeDtypeStruct((4 * width, depth), BF16)
     left = call(functools.partial(prepare_kernel, width), shape, core, *base, *base_peer, scalar=True)
     level = occ_energy[0] + occ_energy[1]
@@ -190,12 +209,16 @@
     def after(values, *others):
         return lax.optimization_barrier((values, others))[0]
 
-    def combined(blocks):
-        kept, given = products(left, blocks, width)
-        return (kept + swap(given, "c").astype(F32)).astype(BF16).reshape(CHIPS, rows, -1)
-
-    def scatter(summed):
-        return lax.all_to_all(summed, ("x", "yl"), 0, 0, tiled=True)
+    def halves(blocks, cost=0):
+        kept, given = products(left, blocks, width, cost)
+        return kept, [swap(part, "c") for part in given]
+
+    def scatter(sets):
+        counts = [len(given) for _, given in sets]
+        shape = jax.ShapeDtypeStruct((width, 2 * width * sum(counts)), BF16)
+        flat = [part for kept, given in sets for part in [kept, *given]]
+        summed = call(functools.partial(sum_kernel, counts, width), shape, *flat)
+        return lax.all_to_all(summed.reshape(CHIPS, rows, -1), ("x", "yl"), 0, 0, tiled=True)
 
     def amplitudes(group, pieces, copies):
         cols = jnp.concatenate([col_energy[d] for d in group], axis=1)
@@ -207,7 +230,7 @@
         return lax.all_to_all(copies, ("x", "yl"), 0, 0, tiled=True).reshape(width, -1)
 
     def gamma(side, blocks, mine, other, sums):
-        kernel = functools.partial(gamma_kernel, len(blocks), width, step, side, sums is not None)
+        kernel = functools.partial(gamma_kernel, [len(block) for block in blocks], width, step, side, sums is not None)
         shape = (depth, width)
         shapes = jax.ShapeDtypeStruct(shape, F32), jax.ShapeDtypeStruct(shape, F32 if sums is None else BF16)
         flat = [part for block in blocks for part in block]
@@ -219,19 +242,20 @@
     up1, down1 = both(base, 1), both(base, -1)
     up2, down2 = both(up1, 1), both(down1, -1)
     up3, down3 = both(up2, 1), both(down2, -1)
-    far = shift(up3[0], "z", NZ, 1), shift(down3[1], "z", NZ, -1)
-
-    near, distant = (0, 1, -1, 2, -2), (3, -3, 4)
-    near_blocks, distant_blocks = [base, down1, up1, down2, up2], [down3, up3, far]
-    pieces_a = scatter(after(combined(near_blocks), up3[0], down3[0]))
-    amp_a = amplitudes(near, after(pieces_a, far), CHIPS)
-    pieces_b = scatter(combined(distant_blocks))
+    far = shift(up3[0][:half], "z", NZ, 1), shift(down3[0][half:], "z", NZ, -1)
+    near, distant = (0, 1, -1), (2, -2, 3, -3, 4)
+    near_blocks, distant_blocks = [base, down1, up1], [down2, up2, down3, up3, far]
+    pieces_a = scatter([after(halves(near_blocks), up2, down2)])
+    amp_a = amplitudes(near, after(pieces_a, up3, down3), CHIPS)
     mine_a = spread(amp_a)
     other_a = swap(mine_a, "c")
+    middle_halves = halves(after(distant_blocks[:2], pieces_a))
+    last_halves = halves(distant_blocks[2:])
+    pieces_b = scatter([after(middle_halves, far), after(last_halves, mine_a)])
     sums = [gamma(side, near_blocks, mine_a, other_a, None) for side in range(2)]
-    amp_b = amplitudes(distant, pieces_b, CHIPS)
+    amp_b = amplitudes(distant, after(pieces_b, sums), CHIPS)
     mine_b = spread(amp_b)
-    other_b = swap(after(mine_b, sums), "c")
+    other_b = swap(mine_b, "c")
     outs = []
     for side in range(2):
         here, there = gamma(side, distant_blocks, mine_b, other_b, sums[side])

time: 224 us -> 211 us (0.942)
  waiting for transfers between devices: 106 us -> 79 us
  blocking collectives: 0 us -> 19.9 us
  starting transfers between devices: 56.6 us -> 44.1 us
  Pallas kernels: 42.9 us -> 51.4 us
  other arithmetic: 9.46 us -> 4.09 us
  local copies, waits for them, and re-layouts: 5.92 us -> 9.52 us
    all_to_all x0 -> x1, blocking collectives: none -> 19.9 us  [spread(): lax.all_to_all(copies, ('x', 'yl'), 0, 0, tiled=True).reshape(width, -1)]
    all_to_all x2 -> x1, waiting for transfers between devices: 18.1 us -> 0.01 us  [spread(): lax.all_to_all(copies, ('x', 'yl'), 0, 0, tiled=True).reshape(width, -1)]
    ppermute x14 -> x8, waiting for transfers between devices: 54.7 us -> 42 us  [shift(): lax.ppermute(value, axis, [(i, (i + step) % size) for i in range(size)])]
    pallas_call x9 -> x12, Pallas kernels: 42.9 us -> 51.4 us  [call(): pl.pallas_call(body, out_shape=out_shape, in_specs=specs, out_specs=out_s...]
    convert_element_type x2 -> x0, other arithmetic: 5.38 us -> none  [combined(): (kept + swap(given, 'c').astype(F32)).astype(BF16).reshape(CHIPS, rows, -1)]
    ppermute x8 -> x13, starting transfers between devices: 20.8 us -> 15.5 us  [swap(): return lax.ppermute(value, axis, [(0, 1), (1, 0)])]
    all_to_all x2 -> x1, starting transfers between devices: 9.05 us -> 3.74 us  [spread(): lax.all_to_all(copies, ('x', 'yl'), 0, 0, tiled=True).reshape(width, -1)]
    ppermute x14 -> x8, starting transfers between devices: 19.2 us -> 14.7 us  [shift(): lax.ppermute(value, axis, [(i, (i + step) % size) for i in range(size)])]
  transfers between devices with their start and end apart: 26 -> 24, of which waited for: 17 -> 14; matrix products, arithmetic and copies ran while one was open for 4% -> 2% of each run, Pallas kernels for 14% -> 18%
where the time goes in v2:
time: 211 us; the launch traced here: 210 us
  waiting for transfers between devices  79 us (37%)
  Pallas kernels  51.4 us (24%)
  starting transfers between devices  44.1 us (21%)
  blocking collectives  19.9 us (9%)
  local copies, waits for them, and re-layouts  9.52 us (5%)
  other arithmetic  4.09 us (2%)
  between operations  2.3 us (1%)
    pallas_call x12, Pallas kernels, call(): pl.pallas_call(body, out_shape=out_shape, in_specs=specs, out_specs=out_s...  51.4 us
    ppermute x8, waiting for transfers between devices, shift(): lax.ppermute(value, axis, [(i, (i + step) % size) for i in range(size)])  42 us
    ppermute x13, waiting for transfers between devices, swap(): return lax.ppermute(value, axis, [(0, 1), (1, 0)])  25.5 us
    all_to_all x1, blocking collectives, spread(): lax.all_to_all(copies, ('x', 'yl'), 0, 0, tiled=True).reshape(width, -1)  19.9 us
    ppermute x13, starting transfers between devices, swap(): return lax.ppermute(value, axis, [(0, 1), (1, 0)])  15.5 us
    ppermute x8, starting transfers between devices, shift(): lax.ppermute(value, axis, [(i, (i + step) % size) for i in range(size)])  14.7 us
    all_to_all x2, waiting for transfers between devices, scatter(): lax.all_to_all(summed.reshape(CHIPS, rows, -1), ('x', 'yl'), 0, 0, tiled=...  11.5 us
    all_to_all x2, starting transfers between devices, scatter(): lax.all_to_all(summed.reshape(CHIPS, rows, -1), ('x', 'yl'), 0, 0, tiled=...  10.2 us
  transfers between devices with their start and end apart: 24, of which 14 were waited for; matrix products, arithmetic and copies ran while one was open for 2% of the time, Pallas kernels for 18%

profile of v2, /device:TPU:1, one launch (start us, length us, event | category | flops | bytes accessed | tf_op | source)
XLA Modules:
  0.0 210.3 jit_solution(11836689632730576929)
XLA Ops:
  1.9 2.5 %collective-permute-start.3 = (bf16[1024,512]{1,0:T(8,128)(2,1)S(1)}, bf16[1024,512]{1,0:T(8,128)(2,1)S(1)}, u32[]{:S(2)}, u32[]{:S(2)}) collective-permute-start(bf16[1024,512]{1,0:T(8,128)(2,1)S(1)} %pad_maximum_fusion.refs_1_.refs_3_), channel_id=1, source_target_pairs={{0,2},{2,4},{4,6},{6,8},{8,10},{10,12},{12,14},{14,0},{1,3},{3,5},... | collective-permute-start | bytes 3145736 | tf_op jit(solution)/shard_map/ppermute | solution.py:18
  4.5 4.0 %collective-permute-start.1 = (bf16[1024,512]{1,0:T(8,128)(2,1)S(1)}, bf16[1024,512]{1,0:T(8,128)(2,1)S(1)}, u32[]{:S(2)}, u32[]{:S(2)}) collective-permute-start(bf16[1024,512]{1,0:T(8,128)(2,1)S(1)} %pad_maximum_fusion.refs_1_.refs_3_), channel_id=1, source_target_pairs={{0,14},{2,0},{4,2},{6,4},{8,6},{10,8},{12,10},{14,12},{1,15},{3,1}... | collective-permute-start | bytes 3145736 | tf_op jit(solution)/shard_map/ppermute | solution.py:18
  8.5 22.8 %collective-permute-done.3.refs_3_.refs_5_ = bf16[1024,512]{1,0:T(8,128)(2,1)S(1)} collective-permute-done((bf16[1024,512]{1,0:T(8,128)(2,1)S(1)}, bf16[1024,512]{1,0:T(8,128)(2,1)S(1)}, u32[]{:S(2)}, u32[]{:S(2)}) %collective-permute-start.3) | collective-permute-done | bytes 1048608 | tf_op jit(solution)/shard_map/ppermute | solution.py:18
  31.3 2.7 %collective-permute-start.2 = (bf16[1024,512]{1,0:T(8,128)(2,1)S(1)}, bf16[1024,512]{1,0:T(8,128)(2,1)}, u32[]{:S(2)}, u32[]{:S(2)}) collective-permute-start(bf16[1024,512]{1,0:T(8,128)(2,1)S(1)} %collective-permute-done.1.refs_2_.refs_4_), channel_id=1, source_target_pairs={{0,14},{2,0},{4,2},{6,4},{8,6},{10,8},{12,10},{14,12},{1,15},{3,1}... | collective-permute-start | bytes 3145736 | tf_op jit(solution)/shard_map/ppermute | solution.py:18
  34.0 2.9 %collective-permute-start = (bf16[1024,512]{1,0:T(8,128)(2,1)S(1)}, bf16[1024,512]{1,0:T(8,128)(2,1)}, u32[]{:S(2)}, u32[]{:S(2)}) collective-permute-start(bf16[1024,512]{1,0:T(8,128)(2,1)S(1)} %pad_maximum_fusion.refs_1_.refs_3_), channel_id=1, source_target_pairs={{0,1},{1,0},{2,3},{3,2},{4,5},{5,4},{6,7},{7,6},{8,9},{9,8},{10,11... | collective-permute-start | bytes 3145736 | tf_op jit(solution)/shard_map/ppermute | solution.py:22
  36.9 19.1 %collective-permute-done.4.refs_2_.refs_4_ = bf16[1024,512]{1,0:T(8,128)(2,1)} collective-permute-done((bf16[1024,512]{1,0:T(8,128)(2,1)S(1)}, bf16[1024,512]{1,0:T(8,128)(2,1)}, u32[]{:S(2)}, u32[]{:S(2)}) %collective-permute-start.4) | collective-permute-done | bytes 1048608 | tf_op jit(solution)/shard_map/ppermute | solution.py:18
  56.1 2.7 %collective-permute-start.12 = (bf16[1024,512]{1,0:T(8,128)(2,1)}, bf16[1024,512]{1,0:T(8,128)(2,1)S(1)}, u32[]{:S(2)}, u32[]{:S(2)}) collective-permute-start(bf16[1024,512]{1,0:T(8,128)(2,1)} %collective-permute-done.2.refs_1_.refs_3_), channel_id=1, source_target_pairs={{0,14},{2,0},{4,2},{6,4},{8,6},{10,8},{12,10},{14,12},{1,15},{3,1}... | collective-permute-start | bytes 3145736 | tf_op jit(solution)/shard_map/ppermute | solution.py:18
  58.8 3.7 %shard_map.59.refs_0_ = bf16[1024,1024]{1,0:T(8,128)(2,1)} custom-call(s32[1]{0:T(128)} %bitcast.refs_0_, bf16[1024,512]{1,0:T(8,128)(2,1)} %copy-done, bf16[1024,512]{1,0:T(8,128)(2,1)} %collective-permute-done.refs_2_), custom_call_target="tpu_custom_call" | custom-call | tf_op jit(solution)/shard_map/pallas_call | solution.py:58
  62.5 5.3 %shard_map.60 = (f32[256,1536]{1,0:T(8,128)}, f32[256,512]{1,0:T(8,128)}, f32[256,512]{1,0:T(8,128)}, f32[256,512]{1,0:T(8,128)}) custom-call(bf16[1024,1024]{1,0:T(8,128)(2,1)} %shard_map.59.refs_0_, bf16[1024,512]{1,0:T(8,128)(2,1)} %copy-done, bf16[1024,512]{1,0:T(8,128)(2,1)} %copy-done.5, bf16[1024,512]{1,0:T(8,128)(2,1)} %copy-done.4), custom_call_target="tpu_custom_call" | custom-call | tf_op jit(solution)/shard_map/pallas_call | solution.py:58
  67.8 2.8 %collective-permute-start.5 = (f32[256,512]{1,0:T(8,128)}, f32[256,512]{1,0:T(8,128)S(1)}, u32[]{:S(2)}, u32[]{:S(2)}) collective-permute-start(f32[256,512]{1,0:T(8,128)} %get-tuple-element.37), channel_id=1, source_target_pairs={{0,16},{16,0},{1,17},{17,1},{2,18},{18,2},{3,19},{19,3},{4,20},{20... | collective-permute-start | bytes 1572872 | tf_op jit(solution)/shard_map/ppermute | solution.py:22
  74.6 2.8 %shard_map.61 = bf16[256,1536]{1,0:T(8,128)(2,1)} custom-call(f32[256,1536]{1,0:T(8,128)} %get-tuple-element.40.refs_0_, f32[256,512]{1,0:T(8,128)} %copy-done.19, f32[256,512]{1,0:T(8,128)} %copy-done.20, f32[256,512]{1,0:T(8,128)} %copy-done.21), custom_call_target="tpu_custom_call" | custom-call | tf_op jit(solution)/shard_map/pallas_call | solution.py:58
  77.4 5.0 %all-to-all-start = ((bf16[8,32,1536]{2,1,0:T(8,128)(2,1)}), bf16[8,32,1536]{2,1,0:T(8,128)(2,1)}, u32[]{:S(2)}, u32[]{:S(2)}) async-start(bf16[8,32,1536]{2,1,0:T(8,128)(2,1)} %bitcast.44), calls=%async_computation | async-start | bytes 1572864 | tf_op jit(solution)/shard_map/all_to_all | solution.py:221
  84.3 2.7 %collective-permute-start.13 = (bf16[512,512]{1,0:T(8,128)(2,1)}, bf16[512,512]{1,0:T(8,128)(2,1)S(1)}, u32[]{:S(2)}, u32[]{:S(2)}) collective-permute-start(bf16[512,512]{1,0:T(8,128)(2,1)} %slice.17), channel_id=1, source_target_pairs={{0,14},{2,0},{4,2},{6,4},{8,6},{10,8},{12,10},{14,12},{1,15},{3,1}... | collective-permute-start | bytes 1572872 | tf_op jit(solution)/shard_map/ppermute | solution.py:18
  90.3 4.2 %all-to-all-done.refs_0_ = bf16[8,32,1536]{2,1,0:T(8,128)(2,1)} async-done(((bf16[8,32,1536]{2,1,0:T(8,128)(2,1)}), bf16[8,32,1536]{2,1,0:T(8,128)(2,1)}, u32[]{:S(2)}, u32[]{:S(2)}) %all-to-all-start) | async-done | bytes 786464 | tf_op jit(solution)/shard_map/all_to_all | solution.py:221
  94.5 2.2 %shard_map.64 = bf16[8,32,1536]{2,1,0:T(8,128)(2,1)} custom-call(bf16[8,32,1536]{2,1,0:T(8,128)(2,1)} %all-to-all-done.refs_0_, f32[32,1]{1,0:T(8,128)} %copy.6.refs_1_, f32[1,768]{1,0:T(1,128)} %pad_maximum_fusion.1.refs_2_), custom_call_target="tpu_custom_call" | custom-call | tf_op jit(solution)/shard_map/pallas_call | solution.py:58
  96.7 3.7 %all-to-all-start.1 = ((bf16[8,32,1536]{2,1,0:T(8,128)(2,1)}), bf16[8,32,1536]{2,1,0:T(8,128)(2,1)S(1)}, u32[]{:S(2)}, u32[]{:S(2)}) async-start(bf16[8,32,1536]{2,1,0:T(8,128)(2,1)} %shard_map.64), calls=%async_computation.1 | async-start | bytes 1572864 | tf_op jit(solution)/shard_map/all_to_all | solution.py:230
  100.5 4.4 %shard_map.62 = (f32[256,1024]{1,0:T(8,128)}, f32[256,512]{1,0:T(8,128)}, f32[256,512]{1,0:T(8,128)}) custom-call(bf16[1024,1024]{1,0:T(8,128)(2,1)} %shard_map.59.refs_0_, bf16[1024,512]{1,0:T(8,128)(2,1)} %collective-permute-done.2.refs_1_.refs_3_, bf16[1024,512]{1,0:T(8,128)(2,1)} %collective-permute-done.4.refs_2_.refs_4_), custom_call_target="tpu_custom_call" | custom-call | tf_op jit(solution)/shard_map/pallas_call | solution.py:58
  108.1 5.3 %shard_map.63 = (f32[256,1536]{1,0:T(8,128)}, f32[256,512]{1,0:T(8,128)}, f32[256,512]{1,0:T(8,128)}, f32[256,512]{1,0:T(8,128)}) custom-call(bf16[1024,1024]{1,0:T(8,128)(2,1)} %shard_map.59.refs_0_, bf16[1024,512]{1,0:T(8,128)(2,1)} %copy-done.2, bf16[1024,512]{1,0:T(8,128)(2,1)} %copy-done.1, bf16[512,512]{1,0:T(8,128)(2,1)} %copy-done.9, ...), custom_call_target="tpu_custom_call" | custom-call | tf_op jit(solution)/shard_map/pallas_call | solution.py:58
  118.0 3.7 %shard_map.65 = bf16[256,2560]{1,0:T(8,128)(2,1)} custom-call(f32[256,1024]{1,0:T(8,128)} %get-tuple-element.49.refs_0_, f32[256,512]{1,0:T(8,128)} %copy-done.14, f32[256,512]{1,0:T(8,128)} %copy-done.15, f32[256,1536]{1,0:T(8,128)} %get-tuple-element.57.refs_3_, f32[256,512]{1,0:T(8,128)} %copy-done.16, f32[256,512]{1,0:T(8,128)} %copy-done.17, ...), custom_call_target="tpu_custom_call" | custom-call | tf_op jit(solution)/shard_map/pallas_call | solution.py:58
  121.7 5.2 %all-to-all-start.2 = ((bf16[8,32,2560]{2,1,0:T(8,128)(2,1)}), bf16[8,32,2560]{2,1,0:T(8,128)(2,1)S(1)}, u32[]{:S(2)}, u32[]{:S(2)}) async-start(bf16[8,32,2560]{2,1,0:T(8,128)(2,1)} %bitcast.43), calls=%async_computation.2 | async-start | bytes 2621440 | tf_op jit(solution)/shard_map/all_to_all | solution.py:221
  130.4 4.4 %shard_map.66 = (f32[1024,256]{1,0:T(8,128)}, f32[1024,256]{1,0:T(8,128)}) custom-call(s32[1]{0:T(128)} %bitcast.refs_0_, bf16[256,1536]{1,0:T(8,128)(2,1)} %bitcast.41, bf16[256,1536]{1,0:T(8,128)(2,1)} %copy-done.11, bf16[1024,512]{1,0:T(8,128)(2,1)} %copy-done, bf16[1024,512]{1,0:T(8,128)(2,1)} %copy-done.5, bf16[1024,512]{1,0:T(8,128)(2,1)} %copy-done.4), custom_call_target="tpu_custom_call" | custom-call | tf_op jit(solution)/shard_map/pallas_call | solution.py:58
  134.8 4.4 %shard_map.67 = (f32[1024,256]{1,0:T(8,128)}, f32[1024,256]{1,0:T(8,128)}) custom-call(s32[1]{0:T(128)} %bitcast.refs_0_, bf16[256,1536]{1,0:T(8,128)(2,1)} %bitcast.42, bf16[256,1536]{1,0:T(8,128)(2,1)} %copy-done.11, bf16[1024,512]{1,0:T(8,128)(2,1)} %copy-done, bf16[1024,512]{1,0:T(8,128)(2,1)} %copy-done.5, bf16[1024,512]{1,0:T(8,128)(2,1)} %copy-done.4), custom_call_target="tpu_custom_call" | custom-call | tf_op jit(solution)/shard_map/pallas_call | solution.py:58
  139.2 7.4 %all-to-all-done.2.refs_0_ = bf16[8,32,2560]{2,1,0:T(8,128)(2,1)S(1)} async-done(((bf16[8,32,2560]{2,1,0:T(8,128)(2,1)}), bf16[8,32,2560]{2,1,0:T(8,128)(2,1)S(1)}, u32[]{:S(2)}, u32[]{:S(2)}) %all-to-all-start.2) | async-done | bytes 1310752 | tf_op jit(solution)/shard_map/all_to_all | solution.py:221
  147.7 2.6 %shard_map.68 = bf16[8,32,2560]{2,1,0:T(8,128)(2,1)} custom-call(bf16[8,32,2560]{2,1,0:T(8,128)(2,1)} %copy-done.8, f32[32,1]{1,0:T(8,128)} %copy.6.refs_1_, f32[1,1280]{1,0:T(1,128)} %copy-done.23), custom_call_target="tpu_custom_call" | custom-call | tf_op jit(solution)/shard_map/pallas_call | solution.py:58
  150.4 19.9 %all_to_all.20 = bf16[8,32,2560]{2,1,0:T(8,128)(2,1)S(1)} all-to-all(bf16[8,32,2560]{2,1,0:T(8,128)(2,1)} %shard_map.68), channel_id=1, replica_groups=mesh['x'=4,'yl'=2,'c'=2,'z'=8,'yh'=2] {'x','yl'}, dimensions={0} | all-to-all | bytes 2621440 | tf_op jit(solution)/shard_map/all_to_all | solution.py:230
  170.3 2.7 %collective-permute-start.18 = (bf16[256,2560]{1,0:T(8,128)(2,1)S(1)}, bf16[256,2560]{1,0:T(8,128)(2,1)S(1)}, u32[]{:S(2)}, u32[]{:S(2)}) collective-permute-start(bf16[256,2560]{1,0:T(8,128)(2,1)S(1)} %bitcast.37), channel_id=1, source_target_pairs={{0,16},{16,0},{1,17},{17,1},{2,18},{18,2},{3,19},{19,3},{4,20},{20... | collective-permute-start | bytes 3932168 | tf_op jit(solution)/shard_map/ppermute | solution.py:22
  173.0 2.7 %collective-permute-done.18.refs_2_ = bf16[256,2560]{1,0:T(8,128)(2,1)S(1)} collective-permute-done((bf16[256,2560]{1,0:T(8,128)(2,1)S(1)}, bf16[256,2560]{1,0:T(8,128)(2,1)S(1)}, u32[]{:S(2)}, u32[]{:S(2)}) %collective-permute-start.18) | collective-permute-done | bytes 1310752 | tf_op jit(solution)/shard_map/ppermute | solution.py:22
  176.7 6.3 %shard_map.69 = (f32[1024,256]{1,0:T(8,128)}, bf16[1024,256]{1,0:T(8,128)(2,1)}) custom-call(s32[1]{0:T(128)} %bitcast.refs_0_, bf16[256,2560]{1,0:T(8,128)(2,1)} %bitcast.38, bf16[256,2560]{1,0:T(8,128)(2,1)} %copy-done.7, bf16[1024,512]{1,0:T(8,128)(2,1)} %collective-permute-done.2.refs_1_.refs_3_, ...), custom_call_target="tpu_custom_call" | custom-call | tf_op jit(solution)/shard_map/pallas_call | solution.py:58
  183.0 2.7 %collective-permute-start.19 = (bf16[1024,256]{1,0:T(8,128)(2,1)}, bf16[1024,256]{1,0:T(8,128)(2,1)S(1)}, u32[]{:S(2)}, u32[]{:S(2)}) collective-permute-start(bf16[1024,256]{1,0:T(8,128)(2,1)} %get-tuple-element.67), channel_id=1, source_target_pairs={{0,1},{1,0},{2,3},{3,2},{4,5},{5,4},{6,7},{7,6},{8,9},{9,8},{10,11... | collective-permute-start | bytes 1572872 | tf_op jit(solution)/shard_map/ppermute | solution.py:22
  185.8 6.3 %shard_map.70 = (f32[1024,256]{1,0:T(8,128)}, bf16[1024,256]{1,0:T(8,128)(2,1)}) custom-call(s32[1]{0:T(128)} %bitcast.refs_0_, bf16[256,2560]{1,0:T(8,128)(2,1)} %bitcast.39, bf16[256,2560]{1,0:T(8,128)(2,1)} %copy-done.7, bf16[1024,512]{1,0:T(8,128)(2,1)} %collective-permute-done.2.refs_1_.refs_3_, ...), custom_call_target="tpu_custom_call" | custom-call | tf_op jit(solution)/shard_map/pallas_call | solution.py:58
  192.5 5.5 %collective-permute-done.19 = bf16[1024,256]{1,0:T(8,128)(2,1)S(1)} collective-permute-done((bf16[1024,256]{1,0:T(8,128)(2,1)}, bf16[1024,256]{1,0:T(8,128)(2,1)S(1)}, u32[]{:S(2)}, u32[]{:S(2)}) %collective-permute-start.19) | collective-permute-done | bytes 524320 | tf_op jit(solution)/shard_map/ppermute | solution.py:22
  199.1 10.2 %collective-permute-done.20 = bf16[1024,256]{1,0:T(8,128)(2,1)S(1)} collective-permute-done((bf16[1024,256]{1,0:T(8,128)(2,1)}, bf16[1024,256]{1,0:T(8,128)(2,1)S(1)}, u32[]{:S(2)}, u32[]{:S(2)}) %collective-permute-start.20) | collective-permute-done | bytes 524320 | tf_op jit(solution)/shard_map/ppermute | solution.py:22
  (95 shorter events, 25.2 us)
Async XLA Ops:
  1.9 56.9 %copy-start = (bf16[1024,512]{1,0:T(8,128)(2,1)}, bf16[1024,512]{1,0:T(8,128)(2,1)S(1)}, u32[]{:S(2)}) copy-start(bf16[1024,512]{1,0:T(8,128)(2,1)S(1)} %pad_maximum_fusion.refs_1_.refs_3_) | copy-start | bytes 3145732
  1.9 29.4 %collective-permute-start.3 = (bf16[1024,512]{1,0:T(8,128)(2,1)S(1)}, bf16[1024,512]{1,0:T(8,128)(2,1)S(1)}, u32[]{:S(2)}, u32[]{:S(2)}) collective-permute-start(bf16[1024,512]{1,0:T(8,128)(2,1)S(1)} %pad_maximum_fusion.refs_1_.refs_3_), channel_id=1, source_target_pairs={{0,2},{2,4},{4,6},{6,8},{8,10},{10,12},{12,14},{14,0},{1,3},{3,5},... | collective-permute-start | bytes 3145736 | tf_op jit(solution)/shard_map/ppermute | solution.py:18
  4.5 26.8 %collective-permute-start.1 = (bf16[1024,512]{1,0:T(8,128)(2,1)S(1)}, bf16[1024,512]{1,0:T(8,128)(2,1)S(1)}, u32[]{:S(2)}, u32[]{:S(2)}) collective-permute-start(bf16[1024,512]{1,0:T(8,128)(2,1)S(1)} %pad_maximum_fusion.refs_1_.refs_3_), channel_id=1, source_target_pairs={{0,14},{2,0},{4,2},{6,4},{8,6},{10,8},{12,10},{14,12},{1,15},{3,1}... | collective-permute-start | bytes 3145736 | tf_op jit(solution)/shard_map/ppermute | solution.py:18
  31.3 24.7 %copy-start.4 = (bf16[1024,512]{1,0:T(8,128)(2,1)}, bf16[1024,512]{1,0:T(8,128)(2,1)S(1)}, u32[]{:S(2)}) copy-start(bf16[1024,512]{1,0:T(8,128)(2,1)S(1)} %collective-permute-done.3.refs_3_.refs_5_) | copy-start | bytes 3145732
  31.3 24.7 %collective-permute-start.4 = (bf16[1024,512]{1,0:T(8,128)(2,1)S(1)}, bf16[1024,512]{1,0:T(8,128)(2,1)}, u32[]{:S(2)}, u32[]{:S(2)}) collective-permute-start(bf16[1024,512]{1,0:T(8,128)(2,1)S(1)} %collective-permute-done.3.refs_3_.refs_5_), channel_id=1, source_target_pairs={{0,2},{2,4},{4,6},{6,8},{8,10},{10,12},{12,14},{14,0},{1,3},{3,5},... | collective-permute-start | bytes 3145736 | tf_op jit(solution)/shard_map/ppermute | solution.py:18
  31.3 24.7 %copy-start.5 = (bf16[1024,512]{1,0:T(8,128)(2,1)}, bf16[1024,512]{1,0:T(8,128)(2,1)S(1)}, u32[]{:S(2)}) copy-start(bf16[1024,512]{1,0:T(8,128)(2,1)S(1)} %collective-permute-done.1.refs_2_.refs_4_) | copy-start | bytes 3145732
  31.3 24.7 %collective-permute-start.2 = (bf16[1024,512]{1,0:T(8,128)(2,1)S(1)}, bf16[1024,512]{1,0:T(8,128)(2,1)}, u32[]{:S(2)}, u32[]{:S(2)}) collective-permute-start(bf16[1024,512]{1,0:T(8,128)(2,1)S(1)} %collective-permute-done.1.refs_2_.refs_4_), channel_id=1, source_target_pairs={{0,14},{2,0},{4,2},{6,4},{8,6},{10,8},{12,10},{14,12},{1,15},{3,1}... | collective-permute-start | bytes 3145736 | tf_op jit(solution)/shard_map/ppermute | solution.py:18
  34.0 24.8 %collective-permute-start = (bf16[1024,512]{1,0:T(8,128)(2,1)S(1)}, bf16[1024,512]{1,0:T(8,128)(2,1)}, u32[]{:S(2)}, u32[]{:S(2)}) collective-permute-start(bf16[1024,512]{1,0:T(8,128)(2,1)S(1)} %pad_maximum_fusion.refs_1_.refs_3_), channel_id=1, source_target_pairs={{0,1},{1,0},{2,3},{3,2},{4,5},{5,4},{6,7},{7,6},{8,9},{9,8},{10,11... | collective-permute-start | bytes 3145736 | tf_op jit(solution)/shard_map/ppermute | solution.py:22
  56.0 26.4 %collective-permute-start.10 = (bf16[1024,512]{1,0:T(8,128)(2,1)}, bf16[1024,512]{1,0:T(8,128)(2,1)S(1)}, u32[]{:S(2)}, u32[]{:S(2)}) collective-permute-start(bf16[1024,512]{1,0:T(8,128)(2,1)} %collective-permute-done.4.refs_2_.refs_4_), channel_id=1, source_target_pairs={{0,2},{2,4},{4,6},{6,8},{8,10},{10,12},{12,14},{14,0},{1,3},{3,5},... | collective-permute-start | bytes 3145736 | tf_op jit(solution)/shard_map/ppermute | solution.py:18
  56.1 27.3 %collective-permute-start.12 = (bf16[1024,512]{1,0:T(8,128)(2,1)}, bf16[1024,512]{1,0:T(8,128)(2,1)S(1)}, u32[]{:S(2)}, u32[]{:S(2)}) collective-permute-start(bf16[1024,512]{1,0:T(8,128)(2,1)} %collective-permute-done.2.refs_1_.refs_3_), channel_id=1, source_target_pairs={{0,14},{2,0},{4,2},{6,4},{8,6},{10,8},{12,10},{14,12},{1,15},{3,1}... | collective-permute-start | bytes 3145736 | tf_op jit(solution)/shard_map/ppermute | solution.py:18
  67.8 4.5 %collective-permute-start.5 = (f32[256,512]{1,0:T(8,128)}, f32[256,512]{1,0:T(8,128)S(1)}, u32[]{:S(2)}, u32[]{:S(2)}) collective-permute-start(f32[256,512]{1,0:T(8,128)} %get-tuple-element.37), channel_id=1, source_target_pairs={{0,16},{16,0},{1,17},{17,1},{2,18},{18,2},{3,19},{19,3},{4,20},{20... | collective-permute-start | bytes 1572872 | tf_op jit(solution)/shard_map/ppermute | solution.py:22
  70.6 2.5 %collective-permute-start.6 = (f32[256,512]{1,0:T(8,128)}, f32[256,512]{1,0:T(8,128)S(1)}, u32[]{:S(2)}, u32[]{:S(2)}) collective-permute-start(f32[256,512]{1,0:T(8,128)} %get-tuple-element.38), channel_id=1, source_target_pairs={{0,16},{16,0},{1,17},{17,1},{2,18},{18,2},{3,19},{19,3},{4,20},{20... | collective-permute-start | bytes 1572872 | tf_op jit(solution)/shard_map/ppermute | solution.py:22
  70.7 3.1 %collective-permute-start.7 = (f32[256,512]{1,0:T(8,128)}, f32[256,512]{1,0:T(8,128)S(1)}, u32[]{:S(2)}, u32[]{:S(2)}) collective-permute-start(f32[256,512]{1,0:T(8,128)} %get-tuple-element.39), channel_id=1, source_target_pairs={{0,16},{16,0},{1,17},{17,1},{2,18},{18,2},{3,19},{19,3},{4,20},{20... | collective-permute-start | bytes 1572872 | tf_op jit(solution)/shard_map/ppermute | solution.py:22
  77.4 17.1 %all-to-all-start = ((bf16[8,32,1536]{2,1,0:T(8,128)(2,1)}), bf16[8,32,1536]{2,1,0:T(8,128)(2,1)}, u32[]{:S(2)}, u32[]{:S(2)}) async-start(bf16[8,32,1536]{2,1,0:T(8,128)(2,1)} %bitcast.44), calls=%async_computation | async-start | bytes 1572864 | tf_op jit(solution)/shard_map/all_to_all | solution.py:221
  82.5 14.2 %copy-start.1 = (bf16[1024,512]{1,0:T(8,128)(2,1)}, bf16[1024,512]{1,0:T(8,128)(2,1)S(1)}, u32[]{:S(2)}) copy-start(bf16[1024,512]{1,0:T(8,128)(2,1)S(1)} %collective-permute-done.10.refs_2_.refs_6_) | copy-start | bytes 3145732
  83.4 23.1 %collective-permute-start.11 = (bf16[512,512]{1,0:T(8,128)(2,1)}, bf16[512,512]{1,0:T(8,128)(2,1)S(1)}, u32[]{:S(2)}, u32[]{:S(2)}) collective-permute-start(bf16[512,512]{1,0:T(8,128)(2,1)} %slice.16), channel_id=1, source_target_pairs={{0,2},{2,4},{4,6},{6,8},{8,10},{10,12},{12,14},{14,0},{1,3},{3,5},... | collective-permute-start | bytes 1572872 | tf_op jit(solution)/shard_map/ppermute | solution.py:18
  83.4 13.4 %copy-start.2 = (bf16[1024,512]{1,0:T(8,128)(2,1)}, bf16[1024,512]{1,0:T(8,128)(2,1)S(1)}, u32[]{:S(2)}) copy-start(bf16[1024,512]{1,0:T(8,128)(2,1)S(1)} %collective-permute-done.12.refs_1_.refs_5_) | copy-start | bytes 3145732
  84.3 22.2 %collective-permute-start.13 = (bf16[512,512]{1,0:T(8,128)(2,1)}, bf16[512,512]{1,0:T(8,128)(2,1)S(1)}, u32[]{:S(2)}, u32[]{:S(2)}) collective-permute-start(bf16[512,512]{1,0:T(8,128)(2,1)} %slice.17), channel_id=1, source_target_pairs={{0,14},{2,0},{4,2},{6,4},{8,6},{10,8},{12,10},{14,12},{1,15},{3,1}... | collective-permute-start | bytes 1572872 | tf_op jit(solution)/shard_map/ppermute | solution.py:18
  96.7 17.7 %all-to-all-start.1 = ((bf16[8,32,1536]{2,1,0:T(8,128)(2,1)}), bf16[8,32,1536]{2,1,0:T(8,128)(2,1)S(1)}, u32[]{:S(2)}, u32[]{:S(2)}) async-start(bf16[8,32,1536]{2,1,0:T(8,128)(2,1)} %shard_map.64), calls=%async_computation.1 | async-start | bytes 1572864 | tf_op jit(solution)/shard_map/all_to_all | solution.py:230
  104.9 9.6 %collective-permute-start.8 = (f32[256,512]{1,0:T(8,128)}, f32[256,512]{1,0:T(8,128)S(1)}, u32[]{:S(2)}, u32[]{:S(2)}) collective-permute-start(f32[256,512]{1,0:T(8,128)} %get-tuple-element.47), channel_id=1, source_target_pairs={{0,16},{16,0},{1,17},{17,1},{2,18},{18,2},{3,19},{19,3},{4,20},{20... | collective-permute-start | bytes 1572872 | tf_op jit(solution)/shard_map/ppermute | solution.py:22
  106.4 8.0 %collective-permute-start.9 = (f32[256,512]{1,0:T(8,128)}, f32[256,512]{1,0:T(8,128)S(1)}, u32[]{:S(2)}, u32[]{:S(2)}) collective-permute-start(f32[256,512]{1,0:T(8,128)} %get-tuple-element.48), channel_id=1, source_target_pairs={{0,16},{16,0},{1,17},{17,1},{2,18},{18,2},{3,19},{19,3},{4,20},{20... | collective-permute-start | bytes 1572872 | tf_op jit(solution)/shard_map/ppermute | solution.py:22
  113.4 2.2 %collective-permute-start.14 = (f32[256,512]{1,0:T(8,128)}, f32[256,512]{1,0:T(8,128)S(1)}, u32[]{:S(2)}, u32[]{:S(2)}) collective-permute-start(f32[256,512]{1,0:T(8,128)} %get-tuple-element.53), channel_id=1, source_target_pairs={{0,16},{16,0},{1,17},{17,1},{2,18},{18,2},{3,19},{19,3},{4,20},{20... | collective-permute-start | bytes 1572872 | tf_op jit(solution)/shard_map/ppermute | solution.py:22
  113.9 2.5 %collective-permute-start.15 = (f32[256,512]{1,0:T(8,128)}, f32[256,512]{1,0:T(8,128)S(1)}, u32[]{:S(2)}, u32[]{:S(2)}) collective-permute-start(f32[256,512]{1,0:T(8,128)} %get-tuple-element.54), channel_id=1, source_target_pairs={{0,16},{16,0},{1,17},{17,1},{2,18},{18,2},{3,19},{19,3},{4,20},{20... | collective-permute-start | bytes 1572872 | tf_op jit(solution)/shard_map/ppermute | solution.py:22
  114.0 3.1 %collective-permute-start.16 = (f32[256,512]{1,0:T(8,128)}, f32[256,512]{1,0:T(8,128)S(1)}, u32[]{:S(2)}, u32[]{:S(2)}) collective-permute-start(f32[256,512]{1,0:T(8,128)} %get-tuple-element.55), channel_id=1, source_target_pairs={{0,16},{16,0},{1,17},{17,1},{2,18},{18,2},{3,19},{19,3},{4,20},{20... | collective-permute-start | bytes 1572872 | tf_op jit(solution)/shard_map/ppermute | solution.py:22
  114.5 12.4 %copy-start.6 = (bf16[8,32,1536]{2,1,0:T(8,128)(2,1)}, bf16[8,32,1536]{2,1,0:T(8,128)(2,1)S(1)}, u32[]{:S(2)}) copy-start(bf16[8,32,1536]{2,1,0:T(8,128)(2,1)S(1)} %all-to-all-done.1) | copy-start | bytes 2359300
  121.7 24.9 %all-to-all-start.2 = ((bf16[8,32,2560]{2,1,0:T(8,128)(2,1)}), bf16[8,32,2560]{2,1,0:T(8,128)(2,1)S(1)}, u32[]{:S(2)}, u32[]{:S(2)}) async-start(bf16[8,32,2560]{2,1,0:T(8,128)(2,1)} %bitcast.43), calls=%async_computation.2 | async-start | bytes 2621440 | tf_op jit(solution)/shard_map/all_to_all | solution.py:221
  126.9 2.7 %collective-permute-start.17 = (bf16[256,1536]{1,0:T(8,128)(2,1)S(1)}, bf16[256,1536]{1,0:T(8,128)(2,1)S(1)}, u32[]{:S(2)}, u32[]{:S(2)}) collective-permute-start(bf16[256,1536]{1,0:T(8,128)(2,1)S(1)} %bitcast.40), channel_id=1, source_target_pairs={{0,16},{16,0},{1,17},{17,1},{2,18},{18,2},{3,19},{19,3},{4,20},{20... | collective-permute-start | bytes 2359304 | tf_op jit(solution)/shard_map/ppermute | solution.py:22
  170.3 5.4 %collective-permute-start.18 = (bf16[256,2560]{1,0:T(8,128)(2,1)S(1)}, bf16[256,2560]{1,0:T(8,128)(2,1)S(1)}, u32[]{:S(2)}, u32[]{:S(2)}) collective-permute-start(bf16[256,2560]{1,0:T(8,128)(2,1)S(1)} %bitcast.37), channel_id=1, source_target_pairs={{0,16},{16,0},{1,17},{17,1},{2,18},{18,2},{3,19},{19,3},{4,20},{20... | collective-permute-start | bytes 3932168 | tf_op jit(solution)/shard_map/ppermute | solution.py:22
  183.0 14.9 %copy-start.12 = (f32[1024,256]{1,0:T(8,128)S(1)}, f32[1024,256]{1,0:T(8,128)}, u32[]{:S(2)}) copy-start(f32[1024,256]{1,0:T(8,128)} %get-tuple-element.66) | copy-start | bytes 3145732
  183.0 14.9 %collective-permute-start.19 = (bf16[1024,256]{1,0:T(8,128)(2,1)}, bf16[1024,256]{1,0:T(8,128)(2,1)S(1)}, u32[]{:S(2)}, u32[]{:S(2)}) collective-permute-start(bf16[1024,256]{1,0:T(8,128)(2,1)} %get-tuple-element.67), channel_id=1, source_target_pairs={{0,1},{1,0},{2,3},{3,2},{4,5},{5,4},{6,7},{7,6},{8,9},{9,8},{10,11... | collective-permute-start | bytes 1572872 | tf_op jit(solution)/shard_map/ppermute | solution.py:22
  192.1 17.2 %copy-start.13 = (f32[1024,256]{1,0:T(8,128)S(1)}, f32[1024,256]{1,0:T(8,128)}, u32[]{:S(2)}) copy-start(f32[1024,256]{1,0:T(8,128)} %get-tuple-element.68) | copy-start | bytes 3145732
  192.1 17.1 %collective-permute-start.20 = (bf16[1024,256]{1,0:T(8,128)(2,1)}, bf16[1024,256]{1,0:T(8,128)(2,1)S(1)}, u32[]{:S(2)}, u32[]{:S(2)}) collective-permute-start(bf16[1024,256]{1,0:T(8,128)(2,1)} %get-tuple-element.69), channel_id=1, source_target_pairs={{0,1},{1,0},{2,3},{3,2},{4,5},{5,4},{6,7},{7,6},{8,9},{9,8},{10,11... | collective-permute-start | bytes 1572872 | tf_op jit(solution)/shard_map/ppermute | solution.py:22
  (17 other events, 53.0 us)

commit v3 on v2

--- a/solution.py
+++ b/solution.py
@@ -154,7 +154,7 @@
     return lax.dot_general(block, amps, (((1,), (1,)), ((), ())), preferred_element_type=F32)
 
 
-def gamma_kernel(counts, width, step, side, add, *refs):
+def gamma_kernel(counts, width, step, side, store, add, *refs):
     core, mine, other = refs[0], refs[1].get(), refs[2].get()
     count = len(counts)
     blocks = []
@@ -162,27 +162,26 @@
     for parts in counts:
         blocks.append([ref.get() for ref in refs[position:position + parts]])
         position += parts
-    outs = refs[-2:]
-    sums = [ref.get() for ref in refs[position:position + 2]] if add else None
+    out = refs[-1]
+    before = refs[position].get() if add else None
     zero = core[0] == 0
     columns = slice(width, 2 * width) if side == 0 else slice(0, width)
-    for store in range(2):
-        chosen = zero if store == 0 else jnp.logical_not(zero)
-        amps = []
-        for index in range(count):
-            place = slice((2 * index + side) * width, (2 * index + side + 1) * width)
-            amps.append(jnp.where(chosen, mine[:, place], other[:, place]))
-        for start in range(0, outs[store].shape[0], step):
-            into = slice(start, start + step)
-            total = None
-            for index, parts in enumerate(blocks):
-                size = parts[0].shape[0]
-                rows = slice(start % size, start % size + step)
-                value = contract(parts[start // size][rows, columns], amps[index])
-                total = value if total is None else total + value
-            if add:
-                total = total + sums[store][into, :]
-            outs[store][into, :] = total.astype(outs[store].dtype)
+    chosen = zero if store == 0 else jnp.logical_not(zero)
+    amps = []
+    for index in range(count):
+        place = slice((2 * index + side) * width, (2 * index + side + 1) * width)
+        amps.append(jnp.where(chosen, mine[:, place], other[:, place]))
+    for start in range(0, out.shape[0], step):
+        into = slice(start, start + step)
+        total = None
+        for index, parts in enumerate(blocks):
+            size = parts[0].shape[0]
+            rows = slice(start % size, start % size + step)
+            value = contract(parts[start // size][rows, columns], amps[index])
+            total = value if total is None else total + value
+        if add:
+            total = total + before[into, :]
+        out[into, :] = total.astype(out.dtype)
 
 
 def local(own, partner_blocks, occ_energy, virt_energy):
@@ -229,38 +228,43 @@
     def spread(copies):
         return lax.all_to_all(copies, ("x", "yl"), 0, 0, tiled=True).reshape(width, -1)
 
-    def gamma(side, blocks, mine, other, sums):
-        kernel = functools.partial(gamma_kernel, [len(block) for block in blocks], width, step, side, sums is not None)
-        shape = (depth, width)
-        shapes = jax.ShapeDtypeStruct(shape, F32), jax.ShapeDtypeStruct(shape, F32 if sums is None else BF16)
+    def gamma(side, store, blocks, mine, other, before=None, dtype=F32):
+        counts = [len(block) for block in blocks]
+        kernel = functools.partial(gamma_kernel, counts, width, step, side, store, before is not None)
         flat = [part for block in blocks for part in block]
-        return call(kernel, shapes, core, mine, other, *flat, *(sums or ()), scalar=True)
+        extra = [] if before is None else [before]
+        return call(kernel, jax.ShapeDtypeStruct((depth, width), dtype), core, mine, other, *flat, *extra, scalar=True)
 
     def both(parts, way):
         return tuple(shift(part, "z", NZ, way) for part in parts)
 
     up1, down1 = both(base, 1), both(base, -1)
+    up1, down1 = after((up1, down1), base_peer)
     up2, down2 = both(up1, 1), both(down1, -1)
+    near, distant = (0, 1, -1), (2, -2, 3, -3, 4)
+    near_blocks = [base, down1, up1]
+    near_halves = halves(near_blocks)
+    (up2, down2), near_halves = lax.optimization_barrier(((up2, down2), near_halves))
     up3, down3 = both(up2, 1), both(down2, -1)
     far = shift(up3[0][:half], "z", NZ, 1), shift(down3[0][half:], "z", NZ, -1)
-    near, distant = (0, 1, -1), (2, -2, 3, -3, 4)
-    near_blocks, distant_blocks = [base, down1, up1], [down2, up2, down3, up3, far]
-    pieces_a = scatter([after(halves(near_blocks), up2, down2)])
+
+    distant_blocks = [down2, up2, down3, up3, far]
+    pieces_a = scatter([near_halves])
     amp_a = amplitudes(near, after(pieces_a, up3, down3), CHIPS)
     mine_a = spread(amp_a)
     other_a = swap(mine_a, "c")
     middle_halves = halves(after(distant_blocks[:2], pieces_a))
     last_halves = halves(distant_blocks[2:])
     pieces_b = scatter([after(middle_halves, far), after(last_halves, mine_a)])
-    sums = [gamma(side, near_blocks, mine_a, other_a, None) for side in range(2)]
+    sums = [[gamma(side, store, near_blocks, mine_a, other_a) for store in range(2)] for side in range(2)]
     amp_b = amplitudes(distant, after(pieces_b, sums), CHIPS)
     mine_b = spread(amp_b)
     other_b = swap(mine_b, "c")
-    outs = []
-    for side in range(2):
-        here, there = gamma(side, distant_blocks, mine_b, other_b, sums[side])
-        outs.append(here + swap(there, "yh").astype(F32))
-    gamma_own, gamma_partner = outs
+    there = [gamma(side, 1, distant_blocks, mine_b, other_b, sums[side][1], BF16) for side in range(2)]
+    arrived = [swap(part, "yh").astype(F32) for part in there]
+    mine_b, other_b = after((mine_b, other_b), there)
+    here = [gamma(side, 0, distant_blocks, mine_b, other_b, sums[side][0]) for side in range(2)]
+    gamma_own, gamma_partner = (here[side] + arrived[side] for side in range(2))
     return gamma_own, gamma_partner[None]
 
 

time: 211 us -> 211 us (level)
  waiting for transfers between devices: 79 us -> 59.3 us
  Pallas kernels: 51.4 us -> 67.7 us
  blocking collectives: 19.9 us -> 22.2 us
    pallas_call x12 -> x16, Pallas kernels: 51.4 us -> 67.7 us  [call(): pl.pallas_call(body, out_shape=out_shape, in_specs=specs, out_specs=out_s...]
    ppermute x8, waiting for transfers between devices: 42 us -> 27.5 us  [shift(): lax.ppermute(value, axis, [(i, (i + step) % size) for i in range(size)])]
    all_to_all x2, waiting for transfers between devices: 11.5 us -> 0.19 us  [scatter(): lax.all_to_all(summed.reshape(CHIPS, rows, -1), ('x', 'yl'), 0, 0, tiled=...]
    ppermute x13, waiting for transfers between devices: 25.5 us -> 31.6 us  [swap(): return lax.ppermute(value, axis, [(0, 1), (1, 0)])]
    ppermute x13, starting transfers between devices: 15.5 us -> 17.9 us  [swap(): return lax.ppermute(value, axis, [(0, 1), (1, 0)])]
    all_to_all x1, blocking collectives: 19.9 us -> 22.2 us  [spread(): lax.all_to_all(copies, ('x', 'yl'), 0, 0, tiled=True).reshape(width, -1)]
    unnamed x54 -> x56, local copies, waits for them, and re-layouts: 6.37 us -> 6.51 us
  transfers between devices with their start and end apart: 24 -> 24, of which waited for: 14 -> 14; matrix products, arithmetic and copies ran while one was open for 2% -> 2% of each run, Pallas kernels for 18% -> 27%
where the time goes in v3:
time: 211 us; the launch traced here: 210 us
  Pallas kernels  67.7 us (32%)
  waiting for transfers between devices  59.3 us (28%)
  starting transfers between devices  45.3 us (21%)
  blocking collectives  22.2 us (11%)
  local copies, waits for them, and re-layouts  9.7 us (5%)
  other arithmetic  4.09 us (2%)
  between operations  2.14 us (1%)
    pallas_call x16, Pallas kernels, call(): pl.pallas_call(body, out_shape=out_shape, in_specs=specs, out_specs=out_s...  67.7 us
    ppermute x13, waiting for transfers between devices, swap(): return lax.ppermute(value, axis, [(0, 1), (1, 0)])  31.6 us
    ppermute x8, waiting for transfers between devices, shift(): lax.ppermute(value, axis, [(i, (i + step) % size) for i in range(size)])  27.5 us
    all_to_all x1, blocking collectives, spread(): lax.all_to_all(copies, ('x', 'yl'), 0, 0, tiled=True).reshape(width, -1)  22.2 us
    ppermute x13, starting transfers between devices, swap(): return lax.ppermute(value, axis, [(0, 1), (1, 0)])  17.9 us
    ppermute x8, starting transfers between devices, shift(): lax.ppermute(value, axis, [(i, (i + step) % size) for i in range(size)])  13.6 us
    all_to_all x2, starting transfers between devices, scatter(): lax.all_to_all(summed.reshape(CHIPS, rows, -1), ('x', 'yl'), 0, 0, tiled=...  9.65 us
    unnamed x56, local copies, waits for them, and re-layouts  6.51 us
  transfers between devices with their start and end apart: 24, of which 14 were waited for; matrix products, arithmetic and copies ran while one was open for 2% of the time, Pallas kernels for 27%

profile of v3, /device:TPU:1, one launch (start us, length us, event | category | flops | bytes accessed | tf_op | source)
XLA Modules:
  0.0 210.4 jit_solution(3440465523014847011)
XLA Ops:
  1.9 3.8 %collective-permute-start = (bf16[1024,512]{1,0:T(8,128)(2,1)S(1)}, bf16[1024,512]{1,0:T(8,128)(2,1)S(1)}, u32[]{:S(2)}, u32[]{:S(2)}) collective-permute-start(bf16[1024,512]{1,0:T(8,128)(2,1)S(1)} %pad_maximum_fusion.refs_1_.refs_3_), channel_id=1, source_target_pairs={{0,1},{1,0},{2,3},{3,2},{4,5},{5,4},{6,7},{7,6},{8,9},{9,8},{10,11... | collective-permute-start | bytes 3145736 | tf_op jit(solution)/shard_map/ppermute | solution.py:22
  7.4 3.9 %collective-permute-start.2 = (bf16[1024,512]{1,0:T(8,128)(2,1)S(1)}, bf16[1024,512]{1,0:T(8,128)(2,1)}, u32[]{:S(2)}, u32[]{:S(2)}) collective-permute-start(bf16[1024,512]{1,0:T(8,128)(2,1)S(1)} %pad_maximum_fusion.refs_1_.refs_3_), channel_id=1, source_target_pairs={{0,14},{2,0},{4,2},{6,4},{8,6},{10,8},{12,10},{14,12},{1,15},{3,1}... | collective-permute-start | bytes 3145736 | tf_op jit(solution)/shard_map/ppermute | solution.py:18
  11.3 16.2 %collective-permute-done.refs_2_ = bf16[1024,512]{1,0:T(8,128)(2,1)S(1)} collective-permute-done((bf16[1024,512]{1,0:T(8,128)(2,1)S(1)}, bf16[1024,512]{1,0:T(8,128)(2,1)S(1)}, u32[]{:S(2)}, u32[]{:S(2)}) %collective-permute-start) | collective-permute-done | bytes 1048608 | tf_op jit(solution)/shard_map/ppermute | solution.py:22
  27.6 6.4 %collective-permute-done.1.refs_3_.refs_5_ = bf16[1024,512]{1,0:T(8,128)(2,1)} collective-permute-done((bf16[1024,512]{1,0:T(8,128)(2,1)S(1)}, bf16[1024,512]{1,0:T(8,128)(2,1)}, u32[]{:S(2)}, u32[]{:S(2)}) %collective-permute-start.1) | collective-permute-done | bytes 1048608 | tf_op jit(solution)/shard_map/ppermute | solution.py:18
  34.0 2.7 %collective-permute-start.4 = (bf16[1024,512]{1,0:T(8,128)(2,1)}, bf16[1024,512]{1,0:T(8,128)(2,1)S(1)}, u32[]{:S(2)}, u32[]{:S(2)}) collective-permute-start(bf16[1024,512]{1,0:T(8,128)(2,1)} %collective-permute-done.2.refs_2_.refs_4_), channel_id=1, source_target_pairs={{0,14},{2,0},{4,2},{6,4},{8,6},{10,8},{12,10},{14,12},{1,15},{3,1}... | collective-permute-start | bytes 3145736 | tf_op jit(solution)/shard_map/ppermute | solution.py:18
  36.7 3.6 %shard_map.59.refs_0_ = bf16[1024,1024]{1,0:T(8,128)(2,1)} custom-call(s32[1]{0:T(128)} %bitcast.refs_0_, bf16[1024,512]{1,0:T(8,128)(2,1)} %copy-done, bf16[1024,512]{1,0:T(8,128)(2,1)} %copy-done.14), custom_call_target="tpu_custom_call" | custom-call | tf_op jit(solution)/shard_map/pallas_call | solution.py:58
  40.3 5.3 %shard_map.60 = (f32[256,1536]{1,0:T(8,128)}, f32[256,512]{1,0:T(8,128)}, f32[256,512]{1,0:T(8,128)}, f32[256,512]{1,0:T(8,128)}) custom-call(bf16[1024,1024]{1,0:T(8,128)(2,1)} %shard_map.59.refs_0_, bf16[1024,512]{1,0:T(8,128)(2,1)} %copy-done, bf16[1024,512]{1,0:T(8,128)(2,1)} %collective-permute-done.2.refs_2_.refs_4_, ...), custom_call_target="tpu_custom_call" | custom-call | tf_op jit(solution)/shard_map/pallas_call | solution.py:58
  45.6 2.2 %collective-permute-start.5 = (f32[256,512]{1,0:T(8,128)}, f32[256,512]{1,0:T(8,128)S(1)}, u32[]{:S(2)}, u32[]{:S(2)}) collective-permute-start(f32[256,512]{1,0:T(8,128)} %get-tuple-element.37), channel_id=1, source_target_pairs={{0,16},{16,0},{1,17},{17,1},{2,18},{18,2},{3,19},{19,3},{4,20},{20... | collective-permute-start | bytes 1572872 | tf_op jit(solution)/shard_map/ppermute | solution.py:22
  51.1 7.5 %collective-permute-done.3.refs_2_.refs_4_ = bf16[1024,512]{1,0:T(8,128)(2,1)S(1)} collective-permute-done((bf16[1024,512]{1,0:T(8,128)(2,1)}, bf16[1024,512]{1,0:T(8,128)(2,1)S(1)}, u32[]{:S(2)}, u32[]{:S(2)}) %collective-permute-start.3) | collective-permute-done | bytes 1048608 | tf_op jit(solution)/shard_map/ppermute | solution.py:18
  62.2 2.8 %shard_map.61 = bf16[256,1536]{1,0:T(8,128)(2,1)} custom-call(f32[256,1536]{1,0:T(8,128)} %get-tuple-element.42.refs_0_, f32[256,512]{1,0:T(8,128)} %copy-done.18, f32[256,512]{1,0:T(8,128)} %copy-done.20, f32[256,512]{1,0:T(8,128)} %copy-done.22), custom_call_target="tpu_custom_call" | custom-call | tf_op jit(solution)/shard_map/pallas_call | solution.py:58
  65.1 4.2 %all-to-all-start = ((bf16[8,32,1536]{2,1,0:T(8,128)(2,1)}), bf16[8,32,1536]{2,1,0:T(8,128)(2,1)}, u32[]{:S(2)}, u32[]{:S(2)}) async-start(bf16[8,32,1536]{2,1,0:T(8,128)(2,1)} %bitcast.48), calls=%async_computation | async-start | bytes 1572864 | tf_op jit(solution)/shard_map/all_to_all | solution.py:220
  69.3 13.6 %collective-permute-done.10.refs_2_.refs_6_ = bf16[1024,512]{1,0:T(8,128)(2,1)S(1)} collective-permute-done((bf16[1024,512]{1,0:T(8,128)(2,1)S(1)}, bf16[1024,512]{1,0:T(8,128)(2,1)S(1)}, u32[]{:S(2)}, u32[]{:S(2)}) %collective-permute-start.10) | collective-permute-done | bytes 1048608 | tf_op jit(solution)/shard_map/ppermute | solution.py:18
  84.8 2.7 %collective-permute-start.13 = (bf16[512,512]{1,0:T(8,128)(2,1)}, bf16[512,512]{1,0:T(8,128)(2,1)S(1)}, u32[]{:S(2)}, u32[]{:S(2)}) collective-permute-start(bf16[512,512]{1,0:T(8,128)(2,1)} %slice.17), channel_id=1, source_target_pairs={{0,14},{2,0},{4,2},{6,4},{8,6},{10,8},{12,10},{14,12},{1,15},{3,1}... | collective-permute-start | bytes 1572872 | tf_op jit(solution)/shard_map/ppermute | solution.py:18
  90.6 2.2 %shard_map.64 = bf16[8,32,1536]{2,1,0:T(8,128)(2,1)} custom-call(bf16[8,32,1536]{2,1,0:T(8,128)(2,1)} %all-to-all-done.refs_0_, f32[32,1]{1,0:T(8,128)} %copy.6.refs_1_, f32[1,768]{1,0:T(1,128)} %pad_maximum_fusion.1.refs_2_), custom_call_target="tpu_custom_call" | custom-call | tf_op jit(solution)/shard_map/pallas_call | solution.py:58
  92.9 4.1 %all-to-all-start.1 = ((bf16[8,32,1536]{2,1,0:T(8,128)(2,1)}), bf16[8,32,1536]{2,1,0:T(8,128)(2,1)S(1)}, u32[]{:S(2)}, u32[]{:S(2)}) async-start(bf16[8,32,1536]{2,1,0:T(8,128)(2,1)} %shard_map.64), calls=%async_computation.1 | async-start | bytes 1572864 | tf_op jit(solution)/shard_map/all_to_all | solution.py:229
  97.0 4.4 %shard_map.62 = (f32[256,1024]{1,0:T(8,128)}, f32[256,512]{1,0:T(8,128)}, f32[256,512]{1,0:T(8,128)}) custom-call(bf16[1024,1024]{1,0:T(8,128)(2,1)} %shard_map.59.refs_0_, bf16[1024,512]{1,0:T(8,128)(2,1)} %copy-done.5, bf16[1024,512]{1,0:T(8,128)(2,1)} %copy-done.4), custom_call_target="tpu_custom_call" | custom-call | tf_op jit(solution)/shard_map/pallas_call | solution.py:58
  101.5 4.3 %collective-permute-start.8 = (f32[256,512]{1,0:T(8,128)}, f32[256,512]{1,0:T(8,128)S(1)}, u32[]{:S(2)}, u32[]{:S(2)}) collective-permute-start(f32[256,512]{1,0:T(8,128)} %get-tuple-element.49), channel_id=1, source_target_pairs={{0,16},{16,0},{1,17},{17,1},{2,18},{18,2},{3,19},{19,3},{4,20},{20... | collective-permute-start | bytes 1572872 | tf_op jit(solution)/shard_map/ppermute | solution.py:22
  107.5 5.3 %shard_map.63 = (f32[256,1536]{1,0:T(8,128)}, f32[256,512]{1,0:T(8,128)}, f32[256,512]{1,0:T(8,128)}, f32[256,512]{1,0:T(8,128)}) custom-call(bf16[1024,1024]{1,0:T(8,128)(2,1)} %shard_map.59.refs_0_, bf16[1024,512]{1,0:T(8,128)(2,1)} %copy-done.3, bf16[1024,512]{1,0:T(8,128)(2,1)} %copy-done.2, bf16[512,512]{1,0:T(8,128)(2,1)} %copy-done.8, ...), custom_call_target="tpu_custom_call" | custom-call | tf_op jit(solution)/shard_map/pallas_call | solution.py:58
  117.4 3.6 %shard_map.65 = bf16[256,2560]{1,0:T(8,128)(2,1)} custom-call(f32[256,1024]{1,0:T(8,128)} %get-tuple-element.51.refs_0_, f32[256,512]{1,0:T(8,128)} %copy-done.15, f32[256,512]{1,0:T(8,128)} %copy-done.16, f32[256,1536]{1,0:T(8,128)} %get-tuple-element.59.refs_3_, f32[256,512]{1,0:T(8,128)} %copy-done.17, f32[256,512]{1,0:T(8,128)} %copy-done.19, ...), custom_call_target="tpu_custom_call" | custom-call | tf_op jit(solution)/shard_map/pallas_call | solution.py:58
  121.0 5.4 %all-to-all-start.2 = ((bf16[8,32,2560]{2,1,0:T(8,128)(2,1)}), bf16[8,32,2560]{2,1,0:T(8,128)(2,1)S(1)}, u32[]{:S(2)}, u32[]{:S(2)}) async-start(bf16[8,32,2560]{2,1,0:T(8,128)(2,1)} %bitcast.47), calls=%async_computation.2 | async-start | bytes 2621440 | tf_op jit(solution)/shard_map/all_to_all | solution.py:220
  130.0 4.0 %shard_map.66.refs_9_ = f32[1024,256]{1,0:T(8,128)} custom-call(s32[1]{0:T(128)} %bitcast.refs_0_, bf16[256,1536]{1,0:T(8,128)(2,1)} %bitcast.43, bf16[256,1536]{1,0:T(8,128)(2,1)} %copy-done.10, bf16[1024,512]{1,0:T(8,128)(2,1)} %copy-done, bf16[1024,512]{1,0:T(8,128)(2,1)} %collective-permute-done.2.refs_2_.refs_4_, ...), custom_call_target="tpu_custom_call" | custom-call | tf_op jit(solution)/shard_map/pallas_call | solution.py:58
  134.0 4.0 %shard_map.67.refs_9_ = f32[1024,256]{1,0:T(8,128)} custom-call(s32[1]{0:T(128)} %bitcast.refs_0_, bf16[256,1536]{1,0:T(8,128)(2,1)} %bitcast.44, bf16[256,1536]{1,0:T(8,128)(2,1)} %copy-done.10, bf16[1024,512]{1,0:T(8,128)(2,1)} %copy-done, bf16[1024,512]{1,0:T(8,128)(2,1)} %collective-permute-done.2.refs_2_.refs_4_, ...), custom_call_target="tpu_custom_call" | custom-call | tf_op jit(solution)/shard_map/pallas_call | solution.py:58
  138.0 4.0 %shard_map.68.refs_9_ = f32[1024,256]{1,0:T(8,128)} custom-call(s32[1]{0:T(128)} %bitcast.refs_0_, bf16[256,1536]{1,0:T(8,128)(2,1)} %bitcast.45, bf16[256,1536]{1,0:T(8,128)(2,1)} %copy-done.10, bf16[1024,512]{1,0:T(8,128)(2,1)} %copy-done, bf16[1024,512]{1,0:T(8,128)(2,1)} %collective-permute-done.2.refs_2_.refs_4_, ...), custom_call_target="tpu_custom_call" | custom-call | tf_op jit(solution)/shard_map/pallas_call | solution.py:58
  141.9 4.0 %shard_map.69.refs_9_ = f32[1024,256]{1,0:T(8,128)} custom-call(s32[1]{0:T(128)} %bitcast.refs_0_, bf16[256,1536]{1,0:T(8,128)(2,1)} %bitcast.46, bf16[256,1536]{1,0:T(8,128)(2,1)} %copy-done.10, bf16[1024,512]{1,0:T(8,128)(2,1)} %copy-done, bf16[1024,512]{1,0:T(8,128)(2,1)} %collective-permute-done.2.refs_2_.refs_4_, ...), custom_call_target="tpu_custom_call" | custom-call | tf_op jit(solution)/shard_map/pallas_call | solution.py:58
  147.2 2.6 %shard_map.70 = bf16[8,32,2560]{2,1,0:T(8,128)(2,1)} custom-call(bf16[8,32,2560]{2,1,0:T(8,128)(2,1)} %copy-done.11, f32[32,1]{1,0:T(8,128)} %copy.6.refs_1_, f32[1,1280]{1,0:T(1,128)} %copy-done.24), custom_call_target="tpu_custom_call" | custom-call | tf_op jit(solution)/shard_map/pallas_call | solution.py:58
  149.8 22.2 %all_to_all.20 = bf16[8,32,2560]{2,1,0:T(8,128)(2,1)S(1)} all-to-all(bf16[8,32,2560]{2,1,0:T(8,128)(2,1)} %shard_map.70), channel_id=1, replica_groups=mesh['x'=4,'yl'=2,'c'=2,'z'=8,'yh'=2] {'x','yl'}, dimensions={0} | all-to-all | bytes 2621440 | tf_op jit(solution)/shard_map/all_to_all | solution.py:229
  174.1 2.7 %collective-permute-done.18.refs_2_ = bf16[256,2560]{1,0:T(8,128)(2,1)S(1)} collective-permute-done((bf16[256,2560]{1,0:T(8,128)(2,1)S(1)}, bf16[256,2560]{1,0:T(8,128)(2,1)S(1)}, u32[]{:S(2)}, u32[]{:S(2)}) %collective-permute-start.18) | collective-permute-done | bytes 1310752 | tf_op jit(solution)/shard_map/ppermute | solution.py:22
  177.8 5.3 %shard_map.71 = bf16[1024,256]{1,0:T(8,128)(2,1)} custom-call(s32[1]{0:T(128)} %bitcast.refs_0_, bf16[256,2560]{1,0:T(8,128)(2,1)} %bitcast.38, bf16[256,2560]{1,0:T(8,128)(2,1)} %copy-done.6, bf16[1024,512]{1,0:T(8,128)(2,1)} %copy-done.5, bf16[1024,512]{1,0:T(8,128)(2,1)} %copy-done.4, bf16[1024,512]{1,0:T(8,128)(2,1)} %copy-done.3, ...), custom_call_target="tpu_custom_call" | custom-call | tf_op jit(solution)/shard_map/pallas_call | solution.py:58
  185.2 5.4 %shard_map.72 = bf16[1024,256]{1,0:T(8,128)(2,1)} custom-call(s32[1]{0:T(128)} %bitcast.refs_0_, bf16[256,2560]{1,0:T(8,128)(2,1)} %bitcast.39, bf16[256,2560]{1,0:T(8,128)(2,1)} %copy-done.6, bf16[1024,512]{1,0:T(8,128)(2,1)} %copy-done.5, bf16[1024,512]{1,0:T(8,128)(2,1)} %copy-done.4, bf16[1024,512]{1,0:T(8,128)(2,1)} %copy-done.3, ...), custom_call_target="tpu_custom_call" | custom-call | tf_op jit(solution)/shard_map/pallas_call | solution.py:58
  191.7 5.5 %shard_map.73 = f32[1024,256]{1,0:T(8,128)} custom-call(s32[1]{0:T(128)} %bitcast.refs_0_, bf16[256,2560]{1,0:T(8,128)(2,1)} %bitcast.40, bf16[256,2560]{1,0:T(8,128)(2,1)} %copy-done.6, bf16[1024,512]{1,0:T(8,128)(2,1)} %copy-done.5, bf16[1024,512]{1,0:T(8,128)(2,1)} %copy-done.4, bf16[1024,512]{1,0:T(8,128)(2,1)} %copy-done.3, ...), custom_call_target="tpu_custom_call" | custom-call | tf_op jit(solution)/shard_map/pallas_call | solution.py:58
  197.2 5.7 %shard_map.74 = f32[1024,256]{1,0:T(8,128)} custom-call(s32[1]{0:T(128)} %bitcast.refs_0_, bf16[256,2560]{1,0:T(8,128)(2,1)} %bitcast.41, bf16[256,2560]{1,0:T(8,128)(2,1)} %copy-done.6, bf16[1024,512]{1,0:T(8,128)(2,1)} %copy-done.5, bf16[1024,512]{1,0:T(8,128)(2,1)} %copy-done.4, bf16[1024,512]{1,0:T(8,128)(2,1)} %copy-done.3, ...), custom_call_target="tpu_custom_call" | custom-call | tf_op jit(solution)/shard_map/pallas_call | solution.py:58
  204.0 5.4 %collective-permute-done.20 = bf16[1024,256]{1,0:T(8,128)(2,1)S(1)} collective-permute-done((bf16[1024,256]{1,0:T(8,128)(2,1)}, bf16[1024,256]{1,0:T(8,128)(2,1)S(1)}, u32[]{:S(2)}, u32[]{:S(2)}) %collective-permute-start.20) | collective-permute-done | bytes 524320 | tf_op jit(solution)/shard_map/ppermute | solution.py:22
  (101 shorter events, 33.2 us)
Async XLA Ops:
  1.9 34.8 %copy-start = (bf16[1024,512]{1,0:T(8,128)(2,1)}, bf16[1024,512]{1,0:T(8,128)(2,1)S(1)}, u32[]{:S(2)}) copy-start(bf16[1024,512]{1,0:T(8,128)(2,1)S(1)} %pad_maximum_fusion.refs_1_.refs_3_) | copy-start | bytes 3145732
  1.9 25.7 %collective-permute-start = (bf16[1024,512]{1,0:T(8,128)(2,1)S(1)}, bf16[1024,512]{1,0:T(8,128)(2,1)S(1)}, u32[]{:S(2)}, u32[]{:S(2)}) collective-permute-start(bf16[1024,512]{1,0:T(8,128)(2,1)S(1)} %pad_maximum_fusion.refs_1_.refs_3_), channel_id=1, source_target_pairs={{0,1},{1,0},{2,3},{3,2},{4,5},{5,4},{6,7},{7,6},{8,9},{9,8},{10,11... | collective-permute-start | bytes 3145736 | tf_op jit(solution)/shard_map/ppermute | solution.py:22
  5.8 28.2 %collective-permute-start.1 = (bf16[1024,512]{1,0:T(8,128)(2,1)S(1)}, bf16[1024,512]{1,0:T(8,128)(2,1)}, u32[]{:S(2)}, u32[]{:S(2)}) collective-permute-start(bf16[1024,512]{1,0:T(8,128)(2,1)S(1)} %pad_maximum_fusion.refs_1_.refs_3_), channel_id=1, source_target_pairs={{0,2},{2,4},{4,6},{6,8},{8,10},{10,12},{12,14},{14,0},{1,3},{3,5},... | collective-permute-start | bytes 3145736 | tf_op jit(solution)/shard_map/ppermute | solution.py:18
  7.4 26.6 %collective-permute-start.2 = (bf16[1024,512]{1,0:T(8,128)(2,1)S(1)}, bf16[1024,512]{1,0:T(8,128)(2,1)}, u32[]{:S(2)}, u32[]{:S(2)}) collective-permute-start(bf16[1024,512]{1,0:T(8,128)(2,1)S(1)} %pad_maximum_fusion.refs_1_.refs_3_), channel_id=1, source_target_pairs={{0,14},{2,0},{4,2},{6,4},{8,6},{10,8},{12,10},{14,12},{1,15},{3,1}... | collective-permute-start | bytes 3145736 | tf_op jit(solution)/shard_map/ppermute | solution.py:18
  34.0 24.5 %collective-permute-start.3 = (bf16[1024,512]{1,0:T(8,128)(2,1)}, bf16[1024,512]{1,0:T(8,128)(2,1)S(1)}, u32[]{:S(2)}, u32[]{:S(2)}) collective-permute-start(bf16[1024,512]{1,0:T(8,128)(2,1)} %collective-permute-done.1.refs_3_.refs_5_), channel_id=1, source_target_pairs={{0,2},{2,4},{4,6},{6,8},{8,10},{10,12},{12,14},{14,0},{1,3},{3,5},... | collective-permute-start | bytes 3145736 | tf_op jit(solution)/shard_map/ppermute | solution.py:18
  34.0 24.5 %collective-permute-start.4 = (bf16[1024,512]{1,0:T(8,128)(2,1)}, bf16[1024,512]{1,0:T(8,128)(2,1)S(1)}, u32[]{:S(2)}, u32[]{:S(2)}) collective-permute-start(bf16[1024,512]{1,0:T(8,128)(2,1)} %collective-permute-done.2.refs_2_.refs_4_), channel_id=1, source_target_pairs={{0,14},{2,0},{4,2},{6,4},{8,6},{10,8},{12,10},{14,12},{1,15},{3,1}... | collective-permute-start | bytes 3145736 | tf_op jit(solution)/shard_map/ppermute | solution.py:18
  45.6 3.9 %collective-permute-start.5 = (f32[256,512]{1,0:T(8,128)}, f32[256,512]{1,0:T(8,128)S(1)}, u32[]{:S(2)}, u32[]{:S(2)}) collective-permute-start(f32[256,512]{1,0:T(8,128)} %get-tuple-element.37), channel_id=1, source_target_pairs={{0,16},{16,0},{1,17},{17,1},{2,18},{18,2},{3,19},{19,3},{4,20},{20... | collective-permute-start | bytes 1572872 | tf_op jit(solution)/shard_map/ppermute | solution.py:22
  47.8 2.5 %collective-permute-start.6 = (f32[256,512]{1,0:T(8,128)}, f32[256,512]{1,0:T(8,128)S(1)}, u32[]{:S(2)}, u32[]{:S(2)}) collective-permute-start(f32[256,512]{1,0:T(8,128)} %get-tuple-element.38), channel_id=1, source_target_pairs={{0,16},{16,0},{1,17},{17,1},{2,18},{18,2},{3,19},{19,3},{4,20},{20... | collective-permute-start | bytes 1572872 | tf_op jit(solution)/shard_map/ppermute | solution.py:22
  47.9 3.1 %collective-permute-start.7 = (f32[256,512]{1,0:T(8,128)}, f32[256,512]{1,0:T(8,128)S(1)}, u32[]{:S(2)}, u32[]{:S(2)}) collective-permute-start(f32[256,512]{1,0:T(8,128)} %get-tuple-element.39), channel_id=1, source_target_pairs={{0,16},{16,0},{1,17},{17,1},{2,18},{18,2},{3,19},{19,3},{4,20},{20... | collective-permute-start | bytes 1572872 | tf_op jit(solution)/shard_map/ppermute | solution.py:22
  49.6 12.6 %copy-start.18 = (f32[256,512]{1,0:T(8,128)}, f32[256,512]{1,0:T(8,128)S(1)}, u32[]{:S(2)}) copy-start(f32[256,512]{1,0:T(8,128)S(1)} %collective-permute-done.5.refs_1_) | copy-start | bytes 1572868
  50.3 11.9 %copy-start.20 = (f32[256,512]{1,0:T(8,128)}, f32[256,512]{1,0:T(8,128)S(1)}, u32[]{:S(2)}) copy-start(f32[256,512]{1,0:T(8,128)S(1)} %collective-permute-done.6.refs_2_) | copy-start | bytes 1572868
  51.1 11.1 %copy-start.22 = (f32[256,512]{1,0:T(8,128)}, f32[256,512]{1,0:T(8,128)S(1)}, u32[]{:S(2)}) copy-start(f32[256,512]{1,0:T(8,128)S(1)} %collective-permute-done.7.refs_3_) | copy-start | bytes 1572868
  59.5 23.4 %collective-permute-start.10 = (bf16[1024,512]{1,0:T(8,128)(2,1)S(1)}, bf16[1024,512]{1,0:T(8,128)(2,1)S(1)}, u32[]{:S(2)}, u32[]{:S(2)}) collective-permute-start(bf16[1024,512]{1,0:T(8,128)(2,1)S(1)} %collective-permute-done.3.refs_2_.refs_4_), channel_id=1, source_target_pairs={{0,2},{2,4},{4,6},{6,8},{8,10},{10,12},{12,14},{14,0},{1,3},{3,5},... | collective-permute-start | bytes 3145736 | tf_op jit(solution)/shard_map/ppermute | solution.py:18
  60.5 23.4 %collective-permute-start.12 = (bf16[1024,512]{1,0:T(8,128)(2,1)}, bf16[1024,512]{1,0:T(8,128)(2,1)S(1)}, u32[]{:S(2)}, u32[]{:S(2)}) collective-permute-start(bf16[1024,512]{1,0:T(8,128)(2,1)} %copy-done.5), channel_id=1, source_target_pairs={{0,14},{2,0},{4,2},{6,4},{8,6},{10,8},{12,10},{14,12},{1,15},{3,1}... | collective-permute-start | bytes 3145736 | tf_op jit(solution)/shard_map/ppermute | solution.py:18
  65.0 22.4 %copy-start.25 = (f32[2]{0:T(128)S(1)}, f32[2]{0:T(128)}, u32[]{:S(2)}) copy-start(f32[2]{0:T(128)} %param.6) | copy-start | bytes 28
  65.1 23.0 %copy-start.23 = (f32[4096]{0:T(1024)S(1)}, f32[4096]{0:T(1024)}, u32[]{:S(2)}) copy-start(f32[4096]{0:T(1024)} %param.7) | copy-start | bytes 49156
  65.1 25.6 %all-to-all-start = ((bf16[8,32,1536]{2,1,0:T(8,128)(2,1)}), bf16[8,32,1536]{2,1,0:T(8,128)(2,1)}, u32[]{:S(2)}, u32[]{:S(2)}) async-start(bf16[8,32,1536]{2,1,0:T(8,128)(2,1)} %bitcast.48), calls=%async_computation | async-start | bytes 1572864 | tf_op jit(solution)/shard_map/all_to_all | solution.py:220
  83.8 22.0 %collective-permute-start.11 = (bf16[512,512]{1,0:T(8,128)(2,1)}, bf16[512,512]{1,0:T(8,128)(2,1)S(1)}, u32[]{:S(2)}, u32[]{:S(2)}) collective-permute-start(bf16[512,512]{1,0:T(8,128)(2,1)} %slice.16), channel_id=1, source_target_pairs={{0,2},{2,4},{4,6},{6,8},{8,10},{10,12},{12,14},{14,0},{1,3},{3,5},... | collective-permute-start | bytes 1572872 | tf_op jit(solution)/shard_map/ppermute | solution.py:18
  84.8 21.1 %collective-permute-start.13 = (bf16[512,512]{1,0:T(8,128)(2,1)}, bf16[512,512]{1,0:T(8,128)(2,1)S(1)}, u32[]{:S(2)}, u32[]{:S(2)}) collective-permute-start(bf16[512,512]{1,0:T(8,128)(2,1)} %slice.17), channel_id=1, source_target_pairs={{0,14},{2,0},{4,2},{6,4},{8,6},{10,8},{12,10},{14,12},{1,15},{3,1}... | collective-permute-start | bytes 1572872 | tf_op jit(solution)/shard_map/ppermute | solution.py:18
  92.9 21.0 %all-to-all-start.1 = ((bf16[8,32,1536]{2,1,0:T(8,128)(2,1)}), bf16[8,32,1536]{2,1,0:T(8,128)(2,1)S(1)}, u32[]{:S(2)}, u32[]{:S(2)}) async-start(bf16[8,32,1536]{2,1,0:T(8,128)(2,1)} %shard_map.64), calls=%async_computation.1 | async-start | bytes 1572864 | tf_op jit(solution)/shard_map/all_to_all | solution.py:229
  101.5 12.4 %collective-permute-start.8 = (f32[256,512]{1,0:T(8,128)}, f32[256,512]{1,0:T(8,128)S(1)}, u32[]{:S(2)}, u32[]{:S(2)}) collective-permute-start(f32[256,512]{1,0:T(8,128)} %get-tuple-element.49), channel_id=1, source_target_pairs={{0,16},{16,0},{1,17},{17,1},{2,18},{18,2},{3,19},{19,3},{4,20},{20... | collective-permute-start | bytes 1572872 | tf_op jit(solution)/shard_map/ppermute | solution.py:22
  105.8 8.1 %collective-permute-start.9 = (f32[256,512]{1,0:T(8,128)}, f32[256,512]{1,0:T(8,128)S(1)}, u32[]{:S(2)}, u32[]{:S(2)}) collective-permute-start(f32[256,512]{1,0:T(8,128)} %get-tuple-element.50), channel_id=1, source_target_pairs={{0,16},{16,0},{1,17},{17,1},{2,18},{18,2},{3,19},{19,3},{4,20},{20... | collective-permute-start | bytes 1572872 | tf_op jit(solution)/shard_map/ppermute | solution.py:22
  112.8 2.2 %collective-permute-start.14 = (f32[256,512]{1,0:T(8,128)}, f32[256,512]{1,0:T(8,128)S(1)}, u32[]{:S(2)}, u32[]{:S(2)}) collective-permute-start(f32[256,512]{1,0:T(8,128)} %get-tuple-element.55), channel_id=1, source_target_pairs={{0,16},{16,0},{1,17},{17,1},{2,18},{18,2},{3,19},{19,3},{4,20},{20... | collective-permute-start | bytes 1572872 | tf_op jit(solution)/shard_map/ppermute | solution.py:22
  113.3 2.5 %collective-permute-start.15 = (f32[256,512]{1,0:T(8,128)}, f32[256,512]{1,0:T(8,128)S(1)}, u32[]{:S(2)}, u32[]{:S(2)}) collective-permute-start(f32[256,512]{1,0:T(8,128)} %get-tuple-element.56), channel_id=1, source_target_pairs={{0,16},{16,0},{1,17},{17,1},{2,18},{18,2},{3,19},{19,3},{4,20},{20... | collective-permute-start | bytes 1572872 | tf_op jit(solution)/shard_map/ppermute | solution.py:22
  113.4 3.1 %collective-permute-start.16 = (f32[256,512]{1,0:T(8,128)}, f32[256,512]{1,0:T(8,128)S(1)}, u32[]{:S(2)}, u32[]{:S(2)}) collective-permute-start(f32[256,512]{1,0:T(8,128)} %get-tuple-element.57), channel_id=1, source_target_pairs={{0,16},{16,0},{1,17},{17,1},{2,18},{18,2},{3,19},{19,3},{4,20},{20... | collective-permute-start | bytes 1572872 | tf_op jit(solution)/shard_map/ppermute | solution.py:22
  113.9 12.6 %copy-start.7 = (bf16[8,32,1536]{2,1,0:T(8,128)(2,1)}, bf16[8,32,1536]{2,1,0:T(8,128)(2,1)S(1)}, u32[]{:S(2)}) copy-start(bf16[8,32,1536]{2,1,0:T(8,128)(2,1)S(1)} %all-to-all-done.1) | copy-start | bytes 2359300
  121.0 25.2 %all-to-all-start.2 = ((bf16[8,32,2560]{2,1,0:T(8,128)(2,1)}), bf16[8,32,2560]{2,1,0:T(8,128)(2,1)S(1)}, u32[]{:S(2)}, u32[]{:S(2)}) async-start(bf16[8,32,2560]{2,1,0:T(8,128)(2,1)} %bitcast.47), calls=%async_computation.2 | async-start | bytes 2621440 | tf_op jit(solution)/shard_map/all_to_all | solution.py:220
  126.4 2.7 %collective-permute-start.17 = (bf16[256,1536]{1,0:T(8,128)(2,1)S(1)}, bf16[256,1536]{1,0:T(8,128)(2,1)S(1)}, u32[]{:S(2)}, u32[]{:S(2)}) collective-permute-start(bf16[256,1536]{1,0:T(8,128)(2,1)S(1)} %bitcast.42), channel_id=1, source_target_pairs={{0,16},{16,0},{1,17},{17,1},{2,18},{18,2},{3,19},{19,3},{4,20},{20... | collective-permute-start | bytes 2359304 | tf_op jit(solution)/shard_map/ppermute | solution.py:22
  127.3 10.7 %copy-start.24 = (f32[1,1280]{1,0:T(1,128)}, f32[1,1280]{1,0:T(1,128)S(1)}, u32[]{:S(2)}) copy-start(f32[1,1280]{1,0:T(1,128)S(1)} %constant_dynamic-update-slice_fusion.refs_2_) | copy-start | bytes 15364
  172.0 4.7 %collective-permute-start.18 = (bf16[256,2560]{1,0:T(8,128)(2,1)S(1)}, bf16[256,2560]{1,0:T(8,128)(2,1)S(1)}, u32[]{:S(2)}, u32[]{:S(2)}) collective-permute-start(bf16[256,2560]{1,0:T(8,128)(2,1)S(1)} %bitcast.37), channel_id=1, source_target_pairs={{0,16},{16,0},{1,17},{17,1},{2,18},{18,2},{3,19},{19,3},{4,20},{20... | collective-permute-start | bytes 3932168 | tf_op jit(solution)/shard_map/ppermute | solution.py:22
  183.2 19.7 %collective-permute-start.19 = (bf16[1024,256]{1,0:T(8,128)(2,1)}, bf16[1024,256]{1,0:T(8,128)(2,1)S(1)}, u32[]{:S(2)}, u32[]{:S(2)}) collective-permute-start(bf16[1024,256]{1,0:T(8,128)(2,1)} %shard_map.71), channel_id=1, source_target_pairs={{0,1},{1,0},{2,3},{3,2},{4,5},{5,4},{6,7},{7,6},{8,9},{9,8},{10,11... | collective-permute-start | bytes 1572872 | tf_op jit(solution)/shard_map/ppermute | solution.py:22
  190.6 18.8 %collective-permute-start.20 = (bf16[1024,256]{1,0:T(8,128)(2,1)}, bf16[1024,256]{1,0:T(8,128)(2,1)S(1)}, u32[]{:S(2)}, u32[]{:S(2)}) collective-permute-start(bf16[1024,256]{1,0:T(8,128)(2,1)} %shard_map.72), channel_id=1, source_target_pairs={{0,1},{1,0},{2,3},{3,2},{4,5},{5,4},{6,7},{7,6},{8,9},{9,8},{10,11... | collective-permute-start | bytes 1572872 | tf_op jit(solution)/shard_map/ppermute | solution.py:22
  (18 other events, 63.0 us)

commit v4 on v3

--- a/solution.py
+++ b/solution.py
@@ -35,6 +35,8 @@
 
 def call(kernel, out_shape, *args, scalar=False, cost=0):
     lead = 1 if scalar else 0
+    windows = [arg[1] if isinstance(arg, tuple) else None for arg in args[lead:]]
+    args = [arg[0] if isinstance(arg, tuple) else arg for arg in args]
     moved = args[lead:]
     count = len(moved)
     outs = len(jax.tree.leaves(out_shape))
@@ -46,13 +48,20 @@
         sems = refs[-1]
         lazy = []
         for index in range(count):
-            copy = pltpu.make_async_copy(sources[index], scratch[index], sems.at[index])
+            source = sources[index]
+            if windows[index] is not None:
+                source = source.at[:, windows[index]]
+            copy = pltpu.make_async_copy(source, scratch[index], sems.at[index])
             copy.start()
             lazy.append(Lazy(scratch[index], copy))
         kernel(*refs[:lead], *lazy, *targets)
         for item in lazy:
             item.get()
 
+    buffers = []
+    for arg, window in zip(moved, windows):
+        shape = arg.shape if window is None else (arg.shape[0], window.stop - window.start)
+        buffers.append(pltpu.VMEM(shape, arg.dtype))
     specs = [pl.BlockSpec(memory_space=pltpu.SMEM)] * lead + [pl.BlockSpec(memory_space=pltpu.HBM)] * count
     out_specs = jax.tree.map(lambda _: pl.BlockSpec(memory_space=pltpu.VMEM), out_shape)
     return pl.pallas_call(
@@ -60,7 +69,7 @@
         out_shape=out_shape,
         in_specs=specs,
         out_specs=out_specs,
-        scratch_shapes=[pltpu.VMEM(arg.shape, arg.dtype) for arg in moved] + [pltpu.SemaphoreType.DMA((count,))],
+        scratch_shapes=buffers + [pltpu.SemaphoreType.DMA((count,))],
         cost_estimate=pl.CostEstimate(flops=cost, bytes_accessed=0, transcendentals=0),
         compiler_params=pltpu.CompilerParams(vmem_limit_bytes=56 * 1024 * 1024),
     )(*args)
@@ -165,7 +174,6 @@
     out = refs[-1]
     before = refs[position].get() if add else None
     zero = core[0] == 0
-    columns = slice(width, 2 * width) if side == 0 else slice(0, width)
     chosen = zero if store == 0 else jnp.logical_not(zero)
     amps = []
     for index in range(count):
@@ -177,7 +185,7 @@
         for index, parts in enumerate(blocks):
             size = parts[0].shape[0]
             rows = slice(start % size, start % size + step)
-            value = contract(parts[start // size][rows, columns], amps[index])
+            value = contract(parts[start // size][rows, :], amps[index])
             total = value if total is None else total + value
         if add:
             total = total + before[into, :]
@@ -231,7 +239,8 @@
     def gamma(side, store, blocks, mine, other, before=None, dtype=F32):
         counts = [len(block) for block in blocks]
         kernel = functools.partial(gamma_kernel, counts, width, step, side, store, before is not None)
-        flat = [part for block in blocks for part in block]
+        columns = slice(width, 2 * width) if side == 0 else slice(0, width)
+        flat = [(part, columns) for block in blocks for part in block]
         extra = [] if before is None else [before]
         return call(kernel, jax.ShapeDtypeStruct((depth, width), dtype), core, mine, other, *flat, *extra, scalar=True)
 
@@ -246,16 +255,19 @@
     near_halves = halves(near_blocks)
     (up2, down2), near_halves = lax.optimization_barrier(((up2, down2), near_halves))
     up3, down3 = both(up2, 1), both(down2, -1)
+    pieces_a = scatter([near_halves])
+    middle_halves = halves([down2, up2])
+    (up3, down3), middle_halves = lax.optimization_barrier(((up3, down3), middle_halves))
     far = shift(up3[0][:half], "z", NZ, 1), shift(down3[0][half:], "z", NZ, -1)
 
     distant_blocks = [down2, up2, down3, up3, far]
-    pieces_a = scatter([near_halves])
-    amp_a = amplitudes(near, after(pieces_a, up3, down3), CHIPS)
+    amp_a = amplitudes(near, pieces_a, CHIPS)
     mine_a = spread(amp_a)
     other_a = swap(mine_a, "c")
-    middle_halves = halves(after(distant_blocks[:2], pieces_a))
-    last_halves = halves(distant_blocks[2:])
-    pieces_b = scatter([after(middle_halves, far), after(last_halves, mine_a)])
+    third_halves = halves([down3, up3])
+    last, third_halves = lax.optimization_barrier((far, third_halves))
+    last_halves = halves([last])
+    pieces_b = scatter([middle_halves, third_halves, after(last_halves, mine_a)])
     sums = [[gamma(side, store, near_blocks, mine_a, other_a) for store in range(2)] for side in range(2)]
     amp_b = amplitudes(distant, after(pieces_b, sums), CHIPS)
     mine_b = spread(amp_b)

time: 211 us -> 210 us (level)
  starting transfers between devices: 45.3 us -> 49.5 us
  waiting for transfers between devices: 59.3 us -> 55.2 us
  Pallas kernels: 67.7 us -> 65.2 us
    ppermute x8, waiting for transfers between devices: 27.5 us -> 19.3 us  [shift(): lax.ppermute(value, axis, [(i, (i + step) % size) for i in range(size)])]
    all_to_all x1, waiting for transfers between devices: 0.01 us -> 5.89 us  [spread(): lax.all_to_all(copies, ('x', 'yl'), 0, 0, tiled=True).reshape(width, -1)]
    ppermute x13, starting transfers between devices: 17.9 us -> 23.8 us  [swap(): return lax.ppermute(value, axis, [(0, 1), (1, 0)])]
    pallas_call x16 -> x17, Pallas kernels: 67.7 us -> 65.2 us  [call(): pl.pallas_call(body, out_shape=out_shape, in_specs=specs, out_specs=out_s...]
    unnamed x56 -> x50, local copies, waits for them, and re-layouts: 6.51 us -> 5.98 us
  transfers between devices with their start and end apart: 24 -> 24, of which waited for: 14 -> 12; matrix products, arithmetic and copies ran while one was open for 2% -> 3% of each run, Pallas kernels for 27% -> 26%
where the time goes in v4:
time: 210 us; the launch traced here: 209 us
  Pallas kernels  65.2 us (31%)
  waiting for transfers between devices  55.2 us (26%)
  starting transfers between devices  49.5 us (24%)
  blocking collectives  22.3 us (11%)
  local copies, waits for them, and re-layouts  9.06 us (4%)
  other arithmetic  5.41 us (3%)
  between operations  2.32 us (1%)
    pallas_call x17, Pallas kernels, call(): pl.pallas_call(body, out_shape=out_shape, in_specs=specs, out_specs=out_s...  65.2 us
    ppermute x13, waiting for transfers between devices, swap(): return lax.ppermute(value, axis, [(0, 1), (1, 0)])  30 us
    ppermute x13, starting transfers between devices, swap(): return lax.ppermute(value, axis, [(0, 1), (1, 0)])  23.8 us
    all_to_all x1, blocking collectives, spread(): lax.all_to_all(copies, ('x', 'yl'), 0, 0, tiled=True).reshape(width, -1)  22.3 us
    ppermute x8, waiting for transfers between devices, shift(): lax.ppermute(value, axis, [(i, (i + step) % size) for i in range(size)])  19.3 us
    ppermute x8, starting transfers between devices, shift(): lax.ppermute(value, axis, [(i, (i + step) % size) for i in range(size)])  13.6 us
    all_to_all x2, starting transfers between devices, scatter(): lax.all_to_all(summed.reshape(CHIPS, rows, -1), ('x', 'yl'), 0, 0, tiled=...  7.98 us
    unnamed x50, local copies, waits for them, and re-layouts  5.98 us
  transfers between devices with their start and end apart: 24, of which 12 were waited for; matrix products, arithmetic and copies ran while one was open for 3% of the time, Pallas kernels for 26%

profile of v4, /device:TPU:1, one launch (start us, length us, event | category | flops | bytes accessed | tf_op | source)
XLA Modules:
  0.0 209.0 jit_solution(13839208259744683698)
XLA Ops:
  1.9 3.8 %collective-permute-start.2 = (bf16[1024,512]{1,0:T(8,128)(2,1)S(1)}, bf16[1024,512]{1,0:T(8,128)(2,1)S(1)}, u32[]{:S(2)}, u32[]{:S(2)}) collective-permute-start(bf16[1024,512]{1,0:T(8,128)(2,1)S(1)} %pad_maximum_fusion.refs_1_.refs_3_), channel_id=1, source_target_pairs={{0,1},{1,0},{2,3},{3,2},{4,5},{5,4},{6,7},{7,6},{8,9},{9,8},{10,11... | collective-permute-start | bytes 3145736 | tf_op jit(solution)/shard_map/ppermute | solution.py:22
  5.8 5.6 %collective-permute-start.1 = (bf16[1024,512]{1,0:T(8,128)(2,1)S(1)}, bf16[1024,512]{1,0:T(8,128)(2,1)}, u32[]{:S(2)}, u32[]{:S(2)}) collective-permute-start(bf16[1024,512]{1,0:T(8,128)(2,1)S(1)} %pad_maximum_fusion.refs_1_.refs_3_), channel_id=1, source_target_pairs={{0,14},{2,0},{4,2},{6,4},{8,6},{10,8},{12,10},{14,12},{1,15},{3,1}... | collective-permute-start | bytes 3145736 | tf_op jit(solution)/shard_map/ppermute | solution.py:18
  11.3 16.2 %collective-permute-done.2.refs_2_ = bf16[1024,512]{1,0:T(8,128)(2,1)S(1)} collective-permute-done((bf16[1024,512]{1,0:T(8,128)(2,1)S(1)}, bf16[1024,512]{1,0:T(8,128)(2,1)S(1)}, u32[]{:S(2)}, u32[]{:S(2)}) %collective-permute-start.2) | collective-permute-done | bytes 1048608 | tf_op jit(solution)/shard_map/ppermute | solution.py:22
  27.6 5.3 %collective-permute-done.1.refs_2_.refs_4_ = bf16[1024,512]{1,0:T(8,128)(2,1)} collective-permute-done((bf16[1024,512]{1,0:T(8,128)(2,1)S(1)}, bf16[1024,512]{1,0:T(8,128)(2,1)}, u32[]{:S(2)}, u32[]{:S(2)}) %collective-permute-start.1) | collective-permute-done | bytes 1048608 | tf_op jit(solution)/shard_map/ppermute | solution.py:18
  32.8 3.2 %collective-permute-done.refs_3_.refs_5_ = bf16[1024,512]{1,0:T(8,128)(2,1)} collective-permute-done((bf16[1024,512]{1,0:T(8,128)(2,1)S(1)}, bf16[1024,512]{1,0:T(8,128)(2,1)}, u32[]{:S(2)}, u32[]{:S(2)}) %collective-permute-start) | collective-permute-done | bytes 1048608 | tf_op jit(solution)/shard_map/ppermute | solution.py:18
  36.1 2.7 %collective-permute-start.4 = (bf16[1024,512]{1,0:T(8,128)(2,1)}, bf16[1024,512]{1,0:T(8,128)(2,1)S(1)}, u32[]{:S(2)}, u32[]{:S(2)}) collective-permute-start(bf16[1024,512]{1,0:T(8,128)(2,1)} %collective-permute-done.1.refs_2_.refs_4_), channel_id=1, source_target_pairs={{0,14},{2,0},{4,2},{6,4},{8,6},{10,8},{12,10},{14,12},{1,15},{3,1}... | collective-permute-start | bytes 3145736 | tf_op jit(solution)/shard_map/ppermute | solution.py:18
  38.7 3.6 %shard_map.59.refs_0_ = bf16[1024,1024]{1,0:T(8,128)(2,1)} custom-call(s32[1]{0:T(128)} %bitcast.refs_0_, bf16[1024,512]{1,0:T(8,128)(2,1)} %copy-done, bf16[1024,512]{1,0:T(8,128)(2,1)} %copy-done.13), custom_call_target="tpu_custom_call" | custom-call | tf_op jit(solution)/shard_map/pallas_call | solution.py:67
  42.4 5.3 %shard_map.60 = (f32[256,1536]{1,0:T(8,128)}, f32[256,512]{1,0:T(8,128)}, f32[256,512]{1,0:T(8,128)}, f32[256,512]{1,0:T(8,128)}) custom-call(bf16[1024,1024]{1,0:T(8,128)(2,1)} %shard_map.59.refs_0_, bf16[1024,512]{1,0:T(8,128)(2,1)} %copy-done, bf16[1024,512]{1,0:T(8,128)(2,1)} %collective-permute-done.1.refs_2_.refs_4_, ...), custom_call_target="tpu_custom_call" | custom-call | tf_op jit(solution)/shard_map/pallas_call | solution.py:67
  47.7 2.8 %collective-permute-start.5 = (f32[256,512]{1,0:T(8,128)}, f32[256,512]{1,0:T(8,128)S(1)}, u32[]{:S(2)}, u32[]{:S(2)}) collective-permute-start(f32[256,512]{1,0:T(8,128)} %get-tuple-element.40), channel_id=1, source_target_pairs={{0,16},{16,0},{1,17},{17,1},{2,18},{18,2},{3,19},{19,3},{4,20},{20... | collective-permute-start | bytes 1572872 | tf_op jit(solution)/shard_map/ppermute | solution.py:22
  53.7 6.3 %collective-permute-done.3.refs_2_.refs_4_ = bf16[1024,512]{1,0:T(8,128)(2,1)S(1)} collective-permute-done((bf16[1024,512]{1,0:T(8,128)(2,1)}, bf16[1024,512]{1,0:T(8,128)(2,1)S(1)}, u32[]{:S(2)}, u32[]{:S(2)}) %collective-permute-start.3) | collective-permute-done | bytes 1048608 | tf_op jit(solution)/shard_map/ppermute | solution.py:18
  63.7 4.4 %shard_map.61 = (f32[256,1024]{1,0:T(8,128)}, f32[256,512]{1,0:T(8,128)}, f32[256,512]{1,0:T(8,128)}) custom-call(bf16[1024,1024]{1,0:T(8,128)(2,1)} %shard_map.59.refs_0_, bf16[1024,512]{1,0:T(8,128)(2,1)} %copy-done.5, bf16[1024,512]{1,0:T(8,128)(2,1)} %copy-done.4), custom_call_target="tpu_custom_call" | custom-call | tf_op jit(solution)/shard_map/pallas_call | solution.py:67
  68.1 3.7 %collective-permute-start.10 = (f32[256,512]{1,0:T(8,128)}, f32[256,512]{1,0:T(8,128)}, u32[]{:S(2)}, u32[]{:S(2)}) collective-permute-start(f32[256,512]{1,0:T(8,128)} %get-tuple-element.46), channel_id=1, source_target_pairs={{0,16},{16,0},{1,17},{17,1},{2,18},{18,2},{3,19},{19,3},{4,20},{20... | collective-permute-start | bytes 1572872 | tf_op jit(solution)/shard_map/ppermute | solution.py:22
  71.9 2.8 %shard_map.64 = bf16[256,1536]{1,0:T(8,128)(2,1)} custom-call(f32[256,1536]{1,0:T(8,128)} %get-tuple-element.63.refs_0_, f32[256,512]{1,0:T(8,128)} %copy-done.16, f32[256,512]{1,0:T(8,128)} %copy-done.17, f32[256,512]{1,0:T(8,128)} %copy-done.18), custom_call_target="tpu_custom_call" | custom-call | tf_op jit(solution)/shard_map/pallas_call | solution.py:67
  74.8 4.4 %all-to-all-start = ((bf16[8,32,1536]{2,1,0:T(8,128)(2,1)}), bf16[8,32,1536]{2,1,0:T(8,128)(2,1)}, u32[]{:S(2)}, u32[]{:S(2)}) async-start(bf16[8,32,1536]{2,1,0:T(8,128)(2,1)} %bitcast.48), calls=%async_computation | async-start | bytes 1572864 | tf_op jit(solution)/shard_map/all_to_all | solution.py:228
  79.2 4.6 %collective-permute-done.8.refs_2_.refs_6_ = bf16[1024,512]{1,0:T(8,128)(2,1)S(1)} collective-permute-done((bf16[1024,512]{1,0:T(8,128)(2,1)S(1)}, bf16[1024,512]{1,0:T(8,128)(2,1)S(1)}, u32[]{:S(2)}, u32[]{:S(2)}) %collective-permute-start.8) | collective-permute-done | bytes 1048608 | tf_op jit(solution)/shard_map/ppermute | solution.py:18
  85.5 4.4 %shard_map.62 = (f32[256,1024]{1,0:T(8,128)}, f32[256,512]{1,0:T(8,128)}, f32[256,512]{1,0:T(8,128)}) custom-call(bf16[1024,1024]{1,0:T(8,128)(2,1)} %shard_map.59.refs_0_, bf16[1024,512]{1,0:T(8,128)(2,1)} %copy-done.3, bf16[1024,512]{1,0:T(8,128)(2,1)} %copy-done.2), custom_call_target="tpu_custom_call" | custom-call | tf_op jit(solution)/shard_map/pallas_call | solution.py:67
  92.6 4.6 %collective-permute-start.14 = (f32[256,512]{1,0:T(8,128)}, f32[256,512]{1,0:T(8,128)S(1)}, u32[]{:S(2)}, u32[]{:S(2)}) collective-permute-start(f32[256,512]{1,0:T(8,128)} %get-tuple-element.54), channel_id=1, source_target_pairs={{0,16},{16,0},{1,17},{17,1},{2,18},{18,2},{3,19},{19,3},{4,20},{20... | collective-permute-start | bytes 1572872 | tf_op jit(solution)/shard_map/ppermute | solution.py:22
  102.7 4.1 %all-to-all-start.1 = ((bf16[8,32,1536]{2,1,0:T(8,128)(2,1)}), bf16[8,32,1536]{2,1,0:T(8,128)(2,1)S(1)}, u32[]{:S(2)}, u32[]{:S(2)}) async-start(bf16[8,32,1536]{2,1,0:T(8,128)(2,1)} %shard_map.65), calls=%async_computation.1 | async-start | bytes 1572864 | tf_op jit(solution)/shard_map/all_to_all | solution.py:237
  107.9 3.5 %shard_map.63 = (f32[256,512]{1,0:T(8,128)}, f32[256,512]{1,0:T(8,128)}) custom-call(bf16[1024,1024]{1,0:T(8,128)(2,1)} %shard_map.59.refs_0_, bf16[512,512]{1,0:T(8,128)(2,1)} %copy-done.9, bf16[512,512]{1,0:T(8,128)(2,1)} %copy-done.8), custom_call_target="tpu_custom_call" | custom-call | tf_op jit(solution)/shard_map/pallas_call | solution.py:67
  112.7 5.9 %all-to-all-done.1 = bf16[8,32,1536]{2,1,0:T(8,128)(2,1)S(1)} async-done(((bf16[8,32,1536]{2,1,0:T(8,128)(2,1)}), bf16[8,32,1536]{2,1,0:T(8,128)(2,1)S(1)}, u32[]{:S(2)}, u32[]{:S(2)}) %all-to-all-start.1) | async-done | bytes 786464 | tf_op jit(solution)/shard_map/all_to_all | solution.py:237
  119.5 3.7 %shard_map.66 = bf16[256,2560]{1,0:T(8,128)(2,1)} custom-call(f32[256,1024]{1,0:T(8,128)} %get-tuple-element.48.refs_0_, f32[256,512]{1,0:T(8,128)} %collective-permute-done.10.refs_1_, f32[256,512]{1,0:T(8,128)} %collective-permute-done.11.refs_2_, f32[256,1024]{1,0:T(8,128)} %get-tuple-element.56.refs_3_, f32[256,512]{1,0:T(8,128)} %copy-done.14, ...), custom_call_target="tpu_custom_call" | custom-call | tf_op jit(solution)/shard_map/pallas_call | solution.py:67
  123.1 3.6 %all-to-all-start.2 = ((bf16[8,32,2560]{2,1,0:T(8,128)(2,1)}), bf16[8,32,2560]{2,1,0:T(8,128)(2,1)S(1)}, u32[]{:S(2)}, u32[]{:S(2)}) async-start(bf16[8,32,2560]{2,1,0:T(8,128)(2,1)} %bitcast.47), calls=%async_computation.2 | async-start | bytes 2621440 | tf_op jit(solution)/shard_map/all_to_all | solution.py:228
  131.3 3.5 %shard_map.70.refs_9_ = f32[1024,256]{1,0:T(8,128)} custom-call(s32[1]{0:T(128)} %bitcast.refs_0_, bf16[256,1536]{1,0:T(8,128)(2,1)} %bitcast.43, bf16[256,1536]{1,0:T(8,128)(2,1)} %copy-done.10, bf16[1024,512]{1,0:T(8,128)(2,1)} %copy-done, bf16[1024,512]{1,0:T(8,128)(2,1)} %collective-permute-done.1.refs_2_.refs_4_, ...), custom_call_target="tpu_custom_call" | custom-call | tf_op jit(solution)/shard_map/pallas_call | solution.py:67
  134.7 3.5 %shard_map.69.refs_9_ = f32[1024,256]{1,0:T(8,128)} custom-call(s32[1]{0:T(128)} %bitcast.refs_0_, bf16[256,1536]{1,0:T(8,128)(2,1)} %bitcast.44, bf16[256,1536]{1,0:T(8,128)(2,1)} %copy-done.10, bf16[1024,512]{1,0:T(8,128)(2,1)} %copy-done, bf16[1024,512]{1,0:T(8,128)(2,1)} %collective-permute-done.1.refs_2_.refs_4_, ...), custom_call_target="tpu_custom_call" | custom-call | tf_op jit(solution)/shard_map/pallas_call | solution.py:67
  138.2 3.5 %shard_map.68.refs_9_ = f32[1024,256]{1,0:T(8,128)} custom-call(s32[1]{0:T(128)} %bitcast.refs_0_, bf16[256,1536]{1,0:T(8,128)(2,1)} %bitcast.45, bf16[256,1536]{1,0:T(8,128)(2,1)} %copy-done.10, bf16[1024,512]{1,0:T(8,128)(2,1)} %copy-done, bf16[1024,512]{1,0:T(8,128)(2,1)} %collective-permute-done.1.refs_2_.refs_4_, ...), custom_call_target="tpu_custom_call" | custom-call | tf_op jit(solution)/shard_map/pallas_call | solution.py:67
  141.7 3.5 %shard_map.67.refs_9_ = f32[1024,256]{1,0:T(8,128)} custom-call(s32[1]{0:T(128)} %bitcast.refs_0_, bf16[256,1536]{1,0:T(8,128)(2,1)} %bitcast.46, bf16[256,1536]{1,0:T(8,128)(2,1)} %copy-done.10, bf16[1024,512]{1,0:T(8,128)(2,1)} %copy-done, bf16[1024,512]{1,0:T(8,128)(2,1)} %collective-permute-done.1.refs_2_.refs_4_, ...), custom_call_target="tpu_custom_call" | custom-call | tf_op jit(solution)/shard_map/pallas_call | solution.py:67
  149.0 22.3 %all_to_all.20 = bf16[8,32,2560]{2,1,0:T(8,128)(2,1)S(1)} all-to-all(bf16[8,32,2560]{2,1,0:T(8,128)(2,1)} %shard_map.71), channel_id=1, replica_groups=mesh['x'=4,'yl'=2,'c'=2,'z'=8,'yh'=2] {'x','yl'}, dimensions={0} | all-to-all | bytes 2621440 | tf_op jit(solution)/shard_map/all_to_all | solution.py:237
  177.1 4.6 %shard_map.72 = bf16[1024,256]{1,0:T(8,128)(2,1)} custom-call(s32[1]{0:T(128)} %bitcast.refs_0_, bf16[256,2560]{1,0:T(8,128)(2,1)} %bitcast.38, bf16[256,2560]{1,0:T(8,128)(2,1)} %copy-done.6, bf16[1024,512]{1,0:T(8,128)(2,1)} %copy-done.5, bf16[1024,512]{1,0:T(8,128)(2,1)} %copy-done.4, bf16[1024,512]{1,0:T(8,128)(2,1)} %copy-done.3, ...), custom_call_target="tpu_custom_call" | custom-call | tf_op jit(solution)/shard_map/pallas_call | solution.py:67
  183.4 4.6 %shard_map.73 = bf16[1024,256]{1,0:T(8,128)(2,1)} custom-call(s32[1]{0:T(128)} %bitcast.refs_0_, bf16[256,2560]{1,0:T(8,128)(2,1)} %bitcast.39, bf16[256,2560]{1,0:T(8,128)(2,1)} %copy-done.6, bf16[1024,512]{1,0:T(8,128)(2,1)} %copy-done.5, bf16[1024,512]{1,0:T(8,128)(2,1)} %copy-done.4, bf16[1024,512]{1,0:T(8,128)(2,1)} %copy-done.3, ...), custom_call_target="tpu_custom_call" | custom-call | tf_op jit(solution)/shard_map/pallas_call | solution.py:67
  189.5 4.7 %shard_map.75 = f32[1024,256]{1,0:T(8,128)} custom-call(s32[1]{0:T(128)} %bitcast.refs_0_, bf16[256,2560]{1,0:T(8,128)(2,1)} %bitcast.40, bf16[256,2560]{1,0:T(8,128)(2,1)} %copy-done.6, bf16[1024,512]{1,0:T(8,128)(2,1)} %copy-done.5, bf16[1024,512]{1,0:T(8,128)(2,1)} %copy-done.4, bf16[1024,512]{1,0:T(8,128)(2,1)} %copy-done.3, ...), custom_call_target="tpu_custom_call" | custom-call | tf_op jit(solution)/shard_map/pallas_call | solution.py:67
  194.2 4.7 %shard_map.74 = f32[1024,256]{1,0:T(8,128)} custom-call(s32[1]{0:T(128)} %bitcast.refs_0_, bf16[256,2560]{1,0:T(8,128)(2,1)} %bitcast.41, bf16[256,2560]{1,0:T(8,128)(2,1)} %copy-done.6, bf16[1024,512]{1,0:T(8,128)(2,1)} %copy-done.5, bf16[1024,512]{1,0:T(8,128)(2,1)} %copy-done.4, bf16[1024,512]{1,0:T(8,128)(2,1)} %copy-done.3, ...), custom_call_target="tpu_custom_call" | custom-call | tf_op jit(solution)/shard_map/pallas_call | solution.py:67
  201.3 6.6 %collective-permute-done.20 = bf16[1024,256]{1,0:T(8,128)(2,1)S(1)} collective-permute-done((bf16[1024,256]{1,0:T(8,128)(2,1)}, bf16[1024,256]{1,0:T(8,128)(2,1)S(1)}, u32[]{:S(2)}, u32[]{:S(2)}) %collective-permute-start.20) | collective-permute-done | bytes 524320 | tf_op jit(solution)/shard_map/ppermute | solution.py:22
  (96 shorter events, 40.7 us)
Async XLA Ops:
  1.9 36.8 %copy-start = (bf16[1024,512]{1,0:T(8,128)(2,1)}, bf16[1024,512]{1,0:T(8,128)(2,1)S(1)}, u32[]{:S(2)}) copy-start(bf16[1024,512]{1,0:T(8,128)(2,1)S(1)} %pad_maximum_fusion.refs_1_.refs_3_) | copy-start | bytes 3145732
  1.9 25.7 %collective-permute-start.2 = (bf16[1024,512]{1,0:T(8,128)(2,1)S(1)}, bf16[1024,512]{1,0:T(8,128)(2,1)S(1)}, u32[]{:S(2)}, u32[]{:S(2)}) collective-permute-start(bf16[1024,512]{1,0:T(8,128)(2,1)S(1)} %pad_maximum_fusion.refs_1_.refs_3_), channel_id=1, source_target_pairs={{0,1},{1,0},{2,3},{3,2},{4,5},{5,4},{6,7},{7,6},{8,9},{9,8},{10,11... | collective-permute-start | bytes 3145736 | tf_op jit(solution)/shard_map/ppermute | solution.py:22
  5.8 27.1 %collective-permute-start.1 = (bf16[1024,512]{1,0:T(8,128)(2,1)S(1)}, bf16[1024,512]{1,0:T(8,128)(2,1)}, u32[]{:S(2)}, u32[]{:S(2)}) collective-permute-start(bf16[1024,512]{1,0:T(8,128)(2,1)S(1)} %pad_maximum_fusion.refs_1_.refs_3_), channel_id=1, source_target_pairs={{0,14},{2,0},{4,2},{6,4},{8,6},{10,8},{12,10},{14,12},{1,15},{3,1}... | collective-permute-start | bytes 3145736 | tf_op jit(solution)/shard_map/ppermute | solution.py:18
  11.3 24.7 %collective-permute-start = (bf16[1024,512]{1,0:T(8,128)(2,1)S(1)}, bf16[1024,512]{1,0:T(8,128)(2,1)}, u32[]{:S(2)}, u32[]{:S(2)}) collective-permute-start(bf16[1024,512]{1,0:T(8,128)(2,1)S(1)} %pad_maximum_fusion.refs_1_.refs_3_), channel_id=1, source_target_pairs={{0,2},{2,4},{4,6},{6,8},{8,10},{10,12},{12,14},{14,0},{1,3},{3,5},... | collective-permute-start | bytes 3145736 | tf_op jit(solution)/shard_map/ppermute | solution.py:18
  36.1 23.9 %collective-permute-start.3 = (bf16[1024,512]{1,0:T(8,128)(2,1)}, bf16[1024,512]{1,0:T(8,128)(2,1)S(1)}, u32[]{:S(2)}, u32[]{:S(2)}) collective-permute-start(bf16[1024,512]{1,0:T(8,128)(2,1)} %collective-permute-done.refs_3_.refs_5_), channel_id=1, source_target_pairs={{0,2},{2,4},{4,6},{6,8},{8,10},{10,12},{12,14},{14,0},{1,3},{3,5},... | collective-permute-start | bytes 3145736 | tf_op jit(solution)/shard_map/ppermute | solution.py:18
  36.1 23.9 %collective-permute-start.4 = (bf16[1024,512]{1,0:T(8,128)(2,1)}, bf16[1024,512]{1,0:T(8,128)(2,1)S(1)}, u32[]{:S(2)}, u32[]{:S(2)}) collective-permute-start(bf16[1024,512]{1,0:T(8,128)(2,1)} %collective-permute-done.1.refs_2_.refs_4_), channel_id=1, source_target_pairs={{0,14},{2,0},{4,2},{6,4},{8,6},{10,8},{12,10},{14,12},{1,15},{3,1}... | collective-permute-start | bytes 3145736 | tf_op jit(solution)/shard_map/ppermute | solution.py:18
  47.7 4.6 %collective-permute-start.5 = (f32[256,512]{1,0:T(8,128)}, f32[256,512]{1,0:T(8,128)S(1)}, u32[]{:S(2)}, u32[]{:S(2)}) collective-permute-start(f32[256,512]{1,0:T(8,128)} %get-tuple-element.40), channel_id=1, source_target_pairs={{0,16},{16,0},{1,17},{17,1},{2,18},{18,2},{3,19},{19,3},{4,20},{20... | collective-permute-start | bytes 1572872 | tf_op jit(solution)/shard_map/ppermute | solution.py:22
  50.5 2.5 %collective-permute-start.6 = (f32[256,512]{1,0:T(8,128)}, f32[256,512]{1,0:T(8,128)S(1)}, u32[]{:S(2)}, u32[]{:S(2)}) collective-permute-start(f32[256,512]{1,0:T(8,128)} %get-tuple-element.41), channel_id=1, source_target_pairs={{0,16},{16,0},{1,17},{17,1},{2,18},{18,2},{3,19},{19,3},{4,20},{20... | collective-permute-start | bytes 1572872 | tf_op jit(solution)/shard_map/ppermute | solution.py:22
  50.6 3.1 %collective-permute-start.7 = (f32[256,512]{1,0:T(8,128)}, f32[256,512]{1,0:T(8,128)S(1)}, u32[]{:S(2)}, u32[]{:S(2)}) collective-permute-start(f32[256,512]{1,0:T(8,128)} %get-tuple-element.42), channel_id=1, source_target_pairs={{0,16},{16,0},{1,17},{17,1},{2,18},{18,2},{3,19},{19,3},{4,20},{20... | collective-permute-start | bytes 1572872 | tf_op jit(solution)/shard_map/ppermute | solution.py:22
  52.2 19.7 %copy-start.16 = (f32[256,512]{1,0:T(8,128)}, f32[256,512]{1,0:T(8,128)S(1)}, u32[]{:S(2)}) copy-start(f32[256,512]{1,0:T(8,128)S(1)} %collective-permute-done.5.refs_1_) | copy-start | bytes 1572868
  53.0 19.0 %copy-start.17 = (f32[256,512]{1,0:T(8,128)}, f32[256,512]{1,0:T(8,128)S(1)}, u32[]{:S(2)}) copy-start(f32[256,512]{1,0:T(8,128)S(1)} %collective-permute-done.6.refs_2_) | copy-start | bytes 1572868
  53.7 18.2 %copy-start.18 = (f32[256,512]{1,0:T(8,128)}, f32[256,512]{1,0:T(8,128)S(1)}, u32[]{:S(2)}) copy-start(f32[256,512]{1,0:T(8,128)S(1)} %collective-permute-done.7.refs_3_) | copy-start | bytes 1572868
  61.0 22.8 %collective-permute-start.8 = (bf16[1024,512]{1,0:T(8,128)(2,1)S(1)}, bf16[1024,512]{1,0:T(8,128)(2,1)S(1)}, u32[]{:S(2)}, u32[]{:S(2)}) collective-permute-start(bf16[1024,512]{1,0:T(8,128)(2,1)S(1)} %collective-permute-done.3.refs_2_.refs_4_), channel_id=1, source_target_pairs={{0,2},{2,4},{4,6},{6,8},{8,10},{10,12},{12,14},{14,0},{1,3},{3,5},... | collective-permute-start | bytes 3145736 | tf_op jit(solution)/shard_map/ppermute | solution.py:18
  61.0 22.8 %collective-permute-start.9 = (bf16[1024,512]{1,0:T(8,128)(2,1)}, bf16[1024,512]{1,0:T(8,128)(2,1)S(1)}, u32[]{:S(2)}, u32[]{:S(2)}) collective-permute-start(bf16[1024,512]{1,0:T(8,128)(2,1)} %copy-done.5), channel_id=1, source_target_pairs={{0,14},{2,0},{4,2},{6,4},{8,6},{10,8},{12,10},{14,12},{1,15},{3,1}... | collective-permute-start | bytes 3145736 | tf_op jit(solution)/shard_map/ppermute | solution.py:18
  68.1 11.1 %collective-permute-start.10 = (f32[256,512]{1,0:T(8,128)}, f32[256,512]{1,0:T(8,128)}, u32[]{:S(2)}, u32[]{:S(2)}) collective-permute-start(f32[256,512]{1,0:T(8,128)} %get-tuple-element.46), channel_id=1, source_target_pairs={{0,16},{16,0},{1,17},{17,1},{2,18},{18,2},{3,19},{19,3},{4,20},{20... | collective-permute-start | bytes 1572872 | tf_op jit(solution)/shard_map/ppermute | solution.py:22
  71.8 7.4 %collective-permute-start.11 = (f32[256,512]{1,0:T(8,128)}, f32[256,512]{1,0:T(8,128)}, u32[]{:S(2)}, u32[]{:S(2)}) collective-permute-start(f32[256,512]{1,0:T(8,128)} %get-tuple-element.47), channel_id=1, source_target_pairs={{0,16},{16,0},{1,17},{17,1},{2,18},{18,2},{3,19},{19,3},{4,20},{20... | collective-permute-start | bytes 1572872 | tf_op jit(solution)/shard_map/ppermute | solution.py:22
  74.8 25.7 %all-to-all-start = ((bf16[8,32,1536]{2,1,0:T(8,128)(2,1)}), bf16[8,32,1536]{2,1,0:T(8,128)(2,1)}, u32[]{:S(2)}, u32[]{:S(2)}) async-start(bf16[8,32,1536]{2,1,0:T(8,128)(2,1)} %bitcast.48), calls=%async_computation | async-start | bytes 1572864 | tf_op jit(solution)/shard_map/all_to_all | solution.py:228
  85.5 11.7 %copy-start.22 = (f32[2]{0:T(128)S(1)}, f32[2]{0:T(128)}, u32[]{:S(2)}) copy-start(f32[2]{0:T(128)} %param.6) | copy-start | bytes 28
  85.5 12.3 %copy-start.20 = (f32[4096]{0:T(1024)S(1)}, f32[4096]{0:T(1024)}, u32[]{:S(2)}) copy-start(f32[4096]{0:T(1024)} %param.7) | copy-start | bytes 49156
  89.9 17.0 %collective-permute-start.13 = (bf16[512,512]{1,0:T(8,128)(2,1)}, bf16[512,512]{1,0:T(8,128)(2,1)S(1)}, u32[]{:S(2)}, u32[]{:S(2)}) collective-permute-start(bf16[512,512]{1,0:T(8,128)(2,1)} %slice.13), channel_id=1, source_target_pairs={{0,14},{2,0},{4,2},{6,4},{8,6},{10,8},{12,10},{14,12},{1,15},{3,1}... | collective-permute-start | bytes 1572872 | tf_op jit(solution)/shard_map/ppermute | solution.py:18
  92.6 14.3 %collective-permute-start.12 = (bf16[512,512]{1,0:T(8,128)(2,1)}, bf16[512,512]{1,0:T(8,128)(2,1)S(1)}, u32[]{:S(2)}, u32[]{:S(2)}) collective-permute-start(bf16[512,512]{1,0:T(8,128)(2,1)} %slice.12), channel_id=1, source_target_pairs={{0,2},{2,4},{4,6},{6,8},{8,10},{10,12},{12,14},{14,0},{1,3},{3,5},... | collective-permute-start | bytes 1572872 | tf_op jit(solution)/shard_map/ppermute | solution.py:18
  92.6 14.3 %collective-permute-start.14 = (f32[256,512]{1,0:T(8,128)}, f32[256,512]{1,0:T(8,128)S(1)}, u32[]{:S(2)}, u32[]{:S(2)}) collective-permute-start(f32[256,512]{1,0:T(8,128)} %get-tuple-element.54), channel_id=1, source_target_pairs={{0,16},{16,0},{1,17},{17,1},{2,18},{18,2},{3,19},{19,3},{4,20},{20... | collective-permute-start | bytes 1572872 | tf_op jit(solution)/shard_map/ppermute | solution.py:22
  97.1 9.8 %collective-permute-start.15 = (f32[256,512]{1,0:T(8,128)}, f32[256,512]{1,0:T(8,128)S(1)}, u32[]{:S(2)}, u32[]{:S(2)}) collective-permute-start(f32[256,512]{1,0:T(8,128)} %get-tuple-element.55), channel_id=1, source_target_pairs={{0,16},{16,0},{1,17},{17,1},{2,18},{18,2},{3,19},{19,3},{4,20},{20... | collective-permute-start | bytes 1572872 | tf_op jit(solution)/shard_map/ppermute | solution.py:22
  102.7 15.9 %all-to-all-start.1 = ((bf16[8,32,1536]{2,1,0:T(8,128)(2,1)}), bf16[8,32,1536]{2,1,0:T(8,128)(2,1)S(1)}, u32[]{:S(2)}, u32[]{:S(2)}) async-start(bf16[8,32,1536]{2,1,0:T(8,128)(2,1)} %shard_map.65), calls=%async_computation.1 | async-start | bytes 1572864 | tf_op jit(solution)/shard_map/all_to_all | solution.py:237
  111.4 7.2 %collective-permute-start.16 = (f32[256,512]{1,0:T(8,128)}, f32[256,512]{1,0:T(8,128)S(1)}, u32[]{:S(2)}, u32[]{:S(2)}) collective-permute-start(f32[256,512]{1,0:T(8,128)} %get-tuple-element.62), channel_id=1, source_target_pairs={{0,16},{16,0},{1,17},{17,1},{2,18},{18,2},{3,19},{19,3},{4,20},{20... | collective-permute-start | bytes 1572872 | tf_op jit(solution)/shard_map/ppermute | solution.py:22
  123.1 22.1 %all-to-all-start.2 = ((bf16[8,32,2560]{2,1,0:T(8,128)(2,1)}), bf16[8,32,2560]{2,1,0:T(8,128)(2,1)S(1)}, u32[]{:S(2)}, u32[]{:S(2)}) async-start(bf16[8,32,2560]{2,1,0:T(8,128)(2,1)} %bitcast.47), calls=%async_computation.2 | async-start | bytes 2621440 | tf_op jit(solution)/shard_map/all_to_all | solution.py:228
  126.7 3.6 %collective-permute-start.17 = (bf16[256,1536]{1,0:T(8,128)(2,1)S(1)}, bf16[256,1536]{1,0:T(8,128)(2,1)S(1)}, u32[]{:S(2)}, u32[]{:S(2)}) collective-permute-start(bf16[256,1536]{1,0:T(8,128)(2,1)S(1)} %bitcast.42), channel_id=1, source_target_pairs={{0,16},{16,0},{1,17},{17,1},{2,18},{18,2},{3,19},{19,3},{4,20},{20... | collective-permute-start | bytes 2359304 | tf_op jit(solution)/shard_map/ppermute | solution.py:22
  128.5 9.7 %copy-start.21 = (f32[1,1280]{1,0:T(1,128)}, f32[1,1280]{1,0:T(1,128)S(1)}, u32[]{:S(2)}) copy-start(f32[1,1280]{1,0:T(1,128)S(1)} %constant_dynamic-update-slice_fusion.refs_2_) | copy-start | bytes 15364
  171.3 4.7 %collective-permute-start.18 = (bf16[256,2560]{1,0:T(8,128)(2,1)S(1)}, bf16[256,2560]{1,0:T(8,128)(2,1)S(1)}, u32[]{:S(2)}, u32[]{:S(2)}) collective-permute-start(bf16[256,2560]{1,0:T(8,128)(2,1)S(1)} %bitcast.37), channel_id=1, source_target_pairs={{0,16},{16,0},{1,17},{17,1},{2,18},{18,2},{3,19},{19,3},{4,20},{20... | collective-permute-start | bytes 3932168 | tf_op jit(solution)/shard_map/ppermute | solution.py:22
  181.7 17.2 %collective-permute-start.19 = (bf16[1024,256]{1,0:T(8,128)(2,1)}, bf16[1024,256]{1,0:T(8,128)(2,1)S(1)}, u32[]{:S(2)}, u32[]{:S(2)}) collective-permute-start(bf16[1024,256]{1,0:T(8,128)(2,1)} %shard_map.72), channel_id=1, source_target_pairs={{0,1},{1,0},{2,3},{3,2},{4,5},{5,4},{6,7},{7,6},{8,9},{9,8},{10,11... | collective-permute-start | bytes 1572872 | tf_op jit(solution)/shard_map/ppermute | solution.py:22
  188.0 19.9 %collective-permute-start.20 = (bf16[1024,256]{1,0:T(8,128)(2,1)}, bf16[1024,256]{1,0:T(8,128)(2,1)S(1)}, u32[]{:S(2)}, u32[]{:S(2)}) collective-permute-start(bf16[1024,256]{1,0:T(8,128)(2,1)} %shard_map.73), channel_id=1, source_target_pairs={{0,1},{1,0},{2,3},{3,2},{4,5},{5,4},{6,7},{7,6},{8,9},{9,8},{10,11... | collective-permute-start | bytes 1572872 | tf_op jit(solution)/shard_map/ppermute | solution.py:22
  198.9 9.0 %copy-start.12 = (f32[1024,256]{1,0:T(8,128)S(1)}, f32[1024,256]{1,0:T(8,128)}, u32[]{:S(2)}) copy-start(f32[1024,256]{1,0:T(8,128)} %shard_map.75) | copy-start | bytes 3145732
  (15 other events, 44.1 us)

commit v5 on v4

--- a/solution.py
+++ b/solution.py
@@ -220,11 +220,13 @@
         kept, given = products(left, blocks, width, cost)
         return kept, [swap(part, "c") for part in given]
 
-    def scatter(sets):
+    def added(sets):
         counts = [len(given) for _, given in sets]
         shape = jax.ShapeDtypeStruct((width, 2 * width * sum(counts)), BF16)
         flat = [part for kept, given in sets for part in [kept, *given]]
-        summed = call(functools.partial(sum_kernel, counts, width), shape, *flat)
+        return call(functools.partial(sum_kernel, counts, width), shape, *flat)
+
+    def scatter(summed):
         return lax.all_to_all(summed.reshape(CHIPS, rows, -1), ("x", "yl"), 0, 0, tiled=True)
 
     def amplitudes(group, pieces, copies):
@@ -255,8 +257,9 @@
     near_halves = halves(near_blocks)
     (up2, down2), near_halves = lax.optimization_barrier(((up2, down2), near_halves))
     up3, down3 = both(up2, 1), both(down2, -1)
-    pieces_a = scatter([near_halves])
-    middle_halves = halves([down2, up2])
+    summed_a = added([near_halves])
+    pieces_a = scatter(summed_a)
+    middle_halves = halves(after([down2, up2], summed_a))
     (up3, down3), middle_halves = lax.optimization_barrier(((up3, down3), middle_halves))
     far = shift(up3[0][:half], "z", NZ, 1), shift(down3[0][half:], "z", NZ, -1)
 
@@ -264,10 +267,8 @@
     amp_a = amplitudes(near, pieces_a, CHIPS)
     mine_a = spread(amp_a)
     other_a = swap(mine_a, "c")
-    third_halves = halves([down3, up3])
-    last, third_halves = lax.optimization_barrier((far, third_halves))
-    last_halves = halves([last])
-    pieces_b = scatter([middle_halves, third_halves, after(last_halves, mine_a)])
+    last_halves = halves(distant_blocks[2:])
+    pieces_b = scatter(after(added([middle_halves, last_halves]), mine_a))
     sums = [[gamma(side, store, near_blocks, mine_a, other_a) for store in range(2)] for side in range(2)]
     amp_b = amplitudes(distant, after(pieces_b, sums), CHIPS)
     mine_b = spread(amp_b)

time: 210 us -> 205 us (0.976)
  Pallas kernels: 65.2 us -> 62.5 us
  blocking collectives: 22.3 us -> 19.9 us
    ppermute x8, waiting for transfers between devices: 19.3 us -> 31.3 us  [shift(): lax.ppermute(value, axis, [(i, (i + step) % size) for i in range(size)])]
    ppermute x13, waiting for transfers between devices: 30 us -> 20 us  [swap(): return lax.ppermute(value, axis, [(0, 1), (1, 0)])]
    all_to_all x1, waiting for transfers between devices: 5.89 us -> 0.01 us  [spread(): lax.all_to_all(copies, ('x', 'yl'), 0, 0, tiled=True).reshape(width, -1)]
    pallas_call x17 -> x16, Pallas kernels: 65.2 us -> 62.5 us  [call(): pl.pallas_call(body, out_shape=out_shape, in_specs=specs, out_specs=out_s...]
    ppermute x13, starting transfers between devices: 23.8 us -> 21.1 us  [swap(): return lax.ppermute(value, axis, [(0, 1), (1, 0)])]
    all_to_all x2, starting transfers between devices: 7.98 us -> 10.6 us  [scatter(): lax.all_to_all(summed.reshape(CHIPS, rows, -1), ('x', 'yl'), 0, 0, tiled=...]
    all_to_all x1, blocking collectives: 22.3 us -> 19.9 us  [spread(): lax.all_to_all(copies, ('x', 'yl'), 0, 0, tiled=True).reshape(width, -1)]
    all_to_all x2, waiting for transfers between devices: 0.01 us -> 2.32 us  [scatter(): lax.all_to_all(summed.reshape(CHIPS, rows, -1), ('x', 'yl'), 0, 0, tiled=...]
  transfers between devices with their start and end apart: 24 -> 24, of which waited for: 12 -> 14; matrix products, arithmetic and copies ran while one was open for 3% -> 2% of each run, Pallas kernels for 26% -> 27%
where the time goes in v5:
time: 205 us; the launch traced here: 204 us
  Pallas kernels  62.5 us (30%)
  waiting for transfers between devices  53.7 us (26%)
  starting transfers between devices  51.4 us (25%)
  blocking collectives  19.9 us (10%)
  local copies, waits for them, and re-layouts  10.6 us (5%)
  other arithmetic  4.09 us (2%)
  between operations  2.18 us (1%)
    pallas_call x16, Pallas kernels, call(): pl.pallas_call(body, out_shape=out_shape, in_specs=specs, out_specs=out_s...  62.5 us
    ppermute x8, waiting for transfers between devices, shift(): lax.ppermute(value, axis, [(i, (i + step) % size) for i in range(size)])  31.3 us
    ppermute x13, starting transfers between devices, swap(): return lax.ppermute(value, axis, [(0, 1), (1, 0)])  21.1 us
    ppermute x13, waiting for transfers between devices, swap(): return lax.ppermute(value, axis, [(0, 1), (1, 0)])  20 us
    all_to_all x1, blocking collectives, spread(): lax.all_to_all(copies, ('x', 'yl'), 0, 0, tiled=True).reshape(width, -1)  19.9 us
    ppermute x8, starting transfers between devices, shift(): lax.ppermute(value, axis, [(i, (i + step) % size) for i in range(size)])  14.6 us
    all_to_all x2, starting transfers between devices, scatter(): lax.all_to_all(summed.reshape(CHIPS, rows, -1), ('x', 'yl'), 0, 0, tiled=...  10.6 us
    unnamed x52, local copies, waits for them, and re-layouts  7.56 us
  transfers between devices with their start and end apart: 24, of which 14 were waited for; matrix products, arithmetic and copies ran while one was open for 2% of the time, Pallas kernels for 27%

profile of v5, /device:TPU:1, one launch (start us, length us, event | category | flops | bytes accessed | tf_op | source)
XLA Modules:
  0.0 204.3 jit_solution(13053188915555616085)
XLA Ops:
  4.5 4.0 %collective-permute-start.1 = (bf16[1024,512]{1,0:T(8,128)(2,1)S(1)}, bf16[1024,512]{1,0:T(8,128)(2,1)}, u32[]{:S(2)}, u32[]{:S(2)}) collective-permute-start(bf16[1024,512]{1,0:T(8,128)(2,1)S(1)} %pad_maximum_fusion.refs_1_.refs_3_), channel_id=1, source_target_pairs={{0,14},{2,0},{4,2},{6,4},{8,6},{10,8},{12,10},{14,12},{1,15},{3,1}... | collective-permute-start | bytes 3145736 | tf_op jit(solution)/shard_map/ppermute | solution.py:18
  8.5 2.9 %collective-permute-start.2 = (bf16[1024,512]{1,0:T(8,128)(2,1)S(1)}, bf16[1024,512]{1,0:T(8,128)(2,1)S(1)}, u32[]{:S(2)}, u32[]{:S(2)}) collective-permute-start(bf16[1024,512]{1,0:T(8,128)(2,1)S(1)} %pad_maximum_fusion.refs_1_.refs_3_), channel_id=1, source_target_pairs={{0,1},{1,0},{2,3},{3,2},{4,5},{5,4},{6,7},{7,6},{8,9},{9,8},{10,11... | collective-permute-start | bytes 3145736 | tf_op jit(solution)/shard_map/ppermute | solution.py:22
  11.4 20.0 %collective-permute-done.refs_3_.refs_5_ = bf16[1024,512]{1,0:T(8,128)(2,1)} collective-permute-done((bf16[1024,512]{1,0:T(8,128)(2,1)S(1)}, bf16[1024,512]{1,0:T(8,128)(2,1)}, u32[]{:S(2)}, u32[]{:S(2)}) %collective-permute-start) | collective-permute-done | bytes 1048608 | tf_op jit(solution)/shard_map/ppermute | solution.py:18
  34.7 2.7 %collective-permute-start.4 = (bf16[1024,512]{1,0:T(8,128)(2,1)}, bf16[1024,512]{1,0:T(8,128)(2,1)S(1)}, u32[]{:S(2)}, u32[]{:S(2)}) collective-permute-start(bf16[1024,512]{1,0:T(8,128)(2,1)} %collective-permute-done.1.refs_2_.refs_4_), channel_id=1, source_target_pairs={{0,14},{2,0},{4,2},{6,4},{8,6},{10,8},{12,10},{14,12},{1,15},{3,1}... | collective-permute-start | bytes 3145736 | tf_op jit(solution)/shard_map/ppermute | solution.py:18
  37.4 3.6 %shard_map.59.refs_0_ = bf16[1024,1024]{1,0:T(8,128)(2,1)} custom-call(s32[1]{0:T(128)} %bitcast.refs_0_, bf16[1024,512]{1,0:T(8,128)(2,1)} %copy-done, bf16[1024,512]{1,0:T(8,128)(2,1)} %copy-done.14), custom_call_target="tpu_custom_call" | custom-call | tf_op jit(solution)/shard_map/pallas_call | solution.py:67
  41.0 5.3 %shard_map.60 = (f32[256,1536]{1,0:T(8,128)}, f32[256,512]{1,0:T(8,128)}, f32[256,512]{1,0:T(8,128)}, f32[256,512]{1,0:T(8,128)}) custom-call(bf16[1024,1024]{1,0:T(8,128)(2,1)} %shard_map.59.refs_0_, bf16[1024,512]{1,0:T(8,128)(2,1)} %copy-done, bf16[1024,512]{1,0:T(8,128)(2,1)} %collective-permute-done.1.refs_2_.refs_4_, ...), custom_call_target="tpu_custom_call" | custom-call | tf_op jit(solution)/shard_map/pallas_call | solution.py:67
  52.0 6.8 %collective-permute-done.3.refs_2_.refs_4_ = bf16[1024,512]{1,0:T(8,128)(2,1)S(1)} collective-permute-done((bf16[1024,512]{1,0:T(8,128)(2,1)}, bf16[1024,512]{1,0:T(8,128)(2,1)S(1)}, u32[]{:S(2)}, u32[]{:S(2)}) %collective-permute-start.3) | collective-permute-done | bytes 1048608 | tf_op jit(solution)/shard_map/ppermute | solution.py:18
  59.9 2.7 %collective-permute-start.9 = (bf16[1024,512]{1,0:T(8,128)(2,1)}, bf16[1024,512]{1,0:T(8,128)(2,1)S(1)}, u32[]{:S(2)}, u32[]{:S(2)}) collective-permute-start(bf16[1024,512]{1,0:T(8,128)(2,1)} %copy-done.5), channel_id=1, source_target_pairs={{0,14},{2,0},{4,2},{6,4},{8,6},{10,8},{12,10},{14,12},{1,15},{3,1}... | collective-permute-start | bytes 3145736 | tf_op jit(solution)/shard_map/ppermute | solution.py:18
  62.6 2.8 %shard_map.61 = bf16[256,1536]{1,0:T(8,128)(2,1)} custom-call(f32[256,1536]{1,0:T(8,128)} %get-tuple-element.40.refs_0_, f32[256,512]{1,0:T(8,128)} %copy-done.15, f32[256,512]{1,0:T(8,128)} %copy-done.16, f32[256,512]{1,0:T(8,128)} %copy-done.17), custom_call_target="tpu_custom_call" | custom-call | tf_op jit(solution)/shard_map/pallas_call | solution.py:67
  65.4 4.4 %shard_map.62 = (f32[256,1024]{1,0:T(8,128)}, f32[256,512]{1,0:T(8,128)}, f32[256,512]{1,0:T(8,128)}) custom-call(bf16[1024,1024]{1,0:T(8,128)(2,1)} %shard_map.59.refs_0_, bf16[1024,512]{1,0:T(8,128)(2,1)} %copy-done.5, bf16[1024,512]{1,0:T(8,128)(2,1)} %copy-done.4), custom_call_target="tpu_custom_call" | custom-call | tf_op jit(solution)/shard_map/pallas_call | solution.py:67
  69.8 3.4 %collective-permute-start.10 = (f32[256,512]{1,0:T(8,128)}, f32[256,512]{1,0:T(8,128)}, u32[]{:S(2)}, u32[]{:S(2)}) collective-permute-start(f32[256,512]{1,0:T(8,128)} %get-tuple-element.47), channel_id=1, source_target_pairs={{0,16},{16,0},{1,17},{17,1},{2,18},{18,2},{3,19},{19,3},{4,20},{20... | collective-permute-start | bytes 1572872 | tf_op jit(solution)/shard_map/ppermute | solution.py:22
  73.3 5.2 %all-to-all-start = ((bf16[8,32,1536]{2,1,0:T(8,128)(2,1)}), bf16[8,32,1536]{2,1,0:T(8,128)(2,1)}, u32[]{:S(2)}, u32[]{:S(2)}) async-start(bf16[8,32,1536]{2,1,0:T(8,128)(2,1)} %bitcast.48), calls=%async_computation | async-start | bytes 1572864 | tf_op jit(solution)/shard_map/all_to_all | solution.py:230
  78.5 4.5 %collective-permute-done.8.refs_2_.refs_6_ = bf16[1024,512]{1,0:T(8,128)(2,1)S(1)} collective-permute-done((bf16[1024,512]{1,0:T(8,128)(2,1)S(1)}, bf16[1024,512]{1,0:T(8,128)(2,1)S(1)}, u32[]{:S(2)}, u32[]{:S(2)}) %collective-permute-start.8) | collective-permute-done | bytes 1048608 | tf_op jit(solution)/shard_map/ppermute | solution.py:18
  92.9 5.0 %all-to-all-start.1 = ((bf16[8,32,1536]{2,1,0:T(8,128)(2,1)}), bf16[8,32,1536]{2,1,0:T(8,128)(2,1)S(1)}, u32[]{:S(2)}, u32[]{:S(2)}) async-start(bf16[8,32,1536]{2,1,0:T(8,128)(2,1)} %shard_map.65), calls=%async_computation.1 | async-start | bytes 1572864 | tf_op jit(solution)/shard_map/all_to_all | solution.py:239
  99.5 5.3 %shard_map.63 = (f32[256,1536]{1,0:T(8,128)}, f32[256,512]{1,0:T(8,128)}, f32[256,512]{1,0:T(8,128)}, f32[256,512]{1,0:T(8,128)}) custom-call(bf16[1024,1024]{1,0:T(8,128)(2,1)} %shard_map.59.refs_0_, bf16[1024,512]{1,0:T(8,128)(2,1)} %copy-done.3, bf16[1024,512]{1,0:T(8,128)(2,1)} %copy-done.2, bf16[512,512]{1,0:T(8,128)(2,1)} %copy-done.8, ...), custom_call_target="tpu_custom_call" | custom-call | tf_op jit(solution)/shard_map/pallas_call | solution.py:67
  104.8 4.6 %collective-permute-start.14 = (f32[256,512]{1,0:T(8,128)}, f32[256,512]{1,0:T(8,128)S(1)}, u32[]{:S(2)}, u32[]{:S(2)}) collective-permute-start(f32[256,512]{1,0:T(8,128)} %get-tuple-element.55), channel_id=1, source_target_pairs={{0,16},{16,0},{1,17},{17,1},{2,18},{18,2},{3,19},{19,3},{4,20},{20... | collective-permute-start | bytes 1572872 | tf_op jit(solution)/shard_map/ppermute | solution.py:22
  113.5 3.7 %shard_map.64 = bf16[256,2560]{1,0:T(8,128)(2,1)} custom-call(f32[256,1024]{1,0:T(8,128)} %get-tuple-element.49.refs_0_, f32[256,512]{1,0:T(8,128)} %collective-permute-done.10.refs_1_, f32[256,512]{1,0:T(8,128)} %collective-permute-done.11.refs_2_, f32[256,1536]{1,0:T(8,128)} %get-tuple-element.54.refs_3_, f32[256,512]{1,0:T(8,128)} %copy-done.18, ...), custom_call_target="tpu_custom_call" | custom-call | tf_op jit(solution)/shard_map/pallas_call | solution.py:67
  117.2 5.4 %all-to-all-start.2 = ((bf16[8,32,2560]{2,1,0:T(8,128)(2,1)}), bf16[8,32,2560]{2,1,0:T(8,128)(2,1)S(1)}, u32[]{:S(2)}, u32[]{:S(2)}) async-start(bf16[8,32,2560]{2,1,0:T(8,128)(2,1)} %bitcast.47), calls=%async_computation.2 | async-start | bytes 2621440 | tf_op jit(solution)/shard_map/all_to_all | solution.py:230
  126.1 3.5 %shard_map.66.refs_9_ = f32[1024,256]{1,0:T(8,128)} custom-call(s32[1]{0:T(128)} %bitcast.refs_0_, bf16[256,1536]{1,0:T(8,128)(2,1)} %bitcast.43, bf16[256,1536]{1,0:T(8,128)(2,1)} %copy-done.10, bf16[1024,512]{1,0:T(8,128)(2,1)} %copy-done, bf16[1024,512]{1,0:T(8,128)(2,1)} %collective-permute-done.1.refs_2_.refs_4_, ...), custom_call_target="tpu_custom_call" | custom-call | tf_op jit(solution)/shard_map/pallas_call | solution.py:67
  129.6 3.5 %shard_map.67.refs_9_ = f32[1024,256]{1,0:T(8,128)} custom-call(s32[1]{0:T(128)} %bitcast.refs_0_, bf16[256,1536]{1,0:T(8,128)(2,1)} %bitcast.44, bf16[256,1536]{1,0:T(8,128)(2,1)} %copy-done.10, bf16[1024,512]{1,0:T(8,128)(2,1)} %copy-done, bf16[1024,512]{1,0:T(8,128)(2,1)} %collective-permute-done.1.refs_2_.refs_4_, ...), custom_call_target="tpu_custom_call" | custom-call | tf_op jit(solution)/shard_map/pallas_call | solution.py:67
  133.1 3.4 %shard_map.68.refs_9_ = f32[1024,256]{1,0:T(8,128)} custom-call(s32[1]{0:T(128)} %bitcast.refs_0_, bf16[256,1536]{1,0:T(8,128)(2,1)} %bitcast.45, bf16[256,1536]{1,0:T(8,128)(2,1)} %copy-done.10, bf16[1024,512]{1,0:T(8,128)(2,1)} %copy-done, bf16[1024,512]{1,0:T(8,128)(2,1)} %collective-permute-done.1.refs_2_.refs_4_, ...), custom_call_target="tpu_custom_call" | custom-call | tf_op jit(solution)/shard_map/pallas_call | solution.py:67
  136.6 3.5 %shard_map.69.refs_9_ = f32[1024,256]{1,0:T(8,128)} custom-call(s32[1]{0:T(128)} %bitcast.refs_0_, bf16[256,1536]{1,0:T(8,128)(2,1)} %bitcast.46, bf16[256,1536]{1,0:T(8,128)(2,1)} %copy-done.10, bf16[1024,512]{1,0:T(8,128)(2,1)} %copy-done, bf16[1024,512]{1,0:T(8,128)(2,1)} %collective-permute-done.1.refs_2_.refs_4_, ...), custom_call_target="tpu_custom_call" | custom-call | tf_op jit(solution)/shard_map/pallas_call | solution.py:67
  143.5 2.6 %shard_map.70 = bf16[8,32,2560]{2,1,0:T(8,128)(2,1)} custom-call(bf16[8,32,2560]{2,1,0:T(8,128)(2,1)} %copy-done.11, f32[32,1]{1,0:T(8,128)} %copy.6.refs_1_, f32[1,1280]{1,0:T(1,128)} %copy-done.22), custom_call_target="tpu_custom_call" | custom-call | tf_op jit(solution)/shard_map/pallas_call | solution.py:67
  146.1 19.9 %all_to_all.20 = bf16[8,32,2560]{2,1,0:T(8,128)(2,1)S(1)} all-to-all(bf16[8,32,2560]{2,1,0:T(8,128)(2,1)} %shard_map.70), channel_id=1, replica_groups=mesh['x'=4,'yl'=2,'c'=2,'z'=8,'yh'=2] {'x','yl'}, dimensions={0} | all-to-all | bytes 2621440 | tf_op jit(solution)/shard_map/all_to_all | solution.py:239
  166.0 2.7 %collective-permute-start.18 = (bf16[256,2560]{1,0:T(8,128)(2,1)S(1)}, bf16[256,2560]{1,0:T(8,128)(2,1)S(1)}, u32[]{:S(2)}, u32[]{:S(2)}) collective-permute-start(bf16[256,2560]{1,0:T(8,128)(2,1)S(1)} %bitcast.37), channel_id=1, source_target_pairs={{0,16},{16,0},{1,17},{17,1},{2,18},{18,2},{3,19},{19,3},{4,20},{20... | collective-permute-start | bytes 3932168 | tf_op jit(solution)/shard_map/ppermute | solution.py:22
  168.7 2.7 %collective-permute-done.18.refs_2_ = bf16[256,2560]{1,0:T(8,128)(2,1)S(1)} collective-permute-done((bf16[256,2560]{1,0:T(8,128)(2,1)S(1)}, bf16[256,2560]{1,0:T(8,128)(2,1)S(1)}, u32[]{:S(2)}, u32[]{:S(2)}) %collective-permute-start.18) | collective-permute-done | bytes 1310752 | tf_op jit(solution)/shard_map/ppermute | solution.py:22
  172.4 4.6 %shard_map.71 = bf16[1024,256]{1,0:T(8,128)(2,1)} custom-call(s32[1]{0:T(128)} %bitcast.refs_0_, bf16[256,2560]{1,0:T(8,128)(2,1)} %bitcast.38, bf16[256,2560]{1,0:T(8,128)(2,1)} %copy-done.6, bf16[1024,512]{1,0:T(8,128)(2,1)} %copy-done.5, bf16[1024,512]{1,0:T(8,128)(2,1)} %copy-done.4, bf16[1024,512]{1,0:T(8,128)(2,1)} %copy-done.3, ...), custom_call_target="tpu_custom_call" | custom-call | tf_op jit(solution)/shard_map/pallas_call | solution.py:67
  177.0 2.7 %collective-permute-start.19 = (bf16[1024,256]{1,0:T(8,128)(2,1)}, bf16[1024,256]{1,0:T(8,128)(2,1)S(1)}, u32[]{:S(2)}, u32[]{:S(2)}) collective-permute-start(bf16[1024,256]{1,0:T(8,128)(2,1)} %shard_map.71), channel_id=1, source_target_pairs={{0,1},{1,0},{2,3},{3,2},{4,5},{5,4},{6,7},{7,6},{8,9},{9,8},{10,11... | collective-permute-start | bytes 1572872 | tf_op jit(solution)/shard_map/ppermute | solution.py:22
  179.8 4.6 %shard_map.72 = bf16[1024,256]{1,0:T(8,128)(2,1)} custom-call(s32[1]{0:T(128)} %bitcast.refs_0_, bf16[256,2560]{1,0:T(8,128)(2,1)} %bitcast.39, bf16[256,2560]{1,0:T(8,128)(2,1)} %copy-done.6, bf16[1024,512]{1,0:T(8,128)(2,1)} %copy-done.5, bf16[1024,512]{1,0:T(8,128)(2,1)} %copy-done.4, bf16[1024,512]{1,0:T(8,128)(2,1)} %copy-done.3, ...), custom_call_target="tpu_custom_call" | custom-call | tf_op jit(solution)/shard_map/pallas_call | solution.py:67
  184.7 4.7 %shard_map.73 = f32[1024,256]{1,0:T(8,128)} custom-call(s32[1]{0:T(128)} %bitcast.refs_0_, bf16[256,2560]{1,0:T(8,128)(2,1)} %bitcast.40, bf16[256,2560]{1,0:T(8,128)(2,1)} %copy-done.6, bf16[1024,512]{1,0:T(8,128)(2,1)} %copy-done.5, bf16[1024,512]{1,0:T(8,128)(2,1)} %copy-done.4, bf16[1024,512]{1,0:T(8,128)(2,1)} %copy-done.3, ...), custom_call_target="tpu_custom_call" | custom-call | tf_op jit(solution)/shard_map/pallas_call | solution.py:67
  189.5 4.8 %shard_map.74 = f32[1024,256]{1,0:T(8,128)} custom-call(s32[1]{0:T(128)} %bitcast.refs_0_, bf16[256,2560]{1,0:T(8,128)(2,1)} %bitcast.41, bf16[256,2560]{1,0:T(8,128)(2,1)} %copy-done.6, bf16[1024,512]{1,0:T(8,128)(2,1)} %copy-done.5, bf16[1024,512]{1,0:T(8,128)(2,1)} %copy-done.4, bf16[1024,512]{1,0:T(8,128)(2,1)} %copy-done.3, ...), custom_call_target="tpu_custom_call" | custom-call | tf_op jit(solution)/shard_map/pallas_call | solution.py:67
  195.4 7.8 %collective-permute-done.20 = bf16[1024,256]{1,0:T(8,128)(2,1)S(1)} collective-permute-done((bf16[1024,256]{1,0:T(8,128)(2,1)}, bf16[1024,256]{1,0:T(8,128)(2,1)S(1)}, u32[]{:S(2)}, u32[]{:S(2)}) %collective-permute-start.20) | collective-permute-done | bytes 524320 | tf_op jit(solution)/shard_map/ppermute | solution.py:22
  (97 shorter events, 38.8 us)
Async XLA Ops:
  1.9 35.4 %copy-start = (bf16[1024,512]{1,0:T(8,128)(2,1)}, bf16[1024,512]{1,0:T(8,128)(2,1)S(1)}, u32[]{:S(2)}) copy-start(bf16[1024,512]{1,0:T(8,128)(2,1)S(1)} %pad_maximum_fusion.refs_1_.refs_3_) | copy-start | bytes 3145732
  1.9 29.5 %collective-permute-start = (bf16[1024,512]{1,0:T(8,128)(2,1)S(1)}, bf16[1024,512]{1,0:T(8,128)(2,1)}, u32[]{:S(2)}, u32[]{:S(2)}) collective-permute-start(bf16[1024,512]{1,0:T(8,128)(2,1)S(1)} %pad_maximum_fusion.refs_1_.refs_3_), channel_id=1, source_target_pairs={{0,2},{2,4},{4,6},{6,8},{8,10},{10,12},{12,14},{14,0},{1,3},{3,5},... | collective-permute-start | bytes 3145736 | tf_op jit(solution)/shard_map/ppermute | solution.py:18
  4.5 26.9 %collective-permute-start.1 = (bf16[1024,512]{1,0:T(8,128)(2,1)S(1)}, bf16[1024,512]{1,0:T(8,128)(2,1)}, u32[]{:S(2)}, u32[]{:S(2)}) collective-permute-start(bf16[1024,512]{1,0:T(8,128)(2,1)S(1)} %pad_maximum_fusion.refs_1_.refs_3_), channel_id=1, source_target_pairs={{0,14},{2,0},{4,2},{6,4},{8,6},{10,8},{12,10},{14,12},{1,15},{3,1}... | collective-permute-start | bytes 3145736 | tf_op jit(solution)/shard_map/ppermute | solution.py:18
  8.5 25.2 %collective-permute-start.2 = (bf16[1024,512]{1,0:T(8,128)(2,1)S(1)}, bf16[1024,512]{1,0:T(8,128)(2,1)S(1)}, u32[]{:S(2)}, u32[]{:S(2)}) collective-permute-start(bf16[1024,512]{1,0:T(8,128)(2,1)S(1)} %pad_maximum_fusion.refs_1_.refs_3_), channel_id=1, source_target_pairs={{0,1},{1,0},{2,3},{3,2},{4,5},{5,4},{6,7},{7,6},{8,9},{9,8},{10,11... | collective-permute-start | bytes 3145736 | tf_op jit(solution)/shard_map/ppermute | solution.py:22
  34.7 24.2 %collective-permute-start.3 = (bf16[1024,512]{1,0:T(8,128)(2,1)}, bf16[1024,512]{1,0:T(8,128)(2,1)S(1)}, u32[]{:S(2)}, u32[]{:S(2)}) collective-permute-start(bf16[1024,512]{1,0:T(8,128)(2,1)} %collective-permute-done.refs_3_.refs_5_), channel_id=1, source_target_pairs={{0,2},{2,4},{4,6},{6,8},{8,10},{10,12},{12,14},{14,0},{1,3},{3,5},... | collective-permute-start | bytes 3145736 | tf_op jit(solution)/shard_map/ppermute | solution.py:18
  34.7 24.2 %collective-permute-start.4 = (bf16[1024,512]{1,0:T(8,128)(2,1)}, bf16[1024,512]{1,0:T(8,128)(2,1)S(1)}, u32[]{:S(2)}, u32[]{:S(2)}) collective-permute-start(bf16[1024,512]{1,0:T(8,128)(2,1)} %collective-permute-done.1.refs_2_.refs_4_), channel_id=1, source_target_pairs={{0,14},{2,0},{4,2},{6,4},{8,6},{10,8},{12,10},{14,12},{1,15},{3,1}... | collective-permute-start | bytes 3145736 | tf_op jit(solution)/shard_map/ppermute | solution.py:18
  46.3 4.3 %collective-permute-start.5 = (f32[256,512]{1,0:T(8,128)}, f32[256,512]{1,0:T(8,128)S(1)}, u32[]{:S(2)}, u32[]{:S(2)}) collective-permute-start(f32[256,512]{1,0:T(8,128)} %get-tuple-element.35), channel_id=1, source_target_pairs={{0,16},{16,0},{1,17},{17,1},{2,18},{18,2},{3,19},{19,3},{4,20},{20... | collective-permute-start | bytes 1572872 | tf_op jit(solution)/shard_map/ppermute | solution.py:22
  48.8 2.5 %collective-permute-start.6 = (f32[256,512]{1,0:T(8,128)}, f32[256,512]{1,0:T(8,128)S(1)}, u32[]{:S(2)}, u32[]{:S(2)}) collective-permute-start(f32[256,512]{1,0:T(8,128)} %get-tuple-element.36), channel_id=1, source_target_pairs={{0,16},{16,0},{1,17},{17,1},{2,18},{18,2},{3,19},{19,3},{4,20},{20... | collective-permute-start | bytes 1572872 | tf_op jit(solution)/shard_map/ppermute | solution.py:22
  48.9 3.1 %collective-permute-start.7 = (f32[256,512]{1,0:T(8,128)}, f32[256,512]{1,0:T(8,128)S(1)}, u32[]{:S(2)}, u32[]{:S(2)}) collective-permute-start(f32[256,512]{1,0:T(8,128)} %get-tuple-element.37), channel_id=1, source_target_pairs={{0,16},{16,0},{1,17},{17,1},{2,18},{18,2},{3,19},{19,3},{4,20},{20... | collective-permute-start | bytes 1572872 | tf_op jit(solution)/shard_map/ppermute | solution.py:22
  50.5 12.0 %copy-start.15 = (f32[256,512]{1,0:T(8,128)}, f32[256,512]{1,0:T(8,128)S(1)}, u32[]{:S(2)}) copy-start(f32[256,512]{1,0:T(8,128)S(1)} %collective-permute-done.5.refs_1_) | copy-start | bytes 1572868
  51.3 11.3 %copy-start.16 = (f32[256,512]{1,0:T(8,128)}, f32[256,512]{1,0:T(8,128)S(1)}, u32[]{:S(2)}) copy-start(f32[256,512]{1,0:T(8,128)S(1)} %collective-permute-done.6.refs_2_) | copy-start | bytes 1572868
  52.0 10.5 %copy-start.17 = (f32[256,512]{1,0:T(8,128)}, f32[256,512]{1,0:T(8,128)S(1)}, u32[]{:S(2)}) copy-start(f32[256,512]{1,0:T(8,128)S(1)} %collective-permute-done.7.refs_3_) | copy-start | bytes 1572868
  59.9 23.1 %collective-permute-start.8 = (bf16[1024,512]{1,0:T(8,128)(2,1)S(1)}, bf16[1024,512]{1,0:T(8,128)(2,1)S(1)}, u32[]{:S(2)}, u32[]{:S(2)}) collective-permute-start(bf16[1024,512]{1,0:T(8,128)(2,1)S(1)} %collective-permute-done.3.refs_2_.refs_4_), channel_id=1, source_target_pairs={{0,2},{2,4},{4,6},{6,8},{8,10},{10,12},{12,14},{14,0},{1,3},{3,5},... | collective-permute-start | bytes 3145736 | tf_op jit(solution)/shard_map/ppermute | solution.py:18
  59.9 23.1 %collective-permute-start.9 = (bf16[1024,512]{1,0:T(8,128)(2,1)}, bf16[1024,512]{1,0:T(8,128)(2,1)S(1)}, u32[]{:S(2)}, u32[]{:S(2)}) collective-permute-start(bf16[1024,512]{1,0:T(8,128)(2,1)} %copy-done.5), channel_id=1, source_target_pairs={{0,14},{2,0},{4,2},{6,4},{8,6},{10,8},{12,10},{14,12},{1,15},{3,1}... | collective-permute-start | bytes 3145736 | tf_op jit(solution)/shard_map/ppermute | solution.py:18
  69.8 8.7 %collective-permute-start.10 = (f32[256,512]{1,0:T(8,128)}, f32[256,512]{1,0:T(8,128)}, u32[]{:S(2)}, u32[]{:S(2)}) collective-permute-start(f32[256,512]{1,0:T(8,128)} %get-tuple-element.47), channel_id=1, source_target_pairs={{0,16},{16,0},{1,17},{17,1},{2,18},{18,2},{3,19},{19,3},{4,20},{20... | collective-permute-start | bytes 1572872 | tf_op jit(solution)/shard_map/ppermute | solution.py:22
  73.2 5.3 %collective-permute-start.11 = (f32[256,512]{1,0:T(8,128)}, f32[256,512]{1,0:T(8,128)}, u32[]{:S(2)}, u32[]{:S(2)}) collective-permute-start(f32[256,512]{1,0:T(8,128)} %get-tuple-element.48), channel_id=1, source_target_pairs={{0,16},{16,0},{1,17},{17,1},{2,18},{18,2},{3,19},{19,3},{4,20},{20... | collective-permute-start | bytes 1572872 | tf_op jit(solution)/shard_map/ppermute | solution.py:22
  73.3 14.1 %copy-start.23 = (f32[2]{0:T(128)S(1)}, f32[2]{0:T(128)}, u32[]{:S(2)}) copy-start(f32[2]{0:T(128)} %param.6) | copy-start | bytes 28
  73.3 14.7 %copy-start.21 = (f32[4096]{0:T(1024)S(1)}, f32[4096]{0:T(1024)}, u32[]{:S(2)}) copy-start(f32[4096]{0:T(1024)} %param.7) | copy-start | bytes 49156
  73.3 17.3 %all-to-all-start = ((bf16[8,32,1536]{2,1,0:T(8,128)(2,1)}), bf16[8,32,1536]{2,1,0:T(8,128)(2,1)}, u32[]{:S(2)}, u32[]{:S(2)}) async-start(bf16[8,32,1536]{2,1,0:T(8,128)(2,1)} %bitcast.48), calls=%async_computation | async-start | bytes 1572864 | tf_op jit(solution)/shard_map/all_to_all | solution.py:230
  83.0 9.9 %copy-start.2 = (bf16[1024,512]{1,0:T(8,128)(2,1)}, bf16[1024,512]{1,0:T(8,128)(2,1)S(1)}, u32[]{:S(2)}) copy-start(bf16[1024,512]{1,0:T(8,128)(2,1)S(1)} %collective-permute-done.8.refs_2_.refs_6_) | copy-start | bytes 3145732
  83.0 9.9 %copy-start.3 = (bf16[1024,512]{1,0:T(8,128)(2,1)}, bf16[1024,512]{1,0:T(8,128)(2,1)S(1)}, u32[]{:S(2)}) copy-start(bf16[1024,512]{1,0:T(8,128)(2,1)S(1)} %collective-permute-done.9.refs_1_.refs_5_) | copy-start | bytes 3145732
  83.9 14.0 %collective-permute-start.12 = (bf16[512,512]{1,0:T(8,128)(2,1)}, bf16[512,512]{1,0:T(8,128)(2,1)S(1)}, u32[]{:S(2)}, u32[]{:S(2)}) collective-permute-start(bf16[512,512]{1,0:T(8,128)(2,1)} %slice.12), channel_id=1, source_target_pairs={{0,2},{2,4},{4,6},{6,8},{8,10},{10,12},{12,14},{14,0},{1,3},{3,5},... | collective-permute-start | bytes 1572872 | tf_op jit(solution)/shard_map/ppermute | solution.py:18
  85.6 12.3 %collective-permute-start.13 = (bf16[512,512]{1,0:T(8,128)(2,1)}, bf16[512,512]{1,0:T(8,128)(2,1)S(1)}, u32[]{:S(2)}, u32[]{:S(2)}) collective-permute-start(bf16[512,512]{1,0:T(8,128)(2,1)} %slice.13), channel_id=1, source_target_pairs={{0,14},{2,0},{4,2},{6,4},{8,6},{10,8},{12,10},{14,12},{1,15},{3,1}... | collective-permute-start | bytes 1572872 | tf_op jit(solution)/shard_map/ppermute | solution.py:18
  92.9 24.3 %all-to-all-start.1 = ((bf16[8,32,1536]{2,1,0:T(8,128)(2,1)}), bf16[8,32,1536]{2,1,0:T(8,128)(2,1)S(1)}, u32[]{:S(2)}, u32[]{:S(2)}) async-start(bf16[8,32,1536]{2,1,0:T(8,128)(2,1)} %shard_map.65), calls=%async_computation.1 | async-start | bytes 1572864 | tf_op jit(solution)/shard_map/all_to_all | solution.py:239
  104.8 6.4 %collective-permute-start.14 = (f32[256,512]{1,0:T(8,128)}, f32[256,512]{1,0:T(8,128)S(1)}, u32[]{:S(2)}, u32[]{:S(2)}) collective-permute-start(f32[256,512]{1,0:T(8,128)} %get-tuple-element.55), channel_id=1, source_target_pairs={{0,16},{16,0},{1,17},{17,1},{2,18},{18,2},{3,19},{19,3},{4,20},{20... | collective-permute-start | bytes 1572872 | tf_op jit(solution)/shard_map/ppermute | solution.py:22
  109.4 2.5 %collective-permute-start.15 = (f32[256,512]{1,0:T(8,128)}, f32[256,512]{1,0:T(8,128)S(1)}, u32[]{:S(2)}, u32[]{:S(2)}) collective-permute-start(f32[256,512]{1,0:T(8,128)} %get-tuple-element.56), channel_id=1, source_target_pairs={{0,16},{16,0},{1,17},{17,1},{2,18},{18,2},{3,19},{19,3},{4,20},{20... | collective-permute-start | bytes 1572872 | tf_op jit(solution)/shard_map/ppermute | solution.py:22
  109.5 3.1 %collective-permute-start.16 = (f32[256,512]{1,0:T(8,128)}, f32[256,512]{1,0:T(8,128)S(1)}, u32[]{:S(2)}, u32[]{:S(2)}) collective-permute-start(f32[256,512]{1,0:T(8,128)} %get-tuple-element.57), channel_id=1, source_target_pairs={{0,16},{16,0},{1,17},{17,1},{2,18},{18,2},{3,19},{19,3},{4,20},{20... | collective-permute-start | bytes 1572872 | tf_op jit(solution)/shard_map/ppermute | solution.py:22
  117.2 25.2 %all-to-all-start.2 = ((bf16[8,32,2560]{2,1,0:T(8,128)(2,1)}), bf16[8,32,2560]{2,1,0:T(8,128)(2,1)S(1)}, u32[]{:S(2)}, u32[]{:S(2)}) async-start(bf16[8,32,2560]{2,1,0:T(8,128)(2,1)} %bitcast.47), calls=%async_computation.2 | async-start | bytes 2621440 | tf_op jit(solution)/shard_map/all_to_all | solution.py:230
  122.6 2.6 %collective-permute-start.17 = (bf16[256,1536]{1,0:T(8,128)(2,1)S(1)}, bf16[256,1536]{1,0:T(8,128)(2,1)S(1)}, u32[]{:S(2)}, u32[]{:S(2)}) collective-permute-start(bf16[256,1536]{1,0:T(8,128)(2,1)S(1)} %bitcast.42), channel_id=1, source_target_pairs={{0,16},{16,0},{1,17},{17,1},{2,18},{18,2},{3,19},{19,3},{4,20},{20... | collective-permute-start | bytes 2359304 | tf_op jit(solution)/shard_map/ppermute | solution.py:22
  166.0 5.4 %collective-permute-start.18 = (bf16[256,2560]{1,0:T(8,128)(2,1)S(1)}, bf16[256,2560]{1,0:T(8,128)(2,1)S(1)}, u32[]{:S(2)}, u32[]{:S(2)}) collective-permute-start(bf16[256,2560]{1,0:T(8,128)(2,1)S(1)} %bitcast.37), channel_id=1, source_target_pairs={{0,16},{16,0},{1,17},{17,1},{2,18},{18,2},{3,19},{19,3},{4,20},{20... | collective-permute-start | bytes 3932168 | tf_op jit(solution)/shard_map/ppermute | solution.py:22
  177.0 17.3 %collective-permute-start.19 = (bf16[1024,256]{1,0:T(8,128)(2,1)}, bf16[1024,256]{1,0:T(8,128)(2,1)S(1)}, u32[]{:S(2)}, u32[]{:S(2)}) collective-permute-start(bf16[1024,256]{1,0:T(8,128)(2,1)} %shard_map.71), channel_id=1, source_target_pairs={{0,1},{1,0},{2,3},{3,2},{4,5},{5,4},{6,7},{7,6},{8,9},{9,8},{10,11... | collective-permute-start | bytes 1572872 | tf_op jit(solution)/shard_map/ppermute | solution.py:22
  184.3 18.9 %collective-permute-start.20 = (bf16[1024,256]{1,0:T(8,128)(2,1)}, bf16[1024,256]{1,0:T(8,128)(2,1)S(1)}, u32[]{:S(2)}, u32[]{:S(2)}) collective-permute-start(bf16[1024,256]{1,0:T(8,128)(2,1)} %shard_map.72), channel_id=1, source_target_pairs={{0,1},{1,0},{2,3},{3,2},{4,5},{5,4},{6,7},{7,6},{8,9},{9,8},{10,11... | collective-permute-start | bytes 1572872 | tf_op jit(solution)/shard_map/ppermute | solution.py:22
  (16 other events, 53.2 us)

commit v6 on v5

--- a/solution.py
+++ b/solution.py
@@ -259,16 +259,15 @@
     up3, down3 = both(up2, 1), both(down2, -1)
     summed_a = added([near_halves])
     pieces_a = scatter(summed_a)
-    middle_halves = halves(after([down2, up2], summed_a))
-    (up3, down3), middle_halves = lax.optimization_barrier(((up3, down3), middle_halves))
+    middle_halves = halves(after([down2, up2], pieces_a))
     far = shift(up3[0][:half], "z", NZ, 1), shift(down3[0][half:], "z", NZ, -1)
 
     distant_blocks = [down2, up2, down3, up3, far]
-    amp_a = amplitudes(near, pieces_a, CHIPS)
+    amp_a = amplitudes(near, after(pieces_a, up3, down3), CHIPS)
     mine_a = spread(amp_a)
     other_a = swap(mine_a, "c")
     last_halves = halves(distant_blocks[2:])
-    pieces_b = scatter(after(added([middle_halves, last_halves]), mine_a))
+    pieces_b = scatter(after(added([after(middle_halves, far), last_halves]), mine_a))
     sums = [[gamma(side, store, near_blocks, mine_a, other_a) for store in range(2)] for side in range(2)]
     amp_b = amplitudes(distant, after(pieces_b, sums), CHIPS)
     mine_b = spread(amp_b)

time: 205 us -> 209 us (1.020)
  waiting for transfers between devices: 53.7 us -> 63.5 us
  starting transfers between devices: 51.4 us -> 45.9 us
    ppermute x13, waiting for transfers between devices: 20 us -> 33.7 us  [swap(): return lax.ppermute(value, axis, [(0, 1), (1, 0)])]
    ppermute x8, waiting for transfers between devices: 31.3 us -> 27.5 us  [shift(): lax.ppermute(value, axis, [(i, (i + step) % size) for i in range(size)])]
    ppermute x13, starting transfers between devices: 21.1 us -> 18.5 us  [swap(): return lax.ppermute(value, axis, [(0, 1), (1, 0)])]
    unnamed x52 -> x56, local copies, waits for them, and re-layouts: 7.56 us -> 6.53 us
where the time goes in v6:
time: 209 us; the launch traced here: 208 us
  waiting for transfers between devices  63.5 us (30%)
  Pallas kernels  62.9 us (30%)
  starting transfers between devices  45.9 us (22%)
  blocking collectives  19.9 us (10%)
  local copies, waits for them, and re-layouts  9.66 us (5%)
  other arithmetic  4.09 us (2%)
  between operations  2.13 us (1%)
    pallas_call x16, Pallas kernels, call(): pl.pallas_call(body, out_shape=out_shape, in_specs=specs, out_specs=out_s...  62.9 us
    ppermute x13, waiting for transfers between devices, swap(): return lax.ppermute(value, axis, [(0, 1), (1, 0)])  33.7 us
    ppermute x8, waiting for transfers between devices, shift(): lax.ppermute(value, axis, [(i, (i + step) % size) for i in range(size)])  27.5 us
    all_to_all x1, blocking collectives, spread(): lax.all_to_all(copies, ('x', 'yl'), 0, 0, tiled=True).reshape(width, -1)  19.9 us
    ppermute x13, starting transfers between devices, swap(): return lax.ppermute(value, axis, [(0, 1), (1, 0)])  18.5 us
    ppermute x8, starting transfers between devices, shift(): lax.ppermute(value, axis, [(i, (i + step) % size) for i in range(size)])  13.6 us
    all_to_all x2, starting transfers between devices, scatter(): lax.all_to_all(summed.reshape(CHIPS, rows, -1), ('x', 'yl'), 0, 0, tiled=...  9.66 us
    unnamed x56, local copies, waits for them, and re-layouts  6.53 us
  transfers between devices with their start and end apart: 24, of which 14 were waited for; matrix products, arithmetic and copies ran while one was open for 2% of the time, Pallas kernels for 27%

profile of v6, /device:TPU:1, one launch (start us, length us, event | category | flops | bytes accessed | tf_op | source)
XLA Modules:
  0.0 208.1 jit_solution(14932021387092296295)
XLA Ops:
  1.9 3.8 %collective-permute-start = (bf16[1024,512]{1,0:T(8,128)(2,1)S(1)}, bf16[1024,512]{1,0:T(8,128)(2,1)S(1)}, u32[]{:S(2)}, u32[]{:S(2)}) collective-permute-start(bf16[1024,512]{1,0:T(8,128)(2,1)S(1)} %pad_maximum_fusion.refs_1_.refs_3_), channel_id=1, source_target_pairs={{0,1},{1,0},{2,3},{3,2},{4,5},{5,4},{6,7},{7,6},{8,9},{9,8},{10,11... | collective-permute-start | bytes 3145736 | tf_op jit(solution)/shard_map/ppermute | solution.py:22
  7.4 3.9 %collective-permute-start.2 = (bf16[1024,512]{1,0:T(8,128)(2,1)S(1)}, bf16[1024,512]{1,0:T(8,128)(2,1)}, u32[]{:S(2)}, u32[]{:S(2)}) collective-permute-start(bf16[1024,512]{1,0:T(8,128)(2,1)S(1)} %pad_maximum_fusion.refs_1_.refs_3_), channel_id=1, source_target_pairs={{0,14},{2,0},{4,2},{6,4},{8,6},{10,8},{12,10},{14,12},{1,15},{3,1}... | collective-permute-start | bytes 3145736 | tf_op jit(solution)/shard_map/ppermute | solution.py:18
  11.3 16.2 %collective-permute-done.refs_2_ = bf16[1024,512]{1,0:T(8,128)(2,1)S(1)} collective-permute-done((bf16[1024,512]{1,0:T(8,128)(2,1)S(1)}, bf16[1024,512]{1,0:T(8,128)(2,1)S(1)}, u32[]{:S(2)}, u32[]{:S(2)}) %collective-permute-start) | collective-permute-done | bytes 1048608 | tf_op jit(solution)/shard_map/ppermute | solution.py:22
  27.6 6.4 %collective-permute-done.1.refs_3_.refs_5_ = bf16[1024,512]{1,0:T(8,128)(2,1)} collective-permute-done((bf16[1024,512]{1,0:T(8,128)(2,1)S(1)}, bf16[1024,512]{1,0:T(8,128)(2,1)}, u32[]{:S(2)}, u32[]{:S(2)}) %collective-permute-start.1) | collective-permute-done | bytes 1048608 | tf_op jit(solution)/shard_map/ppermute | solution.py:18
  34.0 2.7 %collective-permute-start.4 = (bf16[1024,512]{1,0:T(8,128)(2,1)}, bf16[1024,512]{1,0:T(8,128)(2,1)S(1)}, u32[]{:S(2)}, u32[]{:S(2)}) collective-permute-start(bf16[1024,512]{1,0:T(8,128)(2,1)} %collective-permute-done.2.refs_2_.refs_4_), channel_id=1, source_target_pairs={{0,14},{2,0},{4,2},{6,4},{8,6},{10,8},{12,10},{14,12},{1,15},{3,1}... | collective-permute-start | bytes 3145736 | tf_op jit(solution)/shard_map/ppermute | solution.py:18
  36.7 3.6 %shard_map.59.refs_0_ = bf16[1024,1024]{1,0:T(8,128)(2,1)} custom-call(s32[1]{0:T(128)} %bitcast.refs_0_, bf16[1024,512]{1,0:T(8,128)(2,1)} %copy-done, bf16[1024,512]{1,0:T(8,128)(2,1)} %copy-done.14), custom_call_target="tpu_custom_call" | custom-call | tf_op jit(solution)/shard_map/pallas_call | solution.py:67
  40.3 5.3 %shard_map.60 = (f32[256,1536]{1,0:T(8,128)}, f32[256,512]{1,0:T(8,128)}, f32[256,512]{1,0:T(8,128)}, f32[256,512]{1,0:T(8,128)}) custom-call(bf16[1024,1024]{1,0:T(8,128)(2,1)} %shard_map.59.refs_0_, bf16[1024,512]{1,0:T(8,128)(2,1)} %copy-done, bf16[1024,512]{1,0:T(8,128)(2,1)} %collective-permute-done.2.refs_2_.refs_4_, ...), custom_call_target="tpu_custom_call" | custom-call | tf_op jit(solution)/shard_map/pallas_call | solution.py:67
  51.1 7.5 %collective-permute-done.3.refs_2_.refs_4_ = bf16[1024,512]{1,0:T(8,128)(2,1)S(1)} collective-permute-done((bf16[1024,512]{1,0:T(8,128)(2,1)}, bf16[1024,512]{1,0:T(8,128)(2,1)S(1)}, u32[]{:S(2)}, u32[]{:S(2)}) %collective-permute-start.3) | collective-permute-done | bytes 1048608 | tf_op jit(solution)/shard_map/ppermute | solution.py:18
  62.2 2.8 %shard_map.61 = bf16[256,1536]{1,0:T(8,128)(2,1)} custom-call(f32[256,1536]{1,0:T(8,128)} %get-tuple-element.39.refs_0_, f32[256,512]{1,0:T(8,128)} %copy-done.17, f32[256,512]{1,0:T(8,128)} %copy-done.19, f32[256,512]{1,0:T(8,128)} %copy-done.21), custom_call_target="tpu_custom_call" | custom-call | tf_op jit(solution)/shard_map/pallas_call | solution.py:67
  65.1 4.2 %all-to-all-start = ((bf16[8,32,1536]{2,1,0:T(8,128)(2,1)}), bf16[8,32,1536]{2,1,0:T(8,128)(2,1)}, u32[]{:S(2)}, u32[]{:S(2)}) async-start(bf16[8,32,1536]{2,1,0:T(8,128)(2,1)} %bitcast.48), calls=%async_computation | async-start | bytes 1572864 | tf_op jit(solution)/shard_map/all_to_all | solution.py:230
  69.3 13.6 %collective-permute-done.10.refs_2_.refs_6_ = bf16[1024,512]{1,0:T(8,128)(2,1)S(1)} collective-permute-done((bf16[1024,512]{1,0:T(8,128)(2,1)S(1)}, bf16[1024,512]{1,0:T(8,128)(2,1)S(1)}, u32[]{:S(2)}, u32[]{:S(2)}) %collective-permute-start.10) | collective-permute-done | bytes 1048608 | tf_op jit(solution)/shard_map/ppermute | solution.py:18
  84.8 2.7 %collective-permute-start.13 = (bf16[512,512]{1,0:T(8,128)(2,1)}, bf16[512,512]{1,0:T(8,128)(2,1)S(1)}, u32[]{:S(2)}, u32[]{:S(2)}) collective-permute-start(bf16[512,512]{1,0:T(8,128)(2,1)} %slice.17), channel_id=1, source_target_pairs={{0,14},{2,0},{4,2},{6,4},{8,6},{10,8},{12,10},{14,12},{1,15},{3,1}... | collective-permute-start | bytes 1572872 | tf_op jit(solution)/shard_map/ppermute | solution.py:18
  92.8 4.1 %all-to-all-start.1 = ((bf16[8,32,1536]{2,1,0:T(8,128)(2,1)}), bf16[8,32,1536]{2,1,0:T(8,128)(2,1)S(1)}, u32[]{:S(2)}, u32[]{:S(2)}) async-start(bf16[8,32,1536]{2,1,0:T(8,128)(2,1)} %shard_map.65), calls=%async_computation.1 | async-start | bytes 1572864 | tf_op jit(solution)/shard_map/all_to_all | solution.py:239
  97.0 4.4 %shard_map.62 = (f32[256,1024]{1,0:T(8,128)}, f32[256,512]{1,0:T(8,128)}, f32[256,512]{1,0:T(8,128)}) custom-call(bf16[1024,1024]{1,0:T(8,128)(2,1)} %shard_map.59.refs_0_, bf16[1024,512]{1,0:T(8,128)(2,1)} %copy-done.5, bf16[1024,512]{1,0:T(8,128)(2,1)} %copy-done.4), custom_call_target="tpu_custom_call" | custom-call | tf_op jit(solution)/shard_map/pallas_call | solution.py:67
  101.4 4.3 %collective-permute-start.8 = (f32[256,512]{1,0:T(8,128)}, f32[256,512]{1,0:T(8,128)S(1)}, u32[]{:S(2)}, u32[]{:S(2)}) collective-permute-start(f32[256,512]{1,0:T(8,128)} %get-tuple-element.46), channel_id=1, source_target_pairs={{0,16},{16,0},{1,17},{17,1},{2,18},{18,2},{3,19},{19,3},{4,20},{20... | collective-permute-start | bytes 1572872 | tf_op jit(solution)/shard_map/ppermute | solution.py:22
  107.4 5.3 %shard_map.63 = (f32[256,1536]{1,0:T(8,128)}, f32[256,512]{1,0:T(8,128)}, f32[256,512]{1,0:T(8,128)}, f32[256,512]{1,0:T(8,128)}) custom-call(bf16[1024,1024]{1,0:T(8,128)(2,1)} %shard_map.59.refs_0_, bf16[1024,512]{1,0:T(8,128)(2,1)} %copy-done.3, bf16[1024,512]{1,0:T(8,128)(2,1)} %copy-done.2, bf16[512,512]{1,0:T(8,128)(2,1)} %copy-done.8, ...), custom_call_target="tpu_custom_call" | custom-call | tf_op jit(solution)/shard_map/pallas_call | solution.py:67
  117.3 3.6 %shard_map.64 = bf16[256,2560]{1,0:T(8,128)(2,1)} custom-call(f32[256,1024]{1,0:T(8,128)} %get-tuple-element.48.refs_0_, f32[256,512]{1,0:T(8,128)} %copy-done.15, f32[256,512]{1,0:T(8,128)} %copy-done.16, f32[256,1536]{1,0:T(8,128)} %get-tuple-element.51.refs_3_, f32[256,512]{1,0:T(8,128)} %copy-done.18, f32[256,512]{1,0:T(8,128)} %copy-done.20, ...), custom_call_target="tpu_custom_call" | custom-call | tf_op jit(solution)/shard_map/pallas_call | solution.py:67
  120.9 5.4 %all-to-all-start.2 = ((bf16[8,32,2560]{2,1,0:T(8,128)(2,1)}), bf16[8,32,2560]{2,1,0:T(8,128)(2,1)S(1)}, u32[]{:S(2)}, u32[]{:S(2)}) async-start(bf16[8,32,2560]{2,1,0:T(8,128)(2,1)} %bitcast.47), calls=%async_computation.2 | async-start | bytes 2621440 | tf_op jit(solution)/shard_map/all_to_all | solution.py:230
  129.8 3.5 %shard_map.66.refs_9_ = f32[1024,256]{1,0:T(8,128)} custom-call(s32[1]{0:T(128)} %bitcast.refs_0_, bf16[256,1536]{1,0:T(8,128)(2,1)} %bitcast.43, bf16[256,1536]{1,0:T(8,128)(2,1)} %copy-done.10, bf16[1024,512]{1,0:T(8,128)(2,1)} %copy-done, bf16[1024,512]{1,0:T(8,128)(2,1)} %collective-permute-done.2.refs_2_.refs_4_, ...), custom_call_target="tpu_custom_call" | custom-call | tf_op jit(solution)/shard_map/pallas_call | solution.py:67
  133.4 3.4 %shard_map.67.refs_9_ = f32[1024,256]{1,0:T(8,128)} custom-call(s32[1]{0:T(128)} %bitcast.refs_0_, bf16[256,1536]{1,0:T(8,128)(2,1)} %bitcast.44, bf16[256,1536]{1,0:T(8,128)(2,1)} %copy-done.10, bf16[1024,512]{1,0:T(8,128)(2,1)} %copy-done, bf16[1024,512]{1,0:T(8,128)(2,1)} %collective-permute-done.2.refs_2_.refs_4_, ...), custom_call_target="tpu_custom_call" | custom-call | tf_op jit(solution)/shard_map/pallas_call | solution.py:67
  136.8 3.5 %shard_map.68.refs_9_ = f32[1024,256]{1,0:T(8,128)} custom-call(s32[1]{0:T(128)} %bitcast.refs_0_, bf16[256,1536]{1,0:T(8,128)(2,1)} %bitcast.45, bf16[256,1536]{1,0:T(8,128)(2,1)} %copy-done.10, bf16[1024,512]{1,0:T(8,128)(2,1)} %copy-done, bf16[1024,512]{1,0:T(8,128)(2,1)} %collective-permute-done.2.refs_2_.refs_4_, ...), custom_call_target="tpu_custom_call" | custom-call | tf_op jit(solution)/shard_map/pallas_call | solution.py:67
  140.3 3.5 %shard_map.69.refs_9_ = f32[1024,256]{1,0:T(8,128)} custom-call(s32[1]{0:T(128)} %bitcast.refs_0_, bf16[256,1536]{1,0:T(8,128)(2,1)} %bitcast.46, bf16[256,1536]{1,0:T(8,128)(2,1)} %copy-done.10, bf16[1024,512]{1,0:T(8,128)(2,1)} %copy-done, bf16[1024,512]{1,0:T(8,128)(2,1)} %collective-permute-done.2.refs_2_.refs_4_, ...), custom_call_target="tpu_custom_call" | custom-call | tf_op jit(solution)/shard_map/pallas_call | solution.py:67
  143.8 2.3 %all-to-all-done.2.refs_0_ = bf16[8,32,2560]{2,1,0:T(8,128)(2,1)S(1)} async-done(((bf16[8,32,2560]{2,1,0:T(8,128)(2,1)}), bf16[8,32,2560]{2,1,0:T(8,128)(2,1)S(1)}, u32[]{:S(2)}, u32[]{:S(2)}) %all-to-all-start.2) | async-done | bytes 1310752 | tf_op jit(solution)/shard_map/all_to_all | solution.py:230
  147.2 2.6 %shard_map.70 = bf16[8,32,2560]{2,1,0:T(8,128)(2,1)} custom-call(bf16[8,32,2560]{2,1,0:T(8,128)(2,1)} %copy-done.11, f32[32,1]{1,0:T(8,128)} %copy.6.refs_1_, f32[1,1280]{1,0:T(1,128)} %copy-done.24), custom_call_target="tpu_custom_call" | custom-call | tf_op jit(solution)/shard_map/pallas_call | solution.py:67
  149.8 19.9 %all_to_all.20 = bf16[8,32,2560]{2,1,0:T(8,128)(2,1)S(1)} all-to-all(bf16[8,32,2560]{2,1,0:T(8,128)(2,1)} %shard_map.70), channel_id=1, replica_groups=mesh['x'=4,'yl'=2,'c'=2,'z'=8,'yh'=2] {'x','yl'}, dimensions={0} | all-to-all | bytes 2621440 | tf_op jit(solution)/shard_map/all_to_all | solution.py:239
  169.7 2.7 %collective-permute-start.18 = (bf16[256,2560]{1,0:T(8,128)(2,1)S(1)}, bf16[256,2560]{1,0:T(8,128)(2,1)S(1)}, u32[]{:S(2)}, u32[]{:S(2)}) collective-permute-start(bf16[256,2560]{1,0:T(8,128)(2,1)S(1)} %bitcast.37), channel_id=1, source_target_pairs={{0,16},{16,0},{1,17},{17,1},{2,18},{18,2},{3,19},{19,3},{4,20},{20... | collective-permute-start | bytes 3932168 | tf_op jit(solution)/shard_map/ppermute | solution.py:22
  172.4 2.7 %collective-permute-done.18.refs_2_ = bf16[256,2560]{1,0:T(8,128)(2,1)S(1)} collective-permute-done((bf16[256,2560]{1,0:T(8,128)(2,1)S(1)}, bf16[256,2560]{1,0:T(8,128)(2,1)S(1)}, u32[]{:S(2)}, u32[]{:S(2)}) %collective-permute-start.18) | collective-permute-done | bytes 1310752 | tf_op jit(solution)/shard_map/ppermute | solution.py:22
  176.1 4.7 %shard_map.71 = bf16[1024,256]{1,0:T(8,128)(2,1)} custom-call(s32[1]{0:T(128)} %bitcast.refs_0_, bf16[256,2560]{1,0:T(8,128)(2,1)} %bitcast.38, bf16[256,2560]{1,0:T(8,128)(2,1)} %copy-done.6, bf16[1024,512]{1,0:T(8,128)(2,1)} %copy-done.5, bf16[1024,512]{1,0:T(8,128)(2,1)} %copy-done.4, bf16[1024,512]{1,0:T(8,128)(2,1)} %copy-done.3, ...), custom_call_target="tpu_custom_call" | custom-call | tf_op jit(solution)/shard_map/pallas_call | solution.py:67
  182.9 4.5 %shard_map.72 = bf16[1024,256]{1,0:T(8,128)(2,1)} custom-call(s32[1]{0:T(128)} %bitcast.refs_0_, bf16[256,2560]{1,0:T(8,128)(2,1)} %bitcast.39, bf16[256,2560]{1,0:T(8,128)(2,1)} %copy-done.6, bf16[1024,512]{1,0:T(8,128)(2,1)} %copy-done.5, bf16[1024,512]{1,0:T(8,128)(2,1)} %copy-done.4, bf16[1024,512]{1,0:T(8,128)(2,1)} %copy-done.3, ...), custom_call_target="tpu_custom_call" | custom-call | tf_op jit(solution)/shard_map/pallas_call | solution.py:67
  188.5 4.9 %shard_map.73 = f32[1024,256]{1,0:T(8,128)} custom-call(s32[1]{0:T(128)} %bitcast.refs_0_, bf16[256,2560]{1,0:T(8,128)(2,1)} %bitcast.40, bf16[256,2560]{1,0:T(8,128)(2,1)} %copy-done.6, bf16[1024,512]{1,0:T(8,128)(2,1)} %copy-done.5, bf16[1024,512]{1,0:T(8,128)(2,1)} %copy-done.4, bf16[1024,512]{1,0:T(8,128)(2,1)} %copy-done.3, ...), custom_call_target="tpu_custom_call" | custom-call | tf_op jit(solution)/shard_map/pallas_call | solution.py:67
  193.5 4.9 %shard_map.74 = f32[1024,256]{1,0:T(8,128)} custom-call(s32[1]{0:T(128)} %bitcast.refs_0_, bf16[256,2560]{1,0:T(8,128)(2,1)} %bitcast.41, bf16[256,2560]{1,0:T(8,128)(2,1)} %copy-done.6, bf16[1024,512]{1,0:T(8,128)(2,1)} %copy-done.5, bf16[1024,512]{1,0:T(8,128)(2,1)} %copy-done.4, bf16[1024,512]{1,0:T(8,128)(2,1)} %copy-done.3, ...), custom_call_target="tpu_custom_call" | custom-call | tf_op jit(solution)/shard_map/pallas_call | solution.py:67
  199.5 7.5 %collective-permute-done.20 = bf16[1024,256]{1,0:T(8,128)(2,1)S(1)} collective-permute-done((bf16[1024,256]{1,0:T(8,128)(2,1)}, bf16[1024,256]{1,0:T(8,128)(2,1)S(1)}, u32[]{:S(2)}, u32[]{:S(2)}) %collective-permute-start.20) | collective-permute-done | bytes 524320 | tf_op jit(solution)/shard_map/ppermute | solution.py:22
  (101 shorter events, 35.2 us)
Async XLA Ops:
  1.9 34.8 %copy-start = (bf16[1024,512]{1,0:T(8,128)(2,1)}, bf16[1024,512]{1,0:T(8,128)(2,1)S(1)}, u32[]{:S(2)}) copy-start(bf16[1024,512]{1,0:T(8,128)(2,1)S(1)} %pad_maximum_fusion.refs_1_.refs_3_) | copy-start | bytes 3145732
  1.9 25.7 %collective-permute-start = (bf16[1024,512]{1,0:T(8,128)(2,1)S(1)}, bf16[1024,512]{1,0:T(8,128)(2,1)S(1)}, u32[]{:S(2)}, u32[]{:S(2)}) collective-permute-start(bf16[1024,512]{1,0:T(8,128)(2,1)S(1)} %pad_maximum_fusion.refs_1_.refs_3_), channel_id=1, source_target_pairs={{0,1},{1,0},{2,3},{3,2},{4,5},{5,4},{6,7},{7,6},{8,9},{9,8},{10,11... | collective-permute-start | bytes 3145736 | tf_op jit(solution)/shard_map/ppermute | solution.py:22
  5.8 28.2 %collective-permute-start.1 = (bf16[1024,512]{1,0:T(8,128)(2,1)S(1)}, bf16[1024,512]{1,0:T(8,128)(2,1)}, u32[]{:S(2)}, u32[]{:S(2)}) collective-permute-start(bf16[1024,512]{1,0:T(8,128)(2,1)S(1)} %pad_maximum_fusion.refs_1_.refs_3_), channel_id=1, source_target_pairs={{0,2},{2,4},{4,6},{6,8},{8,10},{10,12},{12,14},{14,0},{1,3},{3,5},... | collective-permute-start | bytes 3145736 | tf_op jit(solution)/shard_map/ppermute | solution.py:18
  7.4 26.6 %collective-permute-start.2 = (bf16[1024,512]{1,0:T(8,128)(2,1)S(1)}, bf16[1024,512]{1,0:T(8,128)(2,1)}, u32[]{:S(2)}, u32[]{:S(2)}) collective-permute-start(bf16[1024,512]{1,0:T(8,128)(2,1)S(1)} %pad_maximum_fusion.refs_1_.refs_3_), channel_id=1, source_target_pairs={{0,14},{2,0},{4,2},{6,4},{8,6},{10,8},{12,10},{14,12},{1,15},{3,1}... | collective-permute-start | bytes 3145736 | tf_op jit(solution)/shard_map/ppermute | solution.py:18
  34.0 24.5 %collective-permute-start.3 = (bf16[1024,512]{1,0:T(8,128)(2,1)}, bf16[1024,512]{1,0:T(8,128)(2,1)S(1)}, u32[]{:S(2)}, u32[]{:S(2)}) collective-permute-start(bf16[1024,512]{1,0:T(8,128)(2,1)} %collective-permute-done.1.refs_3_.refs_5_), channel_id=1, source_target_pairs={{0,2},{2,4},{4,6},{6,8},{8,10},{10,12},{12,14},{14,0},{1,3},{3,5},... | collective-permute-start | bytes 3145736 | tf_op jit(solution)/shard_map/ppermute | solution.py:18
  34.0 24.5 %collective-permute-start.4 = (bf16[1024,512]{1,0:T(8,128)(2,1)}, bf16[1024,512]{1,0:T(8,128)(2,1)S(1)}, u32[]{:S(2)}, u32[]{:S(2)}) collective-permute-start(bf16[1024,512]{1,0:T(8,128)(2,1)} %collective-permute-done.2.refs_2_.refs_4_), channel_id=1, source_target_pairs={{0,14},{2,0},{4,2},{6,4},{8,6},{10,8},{12,10},{14,12},{1,15},{3,1}... | collective-permute-start | bytes 3145736 | tf_op jit(solution)/shard_map/ppermute | solution.py:18
  45.6 3.9 %collective-permute-start.5 = (f32[256,512]{1,0:T(8,128)}, f32[256,512]{1,0:T(8,128)S(1)}, u32[]{:S(2)}, u32[]{:S(2)}) collective-permute-start(f32[256,512]{1,0:T(8,128)} %get-tuple-element.34), channel_id=1, source_target_pairs={{0,16},{16,0},{1,17},{17,1},{2,18},{18,2},{3,19},{19,3},{4,20},{20... | collective-permute-start | bytes 1572872 | tf_op jit(solution)/shard_map/ppermute | solution.py:22
  47.8 2.5 %collective-permute-start.6 = (f32[256,512]{1,0:T(8,128)}, f32[256,512]{1,0:T(8,128)S(1)}, u32[]{:S(2)}, u32[]{:S(2)}) collective-permute-start(f32[256,512]{1,0:T(8,128)} %get-tuple-element.35), channel_id=1, source_target_pairs={{0,16},{16,0},{1,17},{17,1},{2,18},{18,2},{3,19},{19,3},{4,20},{20... | collective-permute-start | bytes 1572872 | tf_op jit(solution)/shard_map/ppermute | solution.py:22
  47.9 3.1 %collective-permute-start.7 = (f32[256,512]{1,0:T(8,128)}, f32[256,512]{1,0:T(8,128)S(1)}, u32[]{:S(2)}, u32[]{:S(2)}) collective-permute-start(f32[256,512]{1,0:T(8,128)} %get-tuple-element.36), channel_id=1, source_target_pairs={{0,16},{16,0},{1,17},{17,1},{2,18},{18,2},{3,19},{19,3},{4,20},{20... | collective-permute-start | bytes 1572872 | tf_op jit(solution)/shard_map/ppermute | solution.py:22
  49.6 12.6 %copy-start.17 = (f32[256,512]{1,0:T(8,128)}, f32[256,512]{1,0:T(8,128)S(1)}, u32[]{:S(2)}) copy-start(f32[256,512]{1,0:T(8,128)S(1)} %collective-permute-done.5.refs_1_) | copy-start | bytes 1572868
  50.3 11.9 %copy-start.19 = (f32[256,512]{1,0:T(8,128)}, f32[256,512]{1,0:T(8,128)S(1)}, u32[]{:S(2)}) copy-start(f32[256,512]{1,0:T(8,128)S(1)} %collective-permute-done.6.refs_2_) | copy-start | bytes 1572868
  51.1 11.1 %copy-start.21 = (f32[256,512]{1,0:T(8,128)}, f32[256,512]{1,0:T(8,128)S(1)}, u32[]{:S(2)}) copy-start(f32[256,512]{1,0:T(8,128)S(1)} %collective-permute-done.7.refs_3_) | copy-start | bytes 1572868
  59.5 23.4 %collective-permute-start.10 = (bf16[1024,512]{1,0:T(8,128)(2,1)S(1)}, bf16[1024,512]{1,0:T(8,128)(2,1)S(1)}, u32[]{:S(2)}, u32[]{:S(2)}) collective-permute-start(bf16[1024,512]{1,0:T(8,128)(2,1)S(1)} %collective-permute-done.3.refs_2_.refs_4_), channel_id=1, source_target_pairs={{0,2},{2,4},{4,6},{6,8},{8,10},{10,12},{12,14},{14,0},{1,3},{3,5},... | collective-permute-start | bytes 3145736 | tf_op jit(solution)/shard_map/ppermute | solution.py:18
  60.5 23.4 %collective-permute-start.12 = (bf16[1024,512]{1,0:T(8,128)(2,1)}, bf16[1024,512]{1,0:T(8,128)(2,1)S(1)}, u32[]{:S(2)}, u32[]{:S(2)}) collective-permute-start(bf16[1024,512]{1,0:T(8,128)(2,1)} %copy-done.5), channel_id=1, source_target_pairs={{0,14},{2,0},{4,2},{6,4},{8,6},{10,8},{12,10},{14,12},{1,15},{3,1}... | collective-permute-start | bytes 3145736 | tf_op jit(solution)/shard_map/ppermute | solution.py:18
  65.0 22.4 %copy-start.25 = (f32[2]{0:T(128)S(1)}, f32[2]{0:T(128)}, u32[]{:S(2)}) copy-start(f32[2]{0:T(128)} %param.6) | copy-start | bytes 28
  65.1 23.0 %copy-start.23 = (f32[4096]{0:T(1024)S(1)}, f32[4096]{0:T(1024)}, u32[]{:S(2)}) copy-start(f32[4096]{0:T(1024)} %param.7) | copy-start | bytes 49156
  65.1 25.5 %all-to-all-start = ((bf16[8,32,1536]{2,1,0:T(8,128)(2,1)}), bf16[8,32,1536]{2,1,0:T(8,128)(2,1)}, u32[]{:S(2)}, u32[]{:S(2)}) async-start(bf16[8,32,1536]{2,1,0:T(8,128)(2,1)} %bitcast.48), calls=%async_computation | async-start | bytes 1572864 | tf_op jit(solution)/shard_map/all_to_all | solution.py:230
  82.9 9.9 %copy-start.2 = (bf16[1024,512]{1,0:T(8,128)(2,1)}, bf16[1024,512]{1,0:T(8,128)(2,1)S(1)}, u32[]{:S(2)}) copy-start(bf16[1024,512]{1,0:T(8,128)(2,1)S(1)} %collective-permute-done.10.refs_2_.refs_6_) | copy-start | bytes 3145732
  83.8 21.9 %collective-permute-start.11 = (bf16[512,512]{1,0:T(8,128)(2,1)}, bf16[512,512]{1,0:T(8,128)(2,1)S(1)}, u32[]{:S(2)}, u32[]{:S(2)}) collective-permute-start(bf16[512,512]{1,0:T(8,128)(2,1)} %slice.16), channel_id=1, source_target_pairs={{0,2},{2,4},{4,6},{6,8},{8,10},{10,12},{12,14},{14,0},{1,3},{3,5},... | collective-permute-start | bytes 1572872 | tf_op jit(solution)/shard_map/ppermute | solution.py:18
  84.8 21.0 %collective-permute-start.13 = (bf16[512,512]{1,0:T(8,128)(2,1)}, bf16[512,512]{1,0:T(8,128)(2,1)S(1)}, u32[]{:S(2)}, u32[]{:S(2)}) collective-permute-start(bf16[512,512]{1,0:T(8,128)(2,1)} %slice.17), channel_id=1, source_target_pairs={{0,14},{2,0},{4,2},{6,4},{8,6},{10,8},{12,10},{14,12},{1,15},{3,1}... | collective-permute-start | bytes 1572872 | tf_op jit(solution)/shard_map/ppermute | solution.py:18
  92.8 28.1 %all-to-all-start.1 = ((bf16[8,32,1536]{2,1,0:T(8,128)(2,1)}), bf16[8,32,1536]{2,1,0:T(8,128)(2,1)S(1)}, u32[]{:S(2)}, u32[]{:S(2)}) async-start(bf16[8,32,1536]{2,1,0:T(8,128)(2,1)} %shard_map.65), calls=%async_computation.1 | async-start | bytes 1572864 | tf_op jit(solution)/shard_map/all_to_all | solution.py:239
  101.4 12.4 %collective-permute-start.8 = (f32[256,512]{1,0:T(8,128)}, f32[256,512]{1,0:T(8,128)S(1)}, u32[]{:S(2)}, u32[]{:S(2)}) collective-permute-start(f32[256,512]{1,0:T(8,128)} %get-tuple-element.46), channel_id=1, source_target_pairs={{0,16},{16,0},{1,17},{17,1},{2,18},{18,2},{3,19},{19,3},{4,20},{20... | collective-permute-start | bytes 1572872 | tf_op jit(solution)/shard_map/ppermute | solution.py:22
  105.7 8.1 %collective-permute-start.9 = (f32[256,512]{1,0:T(8,128)}, f32[256,512]{1,0:T(8,128)S(1)}, u32[]{:S(2)}, u32[]{:S(2)}) collective-permute-start(f32[256,512]{1,0:T(8,128)} %get-tuple-element.47), channel_id=1, source_target_pairs={{0,16},{16,0},{1,17},{17,1},{2,18},{18,2},{3,19},{19,3},{4,20},{20... | collective-permute-start | bytes 1572872 | tf_op jit(solution)/shard_map/ppermute | solution.py:22
  112.7 2.2 %collective-permute-start.14 = (f32[256,512]{1,0:T(8,128)}, f32[256,512]{1,0:T(8,128)S(1)}, u32[]{:S(2)}, u32[]{:S(2)}) collective-permute-start(f32[256,512]{1,0:T(8,128)} %get-tuple-element.52), channel_id=1, source_target_pairs={{0,16},{16,0},{1,17},{17,1},{2,18},{18,2},{3,19},{19,3},{4,20},{20... | collective-permute-start | bytes 1572872 | tf_op jit(solution)/shard_map/ppermute | solution.py:22
  113.2 2.5 %collective-permute-start.15 = (f32[256,512]{1,0:T(8,128)}, f32[256,512]{1,0:T(8,128)S(1)}, u32[]{:S(2)}, u32[]{:S(2)}) collective-permute-start(f32[256,512]{1,0:T(8,128)} %get-tuple-element.53), channel_id=1, source_target_pairs={{0,16},{16,0},{1,17},{17,1},{2,18},{18,2},{3,19},{19,3},{4,20},{20... | collective-permute-start | bytes 1572872 | tf_op jit(solution)/shard_map/ppermute | solution.py:22
  113.3 3.1 %collective-permute-start.16 = (f32[256,512]{1,0:T(8,128)}, f32[256,512]{1,0:T(8,128)S(1)}, u32[]{:S(2)}, u32[]{:S(2)}) collective-permute-start(f32[256,512]{1,0:T(8,128)} %get-tuple-element.54), channel_id=1, source_target_pairs={{0,16},{16,0},{1,17},{17,1},{2,18},{18,2},{3,19},{19,3},{4,20},{20... | collective-permute-start | bytes 1572872 | tf_op jit(solution)/shard_map/ppermute | solution.py:22
  120.9 25.2 %all-to-all-start.2 = ((bf16[8,32,2560]{2,1,0:T(8,128)(2,1)}), bf16[8,32,2560]{2,1,0:T(8,128)(2,1)S(1)}, u32[]{:S(2)}, u32[]{:S(2)}) async-start(bf16[8,32,2560]{2,1,0:T(8,128)(2,1)} %bitcast.47), calls=%async_computation.2 | async-start | bytes 2621440 | tf_op jit(solution)/shard_map/all_to_all | solution.py:230
  126.4 2.6 %collective-permute-start.17 = (bf16[256,1536]{1,0:T(8,128)(2,1)S(1)}, bf16[256,1536]{1,0:T(8,128)(2,1)S(1)}, u32[]{:S(2)}, u32[]{:S(2)}) collective-permute-start(bf16[256,1536]{1,0:T(8,128)(2,1)S(1)} %bitcast.42), channel_id=1, source_target_pairs={{0,16},{16,0},{1,17},{17,1},{2,18},{18,2},{3,19},{19,3},{4,20},{20... | collective-permute-start | bytes 2359304 | tf_op jit(solution)/shard_map/ppermute | solution.py:22
  127.1 9.7 %copy-start.24 = (f32[1,1280]{1,0:T(1,128)}, f32[1,1280]{1,0:T(1,128)S(1)}, u32[]{:S(2)}) copy-start(f32[1,1280]{1,0:T(1,128)S(1)} %constant_dynamic-update-slice_fusion.refs_2_) | copy-start | bytes 15364
  169.7 5.4 %collective-permute-start.18 = (bf16[256,2560]{1,0:T(8,128)(2,1)S(1)}, bf16[256,2560]{1,0:T(8,128)(2,1)S(1)}, u32[]{:S(2)}, u32[]{:S(2)}) collective-permute-start(bf16[256,2560]{1,0:T(8,128)(2,1)S(1)} %bitcast.37), channel_id=1, source_target_pairs={{0,16},{16,0},{1,17},{17,1},{2,18},{18,2},{3,19},{19,3},{4,20},{20... | collective-permute-start | bytes 3932168 | tf_op jit(solution)/shard_map/ppermute | solution.py:22
  180.8 17.5 %collective-permute-start.19 = (bf16[1024,256]{1,0:T(8,128)(2,1)}, bf16[1024,256]{1,0:T(8,128)(2,1)S(1)}, u32[]{:S(2)}, u32[]{:S(2)}) collective-permute-start(bf16[1024,256]{1,0:T(8,128)(2,1)} %shard_map.71), channel_id=1, source_target_pairs={{0,1},{1,0},{2,3},{3,2},{4,5},{5,4},{6,7},{7,6},{8,9},{9,8},{10,11... | collective-permute-start | bytes 1572872 | tf_op jit(solution)/shard_map/ppermute | solution.py:22
  187.4 19.6 %collective-permute-start.20 = (bf16[1024,256]{1,0:T(8,128)(2,1)}, bf16[1024,256]{1,0:T(8,128)(2,1)S(1)}, u32[]{:S(2)}, u32[]{:S(2)}) collective-permute-start(bf16[1024,256]{1,0:T(8,128)(2,1)} %shard_map.72), channel_id=1, source_target_pairs={{0,1},{1,0},{2,3},{3,2},{4,5},{5,4},{6,7},{7,6},{8,9},{9,8},{10,11... | collective-permute-start | bytes 1572872 | tf_op jit(solution)/shard_map/ppermute | solution.py:22
  (18 other events, 63.1 us)

commit v7 on v5

--- a/solution.py
+++ b/solution.py
@@ -252,27 +252,27 @@
     up1, down1 = both(base, 1), both(base, -1)
     up1, down1 = after((up1, down1), base_peer)
     up2, down2 = both(up1, 1), both(down1, -1)
-    near, distant = (0, 1, -1), (2, -2, 3, -3, 4)
+    near, distant = (0, 1, -1, 2, -2), (3, -3, 4)
     near_blocks = [base, down1, up1]
     near_halves = halves(near_blocks)
     (up2, down2), near_halves = lax.optimization_barrier(((up2, down2), near_halves))
     up3, down3 = both(up2, 1), both(down2, -1)
-    summed_a = added([near_halves])
-    pieces_a = scatter(summed_a)
-    middle_halves = halves(after([down2, up2], summed_a))
-    (up3, down3), middle_halves = lax.optimization_barrier(((up3, down3), middle_halves))
+    middle_halves = halves([down2, up2])
+    up3, down3 = after((up3, down3), middle_halves)
+    pieces_a = scatter(added([near_halves, middle_halves]))
     far = shift(up3[0][:half], "z", NZ, 1), shift(down3[0][half:], "z", NZ, -1)
 
-    distant_blocks = [down2, up2, down3, up3, far]
+    near_blocks = near_blocks + [down2, up2]
+    distant_blocks = [down3, up3, far]
     amp_a = amplitudes(near, pieces_a, CHIPS)
     mine_a = spread(amp_a)
     other_a = swap(mine_a, "c")
-    last_halves = halves(distant_blocks[2:])
-    pieces_b = scatter(after(added([middle_halves, last_halves]), mine_a))
+    last_halves = halves(distant_blocks)
+    pieces_b = scatter(after(added([last_halves]), mine_a))
     sums = [[gamma(side, store, near_blocks, mine_a, other_a) for store in range(2)] for side in range(2)]
-    amp_b = amplitudes(distant, after(pieces_b, sums), CHIPS)
+    amp_b = amplitudes(distant, after(pieces_b, sums[0]), CHIPS)
     mine_b = spread(amp_b)
-    other_b = swap(mine_b, "c")
+    other_b = swap(after(mine_b, sums[1]), "c")
     there = [gamma(side, 1, distant_blocks, mine_b, other_b, sums[side][1], BF16) for side in range(2)]
     arrived = [swap(part, "yh").astype(F32) for part in there]
     mine_b, other_b = after((mine_b, other_b), there)

time: 205 us -> 209 us (1.020)
  waiting for transfers between devices: 53.7 us -> 81.6 us
  blocking collectives: 19.9 us -> 0 us
  starting transfers between devices: 51.4 us -> 47.5 us
    all_to_all x1 -> x0, blocking collectives: 19.9 us -> none  [spread(): lax.all_to_all(copies, ('x', 'yl'), 0, 0, tiled=True).reshape(width, -1)]
    all_to_all x1 -> x2, waiting for transfers between devices: 0.01 us -> 15.4 us  [spread(): lax.all_to_all(copies, ('x', 'yl'), 0, 0, tiled=True).reshape(width, -1)]
    all_to_all x2, waiting for transfers between devices: 2.32 us -> 17.1 us  [scatter(): lax.all_to_all(summed.reshape(CHIPS, rows, -1), ('x', 'yl'), 0, 0, tiled=...]
    ppermute x13, starting transfers between devices: 21.1 us -> 16.9 us  [swap(): return lax.ppermute(value, axis, [(0, 1), (1, 0)])]
    all_to_all x1 -> x2, starting transfers between devices: 5.04 us -> 7.32 us  [spread(): lax.all_to_all(copies, ('x', 'yl'), 0, 0, tiled=True).reshape(width, -1)]
    unnamed x52 -> x50, local copies, waits for them, and re-layouts: 7.56 us -> 5.65 us
  transfers between devices with their start and end apart: 24 -> 25, of which waited for: 14 -> 20; matrix products, arithmetic and copies ran while one was open for 2% -> 3% of each run, Pallas kernels for 27% -> 23%
where the time goes in v7:
time: 209 us; the launch traced here: 208 us
  waiting for transfers between devices  81.6 us (39%)
  Pallas kernels  62.7 us (30%)
  starting transfers between devices  47.5 us (23%)
  local copies, waits for them, and re-layouts  8.69 us (4%)
  other arithmetic  5.32 us (3%)
  between operations  2.25 us (1%)
    pallas_call x16, Pallas kernels, call(): pl.pallas_call(body, out_shape=out_shape, in_specs=specs, out_specs=out_s...  62.7 us
    ppermute x8, waiting for transfers between devices, shift(): lax.ppermute(value, axis, [(i, (i + step) % size) for i in range(size)])  29.7 us
    ppermute x13, waiting for transfers between devices, swap(): return lax.ppermute(value, axis, [(0, 1), (1, 0)])  19.4 us
    all_to_all x2, waiting for transfers between devices, scatter(): lax.all_to_all(summed.reshape(CHIPS, rows, -1), ('x', 'yl'), 0, 0, tiled=...  17.1 us
    ppermute x13, starting transfers between devices, swap(): return lax.ppermute(value, axis, [(0, 1), (1, 0)])  16.9 us
    all_to_all x2, waiting for transfers between devices, spread(): lax.all_to_all(copies, ('x', 'yl'), 0, 0, tiled=True).reshape(width, -1)  15.4 us
    ppermute x8, starting transfers between devices, shift(): lax.ppermute(value, axis, [(i, (i + step) % size) for i in range(size)])  14.7 us
    all_to_all x2, starting transfers between devices, scatter(): lax.all_to_all(summed.reshape(CHIPS, rows, -1), ('x', 'yl'), 0, 0, tiled=...  8.6 us
  transfers between devices with their start and end apart: 25, of which 20 were waited for; matrix products, arithmetic and copies ran while one was open for 3% of the time, Pallas kernels for 23%

profile of v7, /device:TPU:1, one launch (start us, length us, event | category | flops | bytes accessed | tf_op | source)
XLA Modules:
  0.0 208.0 jit_solution(17349054616434493259)
XLA Ops:
  1.9 6.5 %collective-permute-start.2 = (bf16[1024,512]{1,0:T(8,128)(2,1)S(1)}, bf16[1024,512]{1,0:T(8,128)(2,1)S(1)}, u32[]{:S(2)}, u32[]{:S(2)}) collective-permute-start(bf16[1024,512]{1,0:T(8,128)(2,1)S(1)} %pad_maximum_fusion.refs_1_.refs_3_), channel_id=1, source_target_pairs={{0,14},{2,0},{4,2},{6,4},{8,6},{10,8},{12,10},{14,12},{1,15},{3,1}... | collective-permute-start | bytes 3145736 | tf_op jit(solution)/shard_map/ppermute | solution.py:18
  8.4 2.9 %collective-permute-start = (bf16[1024,512]{1,0:T(8,128)(2,1)S(1)}, bf16[1024,512]{1,0:T(8,128)(2,1)S(1)}, u32[]{:S(2)}, u32[]{:S(2)}) collective-permute-start(bf16[1024,512]{1,0:T(8,128)(2,1)S(1)} %pad_maximum_fusion.refs_1_.refs_3_), channel_id=1, source_target_pairs={{0,1},{1,0},{2,3},{3,2},{4,5},{5,4},{6,7},{7,6},{8,9},{9,8},{10,11... | collective-permute-start | bytes 3145736 | tf_op jit(solution)/shard_map/ppermute | solution.py:22
  11.3 18.9 %collective-permute-done.2.refs_2_.refs_4_ = bf16[1024,512]{1,0:T(8,128)(2,1)S(1)} collective-permute-done((bf16[1024,512]{1,0:T(8,128)(2,1)S(1)}, bf16[1024,512]{1,0:T(8,128)(2,1)S(1)}, u32[]{:S(2)}, u32[]{:S(2)}) %collective-permute-start.2) | collective-permute-done | bytes 1048608 | tf_op jit(solution)/shard_map/ppermute | solution.py:18
  30.2 3.1 %collective-permute-done.1.refs_3_.refs_5_ = bf16[1024,512]{1,0:T(8,128)(2,1)S(1)} collective-permute-done((bf16[1024,512]{1,0:T(8,128)(2,1)S(1)}, bf16[1024,512]{1,0:T(8,128)(2,1)S(1)}, u32[]{:S(2)}, u32[]{:S(2)}) %collective-permute-start.1) | collective-permute-done | bytes 1048608 | tf_op jit(solution)/shard_map/ppermute | solution.py:18
  34.6 2.7 %collective-permute-start.4 = (bf16[1024,512]{1,0:T(8,128)(2,1)S(1)}, bf16[1024,512]{1,0:T(8,128)(2,1)}, u32[]{:S(2)}, u32[]{:S(2)}) collective-permute-start(bf16[1024,512]{1,0:T(8,128)(2,1)S(1)} %collective-permute-done.2.refs_2_.refs_4_), channel_id=1, source_target_pairs={{0,14},{2,0},{4,2},{6,4},{8,6},{10,8},{12,10},{14,12},{1,15},{3,1}... | collective-permute-start | bytes 3145736 | tf_op jit(solution)/shard_map/ppermute | solution.py:18
  37.3 3.6 %shard_map.59.refs_0_ = bf16[1024,1024]{1,0:T(8,128)(2,1)} custom-call(s32[1]{0:T(128)} %bitcast.refs_0_, bf16[1024,512]{1,0:T(8,128)(2,1)} %copy-done, bf16[1024,512]{1,0:T(8,128)(2,1)} %copy-done.11), custom_call_target="tpu_custom_call" | custom-call | tf_op jit(solution)/shard_map/pallas_call | solution.py:67
  41.0 5.3 %shard_map.60 = (f32[256,1536]{1,0:T(8,128)}, f32[256,512]{1,0:T(8,128)}, f32[256,512]{1,0:T(8,128)}, f32[256,512]{1,0:T(8,128)}) custom-call(bf16[1024,1024]{1,0:T(8,128)(2,1)} %shard_map.59.refs_0_, bf16[1024,512]{1,0:T(8,128)(2,1)} %copy-done, bf16[1024,512]{1,0:T(8,128)(2,1)} %copy-done.4, bf16[1024,512]{1,0:T(8,128)(2,1)} %copy-done.5), custom_call_target="tpu_custom_call" | custom-call | tf_op jit(solution)/shard_map/pallas_call | solution.py:67
  52.0 6.7 %collective-permute-done.3.refs_2_.refs_7_ = bf16[1024,512]{1,0:T(8,128)(2,1)} collective-permute-done((bf16[1024,512]{1,0:T(8,128)(2,1)S(1)}, bf16[1024,512]{1,0:T(8,128)(2,1)}, u32[]{:S(2)}, u32[]{:S(2)}) %collective-permute-start.3) | collective-permute-done | bytes 1048608 | tf_op jit(solution)/shard_map/ppermute | solution.py:18
  58.7 4.4 %shard_map.61 = (f32[256,1024]{1,0:T(8,128)}, f32[256,512]{1,0:T(8,128)}, f32[256,512]{1,0:T(8,128)}) custom-call(bf16[1024,1024]{1,0:T(8,128)(2,1)} %shard_map.59.refs_0_, bf16[1024,512]{1,0:T(8,128)(2,1)} %collective-permute-done.4.refs_1_.refs_6_, bf16[1024,512]{1,0:T(8,128)(2,1)} %collective-permute-done.3.refs_2_.refs_7_), custom_call_target="tpu_custom_call" | custom-call | tf_op jit(solution)/shard_map/pallas_call | solution.py:67
  63.2 2.9 %collective-permute-start.10 = (f32[256,512]{1,0:T(8,128)}, f32[256,512]{1,0:T(8,128)S(1)}, u32[]{:S(2)}, u32[]{:S(2)}) collective-permute-start(f32[256,512]{1,0:T(8,128)} %get-tuple-element.37), channel_id=1, source_target_pairs={{0,16},{16,0},{1,17},{17,1},{2,18},{18,2},{3,19},{19,3},{4,20},{20... | collective-permute-start | bytes 1572872 | tf_op jit(solution)/shard_map/ppermute | solution.py:22
  69.4 3.6 %shard_map.64 = bf16[256,2560]{1,0:T(8,128)(2,1)} custom-call(f32[256,1536]{1,0:T(8,128)} %get-tuple-element.45.refs_0_, f32[256,512]{1,0:T(8,128)} %copy-done.12, f32[256,512]{1,0:T(8,128)} %copy-done.13, f32[256,512]{1,0:T(8,128)} %copy-done.14, f32[256,1024]{1,0:T(8,128)} %get-tuple-element.36.refs_4_, f32[256,512]{1,0:T(8,128)} %copy-done.17, ...), custom_call_target="tpu_custom_call" | custom-call | tf_op jit(solution)/shard_map/pallas_call | solution.py:67
  73.0 5.0 %all-to-all-start = ((bf16[8,32,2560]{2,1,0:T(8,128)(2,1)}), bf16[8,32,2560]{2,1,0:T(8,128)(2,1)S(1)}, u32[]{:S(2)}, u32[]{:S(2)}) async-start(bf16[8,32,2560]{2,1,0:T(8,128)(2,1)} %bitcast.47), calls=%async_computation | async-start | bytes 2621440 | tf_op jit(solution)/shard_map/all_to_all | solution.py:230
  80.8 2.7 %collective-permute-start.9 = (bf16[1024,512]{1,0:T(8,128)(2,1)}, bf16[1024,512]{1,0:T(8,128)(2,1)S(1)}, u32[]{:S(2)}, u32[]{:S(2)}) collective-permute-start(bf16[1024,512]{1,0:T(8,128)(2,1)} %collective-permute-done.4.refs_1_.refs_6_), channel_id=1, source_target_pairs={{0,14},{2,0},{4,2},{6,4},{8,6},{10,8},{12,10},{14,12},{1,15},{3,1}... | collective-permute-start | bytes 3145736 | tf_op jit(solution)/shard_map/ppermute | solution.py:18
  83.6 14.2 %all-to-all-done.refs_0_ = bf16[8,32,2560]{2,1,0:T(8,128)(2,1)S(1)} async-done(((bf16[8,32,2560]{2,1,0:T(8,128)(2,1)}), bf16[8,32,2560]{2,1,0:T(8,128)(2,1)S(1)}, u32[]{:S(2)}, u32[]{:S(2)}) %all-to-all-start) | async-done | bytes 1310752 | tf_op jit(solution)/shard_map/all_to_all | solution.py:230
  98.9 2.6 %shard_map.65 = bf16[8,32,2560]{2,1,0:T(8,128)(2,1)} custom-call(bf16[8,32,2560]{2,1,0:T(8,128)(2,1)} %copy-done.8, f32[32,1]{1,0:T(8,128)} %copy.6.refs_1_, f32[1,1280]{1,0:T(1,128)} %copy-done.21), custom_call_target="tpu_custom_call" | custom-call | tf_op jit(solution)/shard_map/pallas_call | solution.py:67
  101.5 3.8 %all-to-all-start.1 = ((bf16[8,32,2560]{2,1,0:T(8,128)(2,1)}), bf16[8,32,2560]{2,1,0:T(8,128)(2,1)S(1)}, u32[]{:S(2)}, u32[]{:S(2)}) async-start(bf16[8,32,2560]{2,1,0:T(8,128)(2,1)} %shard_map.65), calls=%async_computation.1 | async-start | bytes 2621440 | tf_op jit(solution)/shard_map/all_to_all | solution.py:239
  110.7 12.9 %all-to-all-done.1 = bf16[8,32,2560]{2,1,0:T(8,128)(2,1)S(1)} async-done(((bf16[8,32,2560]{2,1,0:T(8,128)(2,1)}), bf16[8,32,2560]{2,1,0:T(8,128)(2,1)S(1)}, u32[]{:S(2)}, u32[]{:S(2)}) %all-to-all-start.1) | async-done | bytes 1310752 | tf_op jit(solution)/shard_map/all_to_all | solution.py:239
  125.5 5.4 %shard_map.62 = (f32[256,1536]{1,0:T(8,128)}, f32[256,512]{1,0:T(8,128)}, f32[256,512]{1,0:T(8,128)}, f32[256,512]{1,0:T(8,128)}) custom-call(bf16[1024,1024]{1,0:T(8,128)(2,1)} %shard_map.59.refs_0_, bf16[1024,512]{1,0:T(8,128)(2,1)} %copy-done.3, bf16[1024,512]{1,0:T(8,128)(2,1)} %copy-done.2, bf16[512,512]{1,0:T(8,128)(2,1)} %collective-permute-done.12.refs_3_.refs_5_, ...), custom_call_target="tpu_custom_call" | custom-call | tf_op jit(solution)/shard_map/pallas_call | solution.py:67
  135.5 2.8 %shard_map.63 = bf16[256,1536]{1,0:T(8,128)(2,1)} custom-call(f32[256,1536]{1,0:T(8,128)} %get-tuple-element.41.refs_0_, f32[256,512]{1,0:T(8,128)} %copy-done.15, f32[256,512]{1,0:T(8,128)} %copy-done.16, f32[256,512]{1,0:T(8,128)} %copy-done.18), custom_call_target="tpu_custom_call" | custom-call | tf_op jit(solution)/shard_map/pallas_call | solution.py:67
  138.4 3.6 %all-to-all-start.2 = ((bf16[8,32,1536]{2,1,0:T(8,128)(2,1)}), bf16[8,32,1536]{2,1,0:T(8,128)(2,1)S(1)}, u32[]{:S(2)}, u32[]{:S(2)}) async-start(bf16[8,32,1536]{2,1,0:T(8,128)(2,1)} %bitcast.48), calls=%async_computation.2 | async-start | bytes 1572864 | tf_op jit(solution)/shard_map/all_to_all | solution.py:230
  142.6 4.4 %shard_map.67.refs_7_ = f32[1024,256]{1,0:T(8,128)} custom-call(s32[1]{0:T(128)} %bitcast.refs_0_, bf16[256,2560]{1,0:T(8,128)(2,1)} %bitcast.38, bf16[256,2560]{1,0:T(8,128)(2,1)} %collective-permute-done.17.refs_2_, bf16[1024,512]{1,0:T(8,128)(2,1)} %copy-done, bf16[1024,512]{1,0:T(8,128)(2,1)} %copy-done.4, bf16[1024,512]{1,0:T(8,128)(2,1)} %copy-done.5, ...), custom_call_target="tpu_custom_call" | custom-call | tf_op jit(solution)/shard_map/pallas_call | solution.py:67
  147.1 4.4 %shard_map.66.refs_7_ = f32[1024,256]{1,0:T(8,128)} custom-call(s32[1]{0:T(128)} %bitcast.refs_0_, bf16[256,2560]{1,0:T(8,128)(2,1)} %bitcast.39, bf16[256,2560]{1,0:T(8,128)(2,1)} %collective-permute-done.17.refs_2_, bf16[1024,512]{1,0:T(8,128)(2,1)} %copy-done, bf16[1024,512]{1,0:T(8,128)(2,1)} %copy-done.4, bf16[1024,512]{1,0:T(8,128)(2,1)} %copy-done.5, ...), custom_call_target="tpu_custom_call" | custom-call | tf_op jit(solution)/shard_map/pallas_call | solution.py:67
  151.4 2.9 %all-to-all-done.2.refs_0_ = bf16[8,32,1536]{2,1,0:T(8,128)(2,1)S(1)} async-done(((bf16[8,32,1536]{2,1,0:T(8,128)(2,1)}), bf16[8,32,1536]{2,1,0:T(8,128)(2,1)S(1)}, u32[]{:S(2)}, u32[]{:S(2)}) %all-to-all-start.2) | async-done | bytes 786464 | tf_op jit(solution)/shard_map/all_to_all | solution.py:230
  157.4 3.6 %all-to-all-start.3 = ((bf16[8,32,1536]{2,1,0:T(8,128)(2,1)}), bf16[8,32,1536]{2,1,0:T(8,128)(2,1)S(1)}, u32[]{:S(2)}, u32[]{:S(2)}) async-start(bf16[8,32,1536]{2,1,0:T(8,128)(2,1)} %shard_map.68), calls=%async_computation.3 | async-start | bytes 1572864 | tf_op jit(solution)/shard_map/all_to_all | solution.py:239
  161.0 4.4 %shard_map.70.refs_7_ = f32[1024,256]{1,0:T(8,128)} custom-call(s32[1]{0:T(128)} %bitcast.refs_0_, bf16[256,2560]{1,0:T(8,128)(2,1)} %bitcast.40, bf16[256,2560]{1,0:T(8,128)(2,1)} %collective-permute-done.17.refs_2_, bf16[1024,512]{1,0:T(8,128)(2,1)} %copy-done, bf16[1024,512]{1,0:T(8,128)(2,1)} %copy-done.4, bf16[1024,512]{1,0:T(8,128)(2,1)} %copy-done.5, ...), custom_call_target="tpu_custom_call" | custom-call | tf_op jit(solution)/shard_map/pallas_call | solution.py:67
  165.4 4.4 %shard_map.69.refs_7_ = f32[1024,256]{1,0:T(8,128)} custom-call(s32[1]{0:T(128)} %bitcast.refs_0_, bf16[256,2560]{1,0:T(8,128)(2,1)} %bitcast.41, bf16[256,2560]{1,0:T(8,128)(2,1)} %collective-permute-done.17.refs_2_, bf16[1024,512]{1,0:T(8,128)(2,1)} %copy-done, bf16[1024,512]{1,0:T(8,128)(2,1)} %copy-done.4, bf16[1024,512]{1,0:T(8,128)(2,1)} %copy-done.5, ...), custom_call_target="tpu_custom_call" | custom-call | tf_op jit(solution)/shard_map/pallas_call | solution.py:67
  177.1 3.7 %shard_map.71 = bf16[1024,256]{1,0:T(8,128)(2,1)} custom-call(s32[1]{0:T(128)} %bitcast.refs_0_, bf16[256,1536]{1,0:T(8,128)(2,1)} %bitcast.43, bf16[256,1536]{1,0:T(8,128)(2,1)} %copy-done.7, bf16[1024,512]{1,0:T(8,128)(2,1)} %copy-done.3, bf16[1024,512]{1,0:T(8,128)(2,1)} %copy-done.2, bf16[512,512]{1,0:T(8,128)(2,1)} %collective-permute-done.12.refs_3_.refs_5_, ...), custom_call_target="tpu_custom_call" | custom-call | tf_op jit(solution)/shard_map/pallas_call | solution.py:67
  180.8 2.7 %collective-permute-start.19 = (bf16[1024,256]{1,0:T(8,128)(2,1)}, bf16[1024,256]{1,0:T(8,128)(2,1)S(1)}, u32[]{:S(2)}, u32[]{:S(2)}) collective-permute-start(bf16[1024,256]{1,0:T(8,128)(2,1)} %shard_map.71), channel_id=1, source_target_pairs={{0,1},{1,0},{2,3},{3,2},{4,5},{5,4},{6,7},{7,6},{8,9},{9,8},{10,11... | collective-permute-start | bytes 1572872 | tf_op jit(solution)/shard_map/ppermute | solution.py:22
  183.5 3.6 %shard_map.72 = bf16[1024,256]{1,0:T(8,128)(2,1)} custom-call(s32[1]{0:T(128)} %bitcast.refs_0_, bf16[256,1536]{1,0:T(8,128)(2,1)} %bitcast.44, bf16[256,1536]{1,0:T(8,128)(2,1)} %copy-done.7, bf16[1024,512]{1,0:T(8,128)(2,1)} %copy-done.3, bf16[1024,512]{1,0:T(8,128)(2,1)} %copy-done.2, bf16[512,512]{1,0:T(8,128)(2,1)} %collective-permute-done.12.refs_3_.refs_5_, ...), custom_call_target="tpu_custom_call" | custom-call | tf_op jit(solution)/shard_map/pallas_call | solution.py:67
  187.6 3.9 %shard_map.74 = f32[1024,256]{1,0:T(8,128)} custom-call(s32[1]{0:T(128)} %bitcast.refs_0_, bf16[256,1536]{1,0:T(8,128)(2,1)} %bitcast.45, bf16[256,1536]{1,0:T(8,128)(2,1)} %copy-done.7, bf16[1024,512]{1,0:T(8,128)(2,1)} %copy-done.3, bf16[1024,512]{1,0:T(8,128)(2,1)} %copy-done.2, bf16[512,512]{1,0:T(8,128)(2,1)} %collective-permute-done.12.refs_3_.refs_5_, ...), custom_call_target="tpu_custom_call" | custom-call | tf_op jit(solution)/shard_map/pallas_call | solution.py:67
  191.5 3.8 %shard_map.73 = f32[1024,256]{1,0:T(8,128)} custom-call(s32[1]{0:T(128)} %bitcast.refs_0_, bf16[256,1536]{1,0:T(8,128)(2,1)} %bitcast.46, bf16[256,1536]{1,0:T(8,128)(2,1)} %copy-done.7, bf16[1024,512]{1,0:T(8,128)(2,1)} %copy-done.3, bf16[1024,512]{1,0:T(8,128)(2,1)} %copy-done.2, bf16[512,512]{1,0:T(8,128)(2,1)} %collective-permute-done.12.refs_3_.refs_5_, ...), custom_call_target="tpu_custom_call" | custom-call | tf_op jit(solution)/shard_map/pallas_call | solution.py:67
  198.0 8.9 %collective-permute-done.20 = bf16[1024,256]{1,0:T(8,128)(2,1)S(1)} collective-permute-done((bf16[1024,256]{1,0:T(8,128)(2,1)}, bf16[1024,256]{1,0:T(8,128)(2,1)S(1)}, u32[]{:S(2)}, u32[]{:S(2)}) %collective-permute-start.20) | collective-permute-done | bytes 524320 | tf_op jit(solution)/shard_map/ppermute | solution.py:22
  (96 shorter events, 41.4 us)
Async XLA Ops:
  1.9 35.4 %copy-start = (bf16[1024,512]{1,0:T(8,128)(2,1)}, bf16[1024,512]{1,0:T(8,128)(2,1)S(1)}, u32[]{:S(2)}) copy-start(bf16[1024,512]{1,0:T(8,128)(2,1)S(1)} %pad_maximum_fusion.refs_1_.refs_3_) | copy-start | bytes 3145732
  1.9 28.3 %collective-permute-start.2 = (bf16[1024,512]{1,0:T(8,128)(2,1)S(1)}, bf16[1024,512]{1,0:T(8,128)(2,1)S(1)}, u32[]{:S(2)}, u32[]{:S(2)}) collective-permute-start(bf16[1024,512]{1,0:T(8,128)(2,1)S(1)} %pad_maximum_fusion.refs_1_.refs_3_), channel_id=1, source_target_pairs={{0,14},{2,0},{4,2},{6,4},{8,6},{10,8},{12,10},{14,12},{1,15},{3,1}... | collective-permute-start | bytes 3145736 | tf_op jit(solution)/shard_map/ppermute | solution.py:18
  8.4 24.9 %collective-permute-start.1 = (bf16[1024,512]{1,0:T(8,128)(2,1)S(1)}, bf16[1024,512]{1,0:T(8,128)(2,1)S(1)}, u32[]{:S(2)}, u32[]{:S(2)}) collective-permute-start(bf16[1024,512]{1,0:T(8,128)(2,1)S(1)} %pad_maximum_fusion.refs_1_.refs_3_), channel_id=1, source_target_pairs={{0,2},{2,4},{4,6},{6,8},{8,10},{10,12},{12,14},{14,0},{1,3},{3,5},... | collective-permute-start | bytes 3145736 | tf_op jit(solution)/shard_map/ppermute | solution.py:18
  8.4 25.2 %collective-permute-start = (bf16[1024,512]{1,0:T(8,128)(2,1)S(1)}, bf16[1024,512]{1,0:T(8,128)(2,1)S(1)}, u32[]{:S(2)}, u32[]{:S(2)}) collective-permute-start(bf16[1024,512]{1,0:T(8,128)(2,1)S(1)} %pad_maximum_fusion.refs_1_.refs_3_), channel_id=1, source_target_pairs={{0,1},{1,0},{2,3},{3,2},{4,5},{5,4},{6,7},{7,6},{8,9},{9,8},{10,11... | collective-permute-start | bytes 3145736 | tf_op jit(solution)/shard_map/ppermute | solution.py:22
  34.6 24.1 %collective-permute-start.3 = (bf16[1024,512]{1,0:T(8,128)(2,1)S(1)}, bf16[1024,512]{1,0:T(8,128)(2,1)}, u32[]{:S(2)}, u32[]{:S(2)}) collective-permute-start(bf16[1024,512]{1,0:T(8,128)(2,1)S(1)} %collective-permute-done.1.refs_3_.refs_5_), channel_id=1, source_target_pairs={{0,2},{2,4},{4,6},{6,8},{8,10},{10,12},{12,14},{14,0},{1,3},{3,5},... | collective-permute-start | bytes 3145736 | tf_op jit(solution)/shard_map/ppermute | solution.py:18
  34.6 24.1 %collective-permute-start.4 = (bf16[1024,512]{1,0:T(8,128)(2,1)S(1)}, bf16[1024,512]{1,0:T(8,128)(2,1)}, u32[]{:S(2)}, u32[]{:S(2)}) collective-permute-start(bf16[1024,512]{1,0:T(8,128)(2,1)S(1)} %collective-permute-done.2.refs_2_.refs_4_), channel_id=1, source_target_pairs={{0,14},{2,0},{4,2},{6,4},{8,6},{10,8},{12,10},{14,12},{1,15},{3,1}... | collective-permute-start | bytes 3145736 | tf_op jit(solution)/shard_map/ppermute | solution.py:18
  46.3 4.3 %collective-permute-start.5 = (f32[256,512]{1,0:T(8,128)}, f32[256,512]{1,0:T(8,128)S(1)}, u32[]{:S(2)}, u32[]{:S(2)}) collective-permute-start(f32[256,512]{1,0:T(8,128)} %get-tuple-element.31), channel_id=1, source_target_pairs={{0,16},{16,0},{1,17},{17,1},{2,18},{18,2},{3,19},{19,3},{4,20},{20... | collective-permute-start | bytes 1572872 | tf_op jit(solution)/shard_map/ppermute | solution.py:22
  48.8 2.5 %collective-permute-start.6 = (f32[256,512]{1,0:T(8,128)}, f32[256,512]{1,0:T(8,128)S(1)}, u32[]{:S(2)}, u32[]{:S(2)}) collective-permute-start(f32[256,512]{1,0:T(8,128)} %get-tuple-element.32), channel_id=1, source_target_pairs={{0,16},{16,0},{1,17},{17,1},{2,18},{18,2},{3,19},{19,3},{4,20},{20... | collective-permute-start | bytes 1572872 | tf_op jit(solution)/shard_map/ppermute | solution.py:22
  48.9 3.1 %collective-permute-start.7 = (f32[256,512]{1,0:T(8,128)}, f32[256,512]{1,0:T(8,128)S(1)}, u32[]{:S(2)}, u32[]{:S(2)}) collective-permute-start(f32[256,512]{1,0:T(8,128)} %get-tuple-element.33), channel_id=1, source_target_pairs={{0,16},{16,0},{1,17},{17,1},{2,18},{18,2},{3,19},{19,3},{4,20},{20... | collective-permute-start | bytes 1572872 | tf_op jit(solution)/shard_map/ppermute | solution.py:22
  50.5 12.6 %copy-start.12 = (f32[256,512]{1,0:T(8,128)}, f32[256,512]{1,0:T(8,128)S(1)}, u32[]{:S(2)}) copy-start(f32[256,512]{1,0:T(8,128)S(1)} %collective-permute-done.5.refs_1_) | copy-start | bytes 1572868
  51.3 11.9 %copy-start.13 = (f32[256,512]{1,0:T(8,128)}, f32[256,512]{1,0:T(8,128)S(1)}, u32[]{:S(2)}) copy-start(f32[256,512]{1,0:T(8,128)S(1)} %collective-permute-done.6.refs_2_) | copy-start | bytes 1572868
  63.2 4.6 %collective-permute-start.10 = (f32[256,512]{1,0:T(8,128)}, f32[256,512]{1,0:T(8,128)S(1)}, u32[]{:S(2)}, u32[]{:S(2)}) collective-permute-start(f32[256,512]{1,0:T(8,128)} %get-tuple-element.37), channel_id=1, source_target_pairs={{0,16},{16,0},{1,17},{17,1},{2,18},{18,2},{3,19},{19,3},{4,20},{20... | collective-permute-start | bytes 1572872 | tf_op jit(solution)/shard_map/ppermute | solution.py:22
  66.1 2.5 %collective-permute-start.11 = (f32[256,512]{1,0:T(8,128)}, f32[256,512]{1,0:T(8,128)S(1)}, u32[]{:S(2)}, u32[]{:S(2)}) collective-permute-start(f32[256,512]{1,0:T(8,128)} %get-tuple-element.38), channel_id=1, source_target_pairs={{0,16},{16,0},{1,17},{17,1},{2,18},{18,2},{3,19},{19,3},{4,20},{20... | collective-permute-start | bytes 1572872 | tf_op jit(solution)/shard_map/ppermute | solution.py:22
  73.0 24.8 %all-to-all-start = ((bf16[8,32,2560]{2,1,0:T(8,128)(2,1)}), bf16[8,32,2560]{2,1,0:T(8,128)(2,1)S(1)}, u32[]{:S(2)}, u32[]{:S(2)}) async-start(bf16[8,32,2560]{2,1,0:T(8,128)(2,1)} %bitcast.47), calls=%async_computation | async-start | bytes 2621440 | tf_op jit(solution)/shard_map/all_to_all | solution.py:230
  80.7 25.5 %collective-permute-start.8 = (bf16[1024,512]{1,0:T(8,128)(2,1)}, bf16[1024,512]{1,0:T(8,128)(2,1)S(1)}, u32[]{:S(2)}, u32[]{:S(2)}) collective-permute-start(bf16[1024,512]{1,0:T(8,128)(2,1)} %collective-permute-done.3.refs_2_.refs_7_), channel_id=1, source_target_pairs={{0,2},{2,4},{4,6},{6,8},{8,10},{10,12},{12,14},{14,0},{1,3},{3,5},... | collective-permute-start | bytes 3145736 | tf_op jit(solution)/shard_map/ppermute | solution.py:18
  80.8 25.5 %collective-permute-start.9 = (bf16[1024,512]{1,0:T(8,128)(2,1)}, bf16[1024,512]{1,0:T(8,128)(2,1)S(1)}, u32[]{:S(2)}, u32[]{:S(2)}) collective-permute-start(bf16[1024,512]{1,0:T(8,128)(2,1)} %collective-permute-done.4.refs_1_.refs_6_), channel_id=1, source_target_pairs={{0,14},{2,0},{4,2},{6,4},{8,6},{10,8},{12,10},{14,12},{1,15},{3,1}... | collective-permute-start | bytes 3145736 | tf_op jit(solution)/shard_map/ppermute | solution.py:18
  83.6 14.2 %copy-start.21 = (f32[1,1280]{1,0:T(1,128)}, f32[1,1280]{1,0:T(1,128)S(1)}, u32[]{:S(2)}) copy-start(f32[1,1280]{1,0:T(1,128)S(1)} %constant_dynamic-update-slice_fusion.refs_2_) | copy-start | bytes 15364
  101.5 22.1 %all-to-all-start.1 = ((bf16[8,32,2560]{2,1,0:T(8,128)(2,1)}), bf16[8,32,2560]{2,1,0:T(8,128)(2,1)S(1)}, u32[]{:S(2)}, u32[]{:S(2)}) async-start(bf16[8,32,2560]{2,1,0:T(8,128)(2,1)} %shard_map.65), calls=%async_computation.1 | async-start | bytes 2621440 | tf_op jit(solution)/shard_map/all_to_all | solution.py:239
  106.2 19.2 %copy-start.2 = (bf16[1024,512]{1,0:T(8,128)(2,1)}, bf16[1024,512]{1,0:T(8,128)(2,1)S(1)}, u32[]{:S(2)}) copy-start(bf16[1024,512]{1,0:T(8,128)(2,1)S(1)} %collective-permute-done.8.refs_2_.refs_4_) | copy-start | bytes 3145732
  106.2 19.2 %copy-start.3 = (bf16[1024,512]{1,0:T(8,128)(2,1)}, bf16[1024,512]{1,0:T(8,128)(2,1)S(1)}, u32[]{:S(2)}) copy-start(bf16[1024,512]{1,0:T(8,128)(2,1)S(1)} %collective-permute-done.9.refs_1_.refs_3_) | copy-start | bytes 3145732
  108.0 17.5 %collective-permute-start.12 = (bf16[512,512]{1,0:T(8,128)(2,1)}, bf16[512,512]{1,0:T(8,128)(2,1)}, u32[]{:S(2)}, u32[]{:S(2)}) collective-permute-start(bf16[512,512]{1,0:T(8,128)(2,1)} %slice.12), channel_id=1, source_target_pairs={{0,2},{2,4},{4,6},{6,8},{8,10},{10,12},{12,14},{14,0},{1,3},{3,5},... | collective-permute-start | bytes 1572872 | tf_op jit(solution)/shard_map/ppermute | solution.py:18
  108.6 16.8 %collective-permute-start.13 = (bf16[512,512]{1,0:T(8,128)(2,1)}, bf16[512,512]{1,0:T(8,128)(2,1)}, u32[]{:S(2)}, u32[]{:S(2)}) collective-permute-start(bf16[512,512]{1,0:T(8,128)(2,1)} %slice.13), channel_id=1, source_target_pairs={{0,14},{2,0},{4,2},{6,4},{8,6},{10,8},{12,10},{14,12},{1,15},{3,1}... | collective-permute-start | bytes 1572872 | tf_op jit(solution)/shard_map/ppermute | solution.py:18
  123.6 19.0 %collective-permute-start.17 = (bf16[256,2560]{1,0:T(8,128)(2,1)S(1)}, bf16[256,2560]{1,0:T(8,128)(2,1)}, u32[]{:S(2)}, u32[]{:S(2)}) collective-permute-start(bf16[256,2560]{1,0:T(8,128)(2,1)S(1)} %bitcast.37), channel_id=1, source_target_pairs={{0,16},{16,0},{1,17},{17,1},{2,18},{18,2},{3,19},{19,3},{4,20},{20... | collective-permute-start | bytes 3932168 | tf_op jit(solution)/shard_map/ppermute | solution.py:22
  130.9 2.3 %collective-permute-start.14 = (f32[256,512]{1,0:T(8,128)}, f32[256,512]{1,0:T(8,128)S(1)}, u32[]{:S(2)}, u32[]{:S(2)}) collective-permute-start(f32[256,512]{1,0:T(8,128)} %get-tuple-element.42), channel_id=1, source_target_pairs={{0,16},{16,0},{1,17},{17,1},{2,18},{18,2},{3,19},{19,3},{4,20},{20... | collective-permute-start | bytes 1572872 | tf_op jit(solution)/shard_map/ppermute | solution.py:22
  131.4 2.5 %collective-permute-start.15 = (f32[256,512]{1,0:T(8,128)}, f32[256,512]{1,0:T(8,128)S(1)}, u32[]{:S(2)}, u32[]{:S(2)}) collective-permute-start(f32[256,512]{1,0:T(8,128)} %get-tuple-element.43), channel_id=1, source_target_pairs={{0,16},{16,0},{1,17},{17,1},{2,18},{18,2},{3,19},{19,3},{4,20},{20... | collective-permute-start | bytes 1572872 | tf_op jit(solution)/shard_map/ppermute | solution.py:22
  131.5 3.1 %collective-permute-start.16 = (f32[256,512]{1,0:T(8,128)}, f32[256,512]{1,0:T(8,128)S(1)}, u32[]{:S(2)}, u32[]{:S(2)}) collective-permute-start(f32[256,512]{1,0:T(8,128)} %get-tuple-element.44), channel_id=1, source_target_pairs={{0,16},{16,0},{1,17},{17,1},{2,18},{18,2},{3,19},{19,3},{4,20},{20... | collective-permute-start | bytes 1572872 | tf_op jit(solution)/shard_map/ppermute | solution.py:22
  138.4 16.0 %all-to-all-start.2 = ((bf16[8,32,1536]{2,1,0:T(8,128)(2,1)}), bf16[8,32,1536]{2,1,0:T(8,128)(2,1)S(1)}, u32[]{:S(2)}, u32[]{:S(2)}) async-start(bf16[8,32,1536]{2,1,0:T(8,128)(2,1)} %bitcast.48), calls=%async_computation.2 | async-start | bytes 1572864 | tf_op jit(solution)/shard_map/all_to_all | solution.py:230
  157.4 14.9 %all-to-all-start.3 = ((bf16[8,32,1536]{2,1,0:T(8,128)(2,1)}), bf16[8,32,1536]{2,1,0:T(8,128)(2,1)S(1)}, u32[]{:S(2)}, u32[]{:S(2)}) async-start(bf16[8,32,1536]{2,1,0:T(8,128)(2,1)} %shard_map.68), calls=%async_computation.3 | async-start | bytes 1572864 | tf_op jit(solution)/shard_map/all_to_all | solution.py:239
  172.3 3.9 %collective-permute-start.18 = (bf16[256,1536]{1,0:T(8,128)(2,1)S(1)}, bf16[256,1536]{1,0:T(8,128)(2,1)S(1)}, u32[]{:S(2)}, u32[]{:S(2)}) collective-permute-start(bf16[256,1536]{1,0:T(8,128)(2,1)S(1)} %bitcast.42), channel_id=1, source_target_pairs={{0,16},{16,0},{1,17},{17,1},{2,18},{18,2},{3,19},{19,3},{4,20},{20... | collective-permute-start | bytes 2359304 | tf_op jit(solution)/shard_map/ppermute | solution.py:22
  180.8 14.9 %collective-permute-start.19 = (bf16[1024,256]{1,0:T(8,128)(2,1)}, bf16[1024,256]{1,0:T(8,128)(2,1)S(1)}, u32[]{:S(2)}, u32[]{:S(2)}) collective-permute-start(bf16[1024,256]{1,0:T(8,128)(2,1)} %shard_map.71), channel_id=1, source_target_pairs={{0,1},{1,0},{2,3},{3,2},{4,5},{5,4},{6,7},{7,6},{8,9},{9,8},{10,11... | collective-permute-start | bytes 1572872 | tf_op jit(solution)/shard_map/ppermute | solution.py:22
  187.1 19.8 %collective-permute-start.20 = (bf16[1024,256]{1,0:T(8,128)(2,1)}, bf16[1024,256]{1,0:T(8,128)(2,1)S(1)}, u32[]{:S(2)}, u32[]{:S(2)}) collective-permute-start(bf16[1024,256]{1,0:T(8,128)(2,1)} %shard_map.72), channel_id=1, source_target_pairs={{0,1},{1,0},{2,3},{3,2},{4,5},{5,4},{6,7},{7,6},{8,9},{9,8},{10,11... | collective-permute-start | bytes 1572872 | tf_op jit(solution)/shard_map/ppermute | solution.py:22
  195.3 11.7 %copy-start.9 = (f32[1024,256]{1,0:T(8,128)S(1)}, f32[1024,256]{1,0:T(8,128)}, u32[]{:S(2)}) copy-start(f32[1024,256]{1,0:T(8,128)} %shard_map.74) | copy-start | bytes 3145732
  (16 other events, 59.5 us)
